TPU v7x, 128 devices: a whole 4x4x4 slice. The times are simulated.
128 devices in a mesh: ctr: 16 (over y, x), bat: 8 (over z, core).
Axes of the slice: x: 4, y: 4, z: 4, core: 2. Of those that a mesh axis runs over, the one named last changes fastest.
Arguments:
- table: bfloat16 [131072, 1024], P('ctr'), may hold values from -6 to 6
- coefs: bfloat16 [131072, 256], P('ctr', 'bat'), may hold values from -6 to 6
- targets: float32 [1024, 256], P(None, 'bat'), may hold values from -6 to 6
- eigvecs: bfloat16 [65536, 256], P('ctr'), may hold values from -0.0234375 to 0.0234375
- correction: float32 [256], replicated, may hold values from 200 to 4000
- batch_idx: int32 [1024], P('bat'), may hold values from 0 to 131071
- nystrom_idx: int32 [65536], P('ctr'), may hold values from 0 to 131071, as said below
Outputs:
- residual: float32 [1024, 256], P(None, 'bat')
- nystrom_update: float32 [65536, 256], P('ctr', 'bat')
Inputs may be any that keep to these rules, and one draw needn't show every extreme that they name: `nystrom_idx`: entry m names a row of the block of 8192 table rows numbered m // 4096.
All inputs are finite; a program needn't handle non-finite values.
Results may differ from a plain program's by a relative error of at most 0.0031.
Values may be sent and summed in bfloat16 or wider, within the bound.
No kernel may reach another device: no remote copies, remote signals or barrier semaphores. Data moves between devices by JAX's collectives and lax.ppermute only.
A program may use at most 128 MiB of HBM per device.

v0:
```python
import jax
import jax.numpy as jnp
from jax import lax
from jax.sharding import PartitionSpec as P

D = 1024


def kernel(left, right):
    sharpness = 4.0 / D
    left_sq = jnp.sum(left.astype(jnp.float32) ** 2, axis=1)
    right_sq = jnp.sum(right.astype(jnp.float32) ** 2, axis=1)
    cross = jnp.dot(left, right.T, preferred_element_type=jnp.float32)
    return jnp.exp(-sharpness * (left_sq[:, None] + right_sq[None, :] - 2.0 * cross))


def per_device(table, coefs, targets, eigvecs, correction, batch_idx, nystrom_idx):
    c_rows = table.shape[0]
    first_row = lax.axis_index("ctr") * c_rows
    local_pos = batch_idx - first_row
    inside = (local_pos >= 0) & (local_pos < c_rows)
    picked = jnp.take(table, jnp.clip(local_pos, 0, c_rows - 1), axis=0).astype(jnp.float32)
    picked = picked * inside[:, None].astype(jnp.float32)
    own_rows = lax.psum(picked.astype(jnp.bfloat16), "ctr")
    nystrom_rows = jnp.take(table, nystrom_idx - first_row, axis=0)
    eig_wide = eigvecs.astype(jnp.float32)
    points = lax.all_gather(own_rows, "bat", axis=0, tiled=True)
    kern = kernel(points, table).astype(jnp.bfloat16)
    partial_pred = jnp.dot(kern, coefs, preferred_element_type=jnp.float32)
    kern_nys = kernel(nystrom_rows, points).astype(jnp.bfloat16)
    pred = lax.psum(partial_pred, "ctr")
    residual = pred - targets
    grad = residual.astype(jnp.bfloat16)
    applied = jnp.dot(kern_nys, grad, preferred_element_type=jnp.float32)
    local_proj = jnp.dot(eig_wide.T, applied, precision=lax.Precision.HIGHEST)
    projected = lax.psum(local_proj, "ctr")
    nystrom_update = jnp.dot(
        eig_wide, correction[:, None] * projected, precision=lax.Precision.HIGHEST
    )
    return (residual, nystrom_update)


def solution(mesh):
    return jax.shard_map(
        per_device,
        mesh=mesh,
        in_specs=(
            P("ctr", None),
            P("ctr", "bat"),
            P(None, "bat"),
            P("ctr", None),
            P(),
            P("bat"),
            P("ctr"),
        ),
        out_specs=(P(None, "bat"), P("ctr", "bat")),
        check_vma=False,
    )
```

profile of v0, /device:TPU:0, one launch (start us, length us, event | category | flops | bytes accessed | tf_op | source)
XLA Modules:
  0.0 355.7 jit_solution(14354933253021364162)
XLA Ops:
  7.2 0.0 all-reduce.3.cloned.1.call-start
  7.2 0.8 compare_and_fusion.1
  8.0 9.0 %gather_fusion = bf16[128,1024]{1,0:T(8,128)(2,1)S(1)} fusion(bf16[8192,1024]{1,0:T(8,128)(2,1)} %param.7, s32[1024]{0:T(1024)S(1)} %pad_clamp_fusion), kind=kCustom, calls=%fused_computation | custom fusion | bytes 524800 | tf_op jit(solution)/shard_map/jit(_take)/gather | solution.py:22
  17.0 0.9 multiply_convert_fusion
  17.9 0.0 all-reduce.3.cloned.1.call-update
  17.9 0.0 all-gather.2.cloned.1.call-start
  18.0 86.6 %all-reduce.3.cloned.1.call-done = bf16[128,1024]{1,0:T(8,128)(2,1)} async-done(((bf16[128,1024]{1,0:T(8,128)(2,1)}), bf16[128,1024]{1,0:T(8,128)(2,1)}) %all-reduce.3.cloned.1.call-update) | async-done | bytes 262160 | tf_op jit(solution)/shard_map/psum | solution.py:24
  104.5 0.0 all-gather.2.cloned.1.call-update
  104.5 0.0 all-reduce.5.cloned.1.call-start
  104.6 0.7 fusion.4
  105.3 29.0 %gather_fusion.1 = bf16[4096,1024]{1,0:T(8,128)(2,1)} fusion(bf16[8192,1024]{1,0:T(8,128)(2,1)} %param.7, s32[4096]{0:T(1024)S(1)} %fusion.4), kind=kCustom, calls=%fused_computation.1 | custom fusion | bytes 16793600 | tf_op jit(solution)/shard_map/jit(_take)/gather | solution.py:25
  134.3 7.2 %multiply_reduce_fusion = f32[8192]{0:T(1024)S(1)} fusion(bf16[8192,1024]{1,0:T(8,128)(2,1)} %param.7), kind=kLoop, calls=%fused_computation.3 | loop fusion | flops 25157632 | bytes 16809984 | tf_op jit(solution)/shard_map/reduce_sum | solution.py:12
  141.6 0.0 all-gather.2.cloned.1.call-done
  141.6 2.1 multiply_reduce_fusion.2
  143.7 28.7 %fusion.9 = f32[1024,32]{0,1:T(8,128)} fusion(bf16[8192,32]{0,1:T(8,128)(2,1)S(1)} %copy-done.5, bf16[1024,1024]{1,0:T(8,128)(2,1)} %all-gather.2.cloned.1.call-done, bf16[8192,1024]{1,0:T(8,128)(2,1)} %param.7, f32[8192]{0:T(1024)S(1)} %multiply_reduce_fusion, f32[1024]{0:T(1024)S(1)} %multiply_reduce_fusion.2), kind=kOutput, calls=%fused_computation.25 | convolution fusion | flops 17758683136 | bytes 19566592 | tf_op jit(solution)/shard_map/dot_general | solution.py:29
  172.4 0.0 all-reduce.5.cloned.1.call-update
  172.5 5.6 %multiply_reduce_fusion.1 = f32[4096]{0:T(1024)S(1)} fusion(bf16[4096,1024]{1,0:T(8,128)(2,1)} %gather_fusion.1, pred[4096]{0:T(1024)(128)(4,1)S(1)} %compare_and_fusion), kind=kLoop, calls=%fused_computation.5 | loop fusion | flops 16773120 | bytes 8409088 | tf_op jit(solution)/shard_map/reduce_sum | solution.py:11
  178.1 75.9 %all-reduce.5.cloned.1.call-done = f32[1024,32]{0,1:T(8,128)} async-done(((f32[1024,32]{0,1:T(8,128)}), f32[1024,32]{0,1:T(8,128)}) %all-reduce.5.cloned.1.call-update) | async-done | bytes 131088 | tf_op jit(solution)/shard_map/psum | solution.py:31
  254.0 0.9 sub.24
  255.0 16.0 %fusion = f32[4096,32]{0,1:T(8,128)S(1)} fusion(bf16[1024,1024]{1,0:T(8,128)(2,1)} %all-gather.2.cloned.1.call-done, f32[1024]{0:T(1024)S(1)} %multiply_reduce_fusion.2, f32[4096]{0:T(1024)S(1)} %multiply_reduce_fusion.1, bf16[4096,1024]{1,0:T(8,128)(2,1)} %gather_fusion.1, pred[4096]{0:T(1024)(128)(4,1)S(1)} %compare_and_fusion, f32[1024,32]{0,1:T(8,128)S(1)} %sub.24), kind=kOutput, calls=%fused_computation.7 | convolution fusion | flops 8883568640 | bytes 11165696 | tf_op jit(solution)/shard_map/dot_general | solution.py:34
  271.0 0.0 copy-done.2
  271.0 2.3 convolution_bitcast_fusion.1
  273.3 72.9 %psum.23 = f32[256,32]{1,0:T(8,128)S(1)} all-reduce(f32[256,32]{1,0:T(8,128)S(1)} %convolution_bitcast_fusion.1), channel_id=1, replica_groups=mesh['ctr'=16,'bat'=8] {'ctr'}, use_global_device_ids=true, to_apply=%region_5.6 | all-reduce | flops 8192 | bytes 65536 | tf_op jit(solution)/shard_map/psum | solution.py:36
  346.3 2.9 convolution_bitcast_fusion
  (13 shorter events, 0.1 us)
Async XLA Ops:
  7.2 263.8 %copy-start = (bf16[4096,256]{1,0:T(8,128)(2,1)S(1)}, bf16[4096,256]{1,0:T(8,128)(2,1)}, u32[]{:S(2)}) copy-start(bf16[4096,256]{1,0:T(8,128)(2,1)} %param.10) | copy-start | bytes 6291460
  7.2 97.3 %all-reduce.3.cloned.1.call-start = ((), (), s32[]{:S(2)}) async-start(), calls=%async_computation | async-start | bytes 524288 | tf_op jit(solution)/shard_map/psum | solution.py:24
  17.9 123.7 %all-gather.2.cloned.1.call-start = ((), (), s32[]{:S(2)}) async-start(), calls=%async_computation.1 | async-start | bytes 2359296 | tf_op jit(solution)/shard_map/all_gather | solution.py:27
  104.5 149.5 %all-reduce.5.cloned.1.call-start = ((), (), s32[]{:S(2)}) async-start(), calls=%async_computation.2 | async-start | bytes 262144 | tf_op jit(solution)/shard_map/psum | solution.py:31
  105.3 29.0 %copy-start.3 = (s32[4096]{0:T(1024)S(1)}, s32[4096]{0:T(1024)}, u32[]{:S(2)}) copy-start(s32[4096]{0:T(1024)} %param.13) | copy-start | bytes 49156
  134.3 9.4 %copy-start.5 = (bf16[8192,32]{0,1:T(8,128)(2,1)S(1)}, bf16[8192,32]{0,1:T(8,128)(2,1)}, u32[]{:S(2)}) copy-start(bf16[8192,32]{0,1:T(8,128)(2,1)} %param.8) | copy-start | bytes 1572868
  172.4 81.6 %copy-start.1 = (f32[1024,32]{0,1:T(8,128)S(1)}, f32[1024,32]{0,1:T(8,128)}, u32[]{:S(2)}) copy-start(f32[1024,32]{0,1:T(8,128)} %param.9) | copy-start | bytes 393220
  254.9 16.1 %copy-start.2 = (f32[1024,32]{0,1:T(8,128)}, f32[1024,32]{0,1:T(8,128)S(1)}, u32[]{:S(2)}) copy-start(f32[1024,32]{0,1:T(8,128)S(1)} %sub.24) | copy-start | bytes 393220
  255.0 91.3 %copy-start.4 = (f32[256]{0:T(256)S(1)}, f32[256]{0:T(256)}, u32[]{:S(2)}) copy-start(f32[256]{0:T(256)} %param.11) | copy-start | bytes 3076
Sparse Core Ops, SparseCore 0:
  18.0 86.4 all-reduce.2
  106.3 24.8 all-gather.1
  172.6 81.3 all-reduce.4
where the time goes:
time: 356 us
  waiting for transfers between devices  163 us (46%)
  blocking collectives  72.9 us (20%)
  matrix products  49.9 us (14%)
  local copies, waits for them, and re-layouts  38 us (11%)
  other arithmetic  18.2 us (5%)
  between operations  13.9 us (4%)
    psum x1, waiting for transfers between devices, per_device(): own_rows = lax.psum(picked.astype(jnp.bfloat16), 'ctr')  86.6 us
    psum x1, waiting for transfers between devices, per_device(): pred = lax.psum(partial_pred, 'ctr')  75.9 us
    psum x1, blocking collectives, per_device(): projected = lax.psum(local_proj, 'ctr')  72.9 us
    gather x1, local copies, waits for them, and re-layouts, per_device(): nystrom_rows = jnp.take(table, nystrom_idx - first_row, axis=0)  29 us
    dot_general x1, matrix products, per_device(): partial_pred = jnp.dot(kern, coefs, preferred_element_type=jnp.float32)  28.7 us
    dot_general x1, matrix products, per_device(): applied = jnp.dot(kern_nys, grad, preferred_element_type=jnp.float32)  16 us
    gather x1, local copies, waits for them, and re-layouts, per_device(): jnp.take(table, jnp.clip(local_pos, 0, c_rows - 1), axis=0)  8.97 us
    reduce_sum x2, other arithmetic, kernel(): left_sq = jnp.sum(left.astype(jnp.float32) ** 2, axis=1)  7.68 us
  transfers between devices with their start and end apart: 3, of which 2 were waited for; matrix products, arithmetic and copies ran while one was open for 12% of the time, Pallas kernels for 0%

commit v1 on v0

v1 whole, which is shorter than its diff:
```python
import functools

import jax
import jax.numpy as jnp
from jax import lax
from jax.experimental import pallas as pl
from jax.experimental.pallas import tpu as pltpu
from jax.sharding import PartitionSpec as P

D = 1024
SHARPNESS = 4.0 / D
N_CTR = 16
N_Z = 4
LANES = 128
GROUP = 16
MIB = 2**20
F32 = jnp.float32
BF16 = jnp.bfloat16
SMEM = pl.BlockSpec(memory_space=pltpu.SMEM)
VMEM = pl.BlockSpec(memory_space=pltpu.VMEM)
HBM = pl.BlockSpec(memory_space=pltpu.HBM)
SWAP = [(i, i ^ 1) for i in range(2 * N_Z)]
SAME_CORE = [[c * 8 + z * 2 + k for c in range(N_CTR) for z in range(N_Z)] for k in range(2)]


def z_shift(k):
    return [(z * 2 + c, (z + k) % N_Z * 2 + c) for z in range(N_Z) for c in range(2)]


def in_vmem(x):
    return pltpu.with_memory_space_constraint(x, pltpu.VMEM)


def pick_kernel(idx_ref, table_ref, out_ref, groups, rows, sems):
    n = rows.shape[0]
    c_rows = table_ref.shape[0]
    first_row = lax.axis_index("ctr") * c_rows
    rows[...] = jnp.zeros_like(rows)

    def copy_of(i, pos):
        start = pl.multiple_of(pos // GROUP * GROUP, GROUP)
        return pltpu.make_async_copy(table_ref.at[pl.ds(start, GROUP)], groups.at[i], sems.at[i])

    def start(i, carry):
        pos = idx_ref[i] - first_row

        @pl.when((pos >= 0) & (pos < c_rows))
        def _():
            copy_of(i, pos).start()

        return carry

    def finish(i, carry):
        pos = idx_ref[i] - first_row

        @pl.when((pos >= 0) & (pos < c_rows))
        def _():
            copy_of(i, pos).wait()
            group = groups[i].astype(F32)
            place = lax.broadcasted_iota(jnp.int32, group.shape, 0)
            kept = jnp.where(place == pos % GROUP, group, 0.0)
            rows[pl.ds(i, 1), :] = jnp.sum(kept, axis=0, keepdims=True)

        return carry

    lax.fori_loop(0, n, start, 0)
    lax.fori_loop(0, n, finish, 0)
    out_ref[...] = rows[...].astype(BF16)


def pick(batch_idx, table):
    n = batch_idx.shape[0]
    return pl.pallas_call(
        pick_kernel,
        in_specs=[SMEM, HBM],
        out_specs=VMEM,
        out_shape=jax.ShapeDtypeStruct((n, D), BF16),
        scratch_shapes=[
            pltpu.VMEM((n, GROUP, D), BF16),
            pltpu.VMEM((n, D), F32),
            pltpu.SemaphoreType.DMA((n,)),
        ],
        compiler_params=pltpu.CompilerParams(vmem_limit_bytes=8 * MIB),
        name="pick",
    )(batch_idx, pltpu.with_memory_space_constraint(table, pltpu.HBM))


def main_kernel(tile, idx_ref, pts_ref, table_ref, *rest):
    coef_refs = rest[:8]
    eig_ref, out_ref, kern, nys, acc = rest[8:]
    pts = pts_ref[...].astype(F32)
    pts_sq = lax.dot_general(
        jnp.ones((8, D), F32), pts * pts, (((1,), (1,)), ((), ())),
        precision=lax.Precision.HIGHEST, preferred_element_type=F32,
    )[0:1]
    acc[...] = jnp.zeros_like(acc)

    def one_tile(i, carry):
        rows = pl.ds(pl.multiple_of(i * tile, tile), tile)
        block = table_ref[rows, :]
        cross = lax.dot_general(
            block, pts_ref[...], (((1,), (1,)), ((), ())), preferred_element_type=F32
        )
        wide = block.astype(F32)
        row_sq = jnp.sum(wide * wide, axis=1, keepdims=True)
        k = jnp.exp(-SHARPNESS * (row_sq + pts_sq - 2.0 * cross)).astype(BF16)
        kern[rows, :] = k.astype(F32)
        coefs = jnp.concatenate([ref[:, rows] for ref in coef_refs], axis=0)
        acc[...] += jnp.dot(coefs, k, preferred_element_type=F32)
        return carry

    lax.fori_loop(0, table_ref.shape[0] // tile, one_tile, 0)

    unroll = 32

    def gather(j, carry):
        for u in range(unroll):
            m = j * unroll + u
            nys[pl.ds(m, 1), :] = kern[pl.ds(idx_ref[m], 1), :]
        return carry

    lax.fori_loop(0, nys.shape[0] // unroll, gather, 0)
    comp = lax.dot_general(
        eig_ref[...], nys[...].astype(BF16), (((0,), (0,)), ((), ())), preferred_element_type=F32
    )
    for c in range(N_CTR):
        out_ref[c, 0:16, :] = comp[c * 16:(c + 1) * 16]
    bat = lax.axis_index("bat")
    z = bat // 2
    core = bat % 2
    for k in range(N_Z):
        for s in range(2):
            from_z = (z + N_Z - k) % N_Z
            from_core = core if s == 0 else 1 - core
            piece = acc[(2 * k + s) * 32:(2 * k + s + 1) * 32, :]
            for i in range(8):
                out_ref[from_core * 8 + i, pl.ds(16 + from_z * 4, 4), :] = piece[4 * i:4 * i + 4]


def main(local_idx, points, table, pieces, eigvecs):
    c_rows = table.shape[0]
    m_rows, q = eigvecs.shape
    return pl.pallas_call(
        functools.partial(main_kernel, 1024),
        in_specs=[SMEM] + [VMEM] * 11,
        out_specs=VMEM,
        out_shape=jax.ShapeDtypeStruct((N_CTR, 32, LANES), F32),
        scratch_shapes=[
            pltpu.VMEM((c_rows, LANES), F32),
            pltpu.VMEM((m_rows, LANES), F32),
            pltpu.VMEM((q, LANES), F32),
        ],
        compiler_params=pltpu.CompilerParams(vmem_limit_bytes=20 * MIB),
        cost_estimate=pl.CostEstimate(flops=3 * 10**9, bytes_accessed=24 * MIB, transcendentals=10**6),
        name="main",
    )(local_idx, points, in_vmem(table), *[in_vmem(x) for x in pieces], in_vmem(eigvecs))


def split3(x):
    hi = x.astype(BF16)
    rest = x - hi.astype(F32)
    mid = rest.astype(BF16)
    lo = (rest - mid.astype(F32)).astype(BF16)
    return hi, mid, lo


def final_kernel(same_ref, other_ref, targets_ref, corr_ref, eig_ref, res_ref, upd_ref, comp):
    core = lax.axis_index("bat") % 2
    for z in range(N_Z):
        for s, ref in enumerate((same_ref, other_ref)):
            from_core = core if s == 0 else 1 - core
            lanes = pl.ds(pl.multiple_of((2 * z + from_core) * LANES, LANES), LANES)
            for c in range(N_CTR):
                comp[c * 16:(c + 1) * 16, lanes] = ref[c * N_Z + z, 0:16, :]
            for i in range(8):
                row = (core * 8 + i) * N_Z + z
                res_ref[4 * i:4 * i + 4, lanes] = ref[row, 16:20, :]
    residual = res_ref[...] - targets_ref[...]
    res_ref[...] = residual
    grad = residual.astype(BF16)
    proj = jnp.zeros((32, comp.shape[0]), F32)
    for part in split3(comp[...]):
        proj += lax.dot_general(grad, part, (((1,), (1,)), ((), ())), preferred_element_type=F32)
    scaled = jnp.concatenate(split3(proj * corr_ref[...]), axis=0)
    upd = lax.dot_general(
        scaled, eig_ref[...], (((1,), (1,)), ((), ())), preferred_element_type=F32
    )
    upd_ref[...] = upd[0:32] + (upd[32:64] + upd[64:96])


def final(same, other, targets, correction, eigvecs):
    cols, n = targets.shape
    m_rows, q = eigvecs.shape
    return pl.pallas_call(
        final_kernel,
        in_specs=[VMEM] * 5,
        out_specs=[VMEM, VMEM],
        out_shape=[
            jax.ShapeDtypeStruct((cols, n), F32),
            jax.ShapeDtypeStruct((cols, m_rows), F32),
        ],
        scratch_shapes=[pltpu.VMEM((q, n), F32)],
        compiler_params=pltpu.CompilerParams(vmem_limit_bytes=16 * MIB),
        name="final",
    )(same, other, targets, correction, in_vmem(eigvecs))


def per_device(table, coefs, targets, eigvecs, correction, batch_idx, nystrom_idx):
    c_rows = table.shape[0]
    first_row = lax.axis_index("ctr") * c_rows
    own = coefs.T
    from_z = [lax.ppermute(own, "bat", z_shift(k)) if k else own for k in range(N_Z)]

    picked = pick(batch_idx, table).reshape(N_CTR, -1, D)
    parts = lax.all_to_all(picked, "ctr", 0, 0)
    own_points = jnp.sum(parts.astype(F32), axis=0).astype(BF16)
    spread = jnp.broadcast_to(own_points[None], parts.shape)
    points = lax.all_to_all(spread, "ctr", 0, 0).reshape(-1, D)

    points, *from_z = lax.optimization_barrier((points, *from_z))
    pieces = [x for here in from_z for x in (here, lax.ppermute(here, "bat", SWAP))]
    partial = main(nystrom_idx - first_row, points, table, pieces, eigvecs)
    mine = jnp.sum(lax.all_to_all(partial, "ctr", 0, 0), axis=0)
    comp = jnp.broadcast_to(mine[None, :16], (N_Z, 16, LANES))
    pred = jnp.pad(mine[16:].reshape(N_Z, 4, LANES), ((0, 0), (0, 4), (0, 0)))
    sent = jnp.concatenate([comp, pred], axis=1)
    sent = jnp.broadcast_to(sent[None], (N_CTR,) + sent.shape).reshape((-1,) + sent.shape[1:])
    same = lax.all_to_all(sent, ("ctr", "bat"), 0, 0, axis_index_groups=SAME_CORE)
    other = lax.ppermute(same, "bat", SWAP)
    residual, update = final(same, other, targets.T, correction[None], eigvecs)
    return residual.T, update.T


def solution(mesh):
    return jax.shard_map(
        per_device,
        mesh=mesh,
        in_specs=(
            P("ctr", None),
            P("ctr", "bat"),
            P(None, "bat"),
            P("ctr", None),
            P(),
            P("bat"),
            P("ctr"),
        ),
        out_specs=(P(None, "bat"), P("ctr", "bat")),
        check_vma=False,
    )
```

time: 356 us -> 107 us (0.30)
  waiting for transfers between devices: 163 us -> 5.05 us
  matrix products: 49.9 us -> 0 us
  local copies, waits for them, and re-layouts: 38 us -> 7.26 us
  Pallas kernels: 0 us -> 24.9 us
  other arithmetic: 18.2 us -> 1.4 us
  blocking collectives: 72.9 us -> 59.5 us
  between operations: 13.9 us -> 0.76 us
  starting transfers between devices: 0.12 us -> 6.54 us
    psum x2 -> x0, waiting for transfers between devices: 162 us -> none  [the longest x1 86.6 us: per_device(): own_rows = lax.psum(picked.astype(jnp.bfloat16), 'ctr')]
    psum x1 -> x0, blocking collectives: 72.9 us -> none  [per_device(): projected = lax.psum(local_proj, 'ctr')]
    all_to_all x0 -> x4, blocking collectives: none -> 59.5 us  [the longest x1 20.4 us: per_device(): lax.all_to_all(sent, ('ctr', 'bat'), 0, 0, axis_index_groups=SAME_CORE)]
    dot_general x4 -> x0, matrix products: 49.9 us -> none  [the longest x1 28.7 us: per_device(): partial_pred = jnp.dot(kern, coefs, preferred_element_type=jnp.float32)]
    gather x2 -> x0, local copies, waits for them, and re-layouts: 38 us -> none  [the longest x1 29 us: per_device(): nystrom_rows = jnp.take(table, nystrom_idx - first_row, axis=0)]
    pallas_call x0 -> x3, Pallas kernels: none -> 24.9 us  [the longest x1 16.5 us: main(): pl.pallas_call(functools.partial(main_kernel, 1024), in_specs=[SMEM] + [V...]
    reduce_sum x3 -> x2, other arithmetic: 14.9 us -> 0.67 us  [the longest x1 0.65 us: per_device(): own_points = jnp.sum(parts.astype(F32), axis=0).astype(BF16)]
    ppermute x0 -> x8, starting transfers between devices: none -> 6.54 us  [the longest x3 5.45 us: per_device(): lax.ppermute(own, 'bat', z_shift(k))]
  transfers between devices with their start and end apart: 3 -> 8, of which waited for: 2 -> 4; matrix products, arithmetic and copies ran while one was open for 12% -> 2% of each run, Pallas kernels for 0% -> 5%
where the time goes in v1:
time: 107 us; the launch traced here: 105 us
  blocking collectives  59.5 us (56%)
  Pallas kernels  24.9 us (23%)
  local copies, waits for them, and re-layouts  7.26 us (7%)
  starting transfers between devices  6.54 us (6%)
  waiting for transfers between devices  5.05 us (5%)
  other arithmetic  1.4 us (1%)
    all_to_all x1, blocking collectives, per_device(): lax.all_to_all(sent, ('ctr', 'bat'), 0, 0, axis_index_groups=SAME_CORE)  20.4 us
    pallas_call x1, Pallas kernels, main(): pl.pallas_call(functools.partial(main_kernel, 1024), in_specs=[SMEM] + [V...  16.5 us
    all_to_all x1, blocking collectives, per_device(): parts = lax.all_to_all(picked, 'ctr', 0, 0)  15.6 us
    all_to_all x1, blocking collectives, per_device(): mine = jnp.sum(lax.all_to_all(partial, 'ctr', 0, 0), axis=0)  11.9 us
    all_to_all x1, blocking collectives, per_device(): points = lax.all_to_all(spread, 'ctr', 0, 0).reshape(-1, D)  11.6 us
    unnamed x12, local copies, waits for them, and re-layouts  6.44 us
    ppermute x3, starting transfers between devices, per_device(): lax.ppermute(own, 'bat', z_shift(k))  5.45 us
    pallas_call x1, Pallas kernels, pick(): pl.pallas_call(pick_kernel, in_specs=[SMEM, HBM], out_specs=VMEM, out_sha...  5.42 us
  transfers between devices with their start and end apart: 8, of which 4 were waited for; matrix products, arithmetic and copies ran while one was open for 2% of the time, Pallas kernels for 5%

profile of v1, /device:TPU:0, one launch (start us, length us, event | category | flops | bytes accessed | tf_op | source)
XLA Modules:
  0.0 105.4 jit_solution(3351696137446408981)
XLA Ops:
  0.7 4.2 %collective-permute-start.2 = (bf16[32,8192]{1,0:T(8,128)(2,1)}, bf16[32,8192]{1,0:T(8,128)(2,1)S(1)}, u32[]{:S(2)}, u32[]{:S(2)}) collective-permute-start(bf16[32,8192]{1,0:T(8,128)(2,1)} %bitcast.11), channel_id=1, source_target_pairs={{0,6},{1,7},{2,0},{3,1},{4,2},{5,3},{6,4},{7,5},{8,14},{9,15},{10,... | collective-permute-start | bytes 1572872 | tf_op jit(solution)/shard_map/ppermute | solution.py:212
  4.8 1.3 %collective-permute-start = (bf16[32,8192]{1,0:T(8,128)(2,1)}, bf16[32,8192]{1,0:T(8,128)(2,1)}, u32[]{:S(2)}, u32[]{:S(2)}) collective-permute-start(bf16[32,8192]{1,0:T(8,128)(2,1)} %bitcast.13), channel_id=1, source_target_pairs={{0,2},{1,3},{2,4},{3,5},{4,6},{5,7},{6,0},{7,1},{8,10},{9,11},{10,... | collective-permute-start | bytes 1572872 | tf_op jit(solution)/shard_map/ppermute | solution.py:212
  6.1 0.7 copy-done.5
  6.8 5.4 %pick.1 = bf16[128,1024]{1,0:T(8,128)(2,1)S(1)} custom-call(s32[128]{0:T(128)S(1)} %copy-done.5, bf16[8192,1024]{1,0:T(8,128)(2,1)} %table_ref.3), custom_call_target="tpu_custom_call" | custom-call | tf_op jit(solution)/shard_map/pick/pallas_call | solution.py:73
  12.2 0.0 copy-start.3
  12.2 15.6 %all_to_all.20 = bf16[16,8,1024]{2,1,0:T(8,128)(2,1)S(1)} all-to-all(bf16[16,8,1024]{2,1,0:T(8,128)(2,1)S(1)} %bitcast.10), channel_id=1, replica_groups=mesh['ctr'=16,'bat'=8] {'ctr'}, dimensions={0} | all-to-all | bytes 524288 | tf_op jit(solution)/shard_map/all_to_all | solution.py:215
  27.8 0.6 reduce_sum.21
  28.5 0.7 broadcast_in_dim.8
  29.2 11.6 %all_to_all.21 = bf16[16,8,1024]{2,1,0:T(8,128)(2,1)S(1)} all-to-all(bf16[16,8,1024]{2,1,0:T(8,128)(2,1)S(1)} %broadcast_in_dim.8), channel_id=1, replica_groups=mesh['ctr'=16,'bat'=8] {'ctr'}, dimensions={0} | all-to-all | bytes 524288 | tf_op jit(solution)/shard_map/all_to_all | solution.py:218
  40.8 0.1 collective-permute-start.3
  40.9 0.5 collective-permute-start.4
  41.4 0.1 collective-permute-start.5
  41.5 0.4 collective-permute-start.6
  41.9 0.7 broadcast_subtract_fusion.idx_ref
  42.7 0.3 collective-permute-done.3.rest_1_
  43.0 1.7 %collective-permute-done.4.rest_3_ = bf16[32,8192]{1,0:T(8,128)(2,1)} collective-permute-done((bf16[32,8192]{1,0:T(8,128)(2,1)}, bf16[32,8192]{1,0:T(8,128)(2,1)}, u32[]{:S(2)}, u32[]{:S(2)}) %collective-permute-start.4) | collective-permute-done | bytes 524320 | tf_op jit(solution)/shard_map/ppermute | solution.py:221
  44.7 0.8 collective-permute-done.5.rest_5_
  45.4 5.8 %copy-done = bf16[8192,1024]{1,0:T(8,128)(2,1)S(1)} copy-done((bf16[8192,1024]{1,0:T(8,128)(2,1)S(1)}, bf16[8192,1024]{1,0:T(8,128)(2,1)}, u32[]{:S(2)}) %copy-start) | copy-done | bytes 16777240
  51.2 16.5 %main.1 = f32[16,32,128]{2,1,0:T(8,128)S(1)} custom-call(s32[4096]{0:T(1024)S(1)} %broadcast_subtract_fusion.idx_ref, bf16[128,1024]{1,0:T(8,128)(2,1)S(1)} %bitcast.9, bf16[8192,1024]{1,0:T(8,128)(2,1)S(1)} %copy-done, bf16[32,8192]{1,0:T(8,128)(2,1)S(1)} %bitcast.15, bf16[32,8192]{1,0:T(8,128)(2,1)} %collective-permute-done.3.rest_1_, ...), custom_call_target="tpu_custom_call" | custom-call | flops 3000000000 | bytes 25165824 | tf_op jit(solution)/shard_map/main/pallas_call | solution.py:143
  67.7 11.9 %all_to_all.22 = f32[16,32,128]{2,1,0:T(8,128)S(1)} all-to-all(f32[16,32,128]{2,1,0:T(8,128)S(1)} %main.1), channel_id=1, replica_groups=mesh['ctr'=16,'bat'=8] {'ctr'}, dimensions={0} | all-to-all | bytes 524288 | tf_op jit(solution)/shard_map/all_to_all | solution.py:223
  79.6 0.1 broadcast_in_dim.10
  79.7 20.4 %all_to_all.23.same_ref = f32[64,24,128]{2,1,0:T(8,128)S(1)} all-to-all(f32[64,24,128]{2,1,0:T(8,128)S(1)} %bitcast.18), channel_id=1, replica_groups={{0,2,4,6,8,10,12,14,16,18,20,22,24,26,28,30,32,34,36,38,40,42,44,46,48,..., dimensions={0} | all-to-all | bytes 1572864 | tf_op jit(solution)/shard_map/all_to_all | solution.py:228
  100.2 2.3 %collective-permute-done.7.other_ref = f32[64,24,128]{2,1,0:T(8,128)S(1)} collective-permute-done((f32[64,24,128]{2,1,0:T(8,128)S(1)}, f32[64,24,128]{2,1,0:T(8,128)S(1)}, u32[]{:S(2)}, u32[]{:S(2)}) %collective-permute-start.7) | collective-permute-done | bytes 786464 | tf_op jit(solution)/shard_map/ppermute | solution.py:229
  102.4 3.0 %final.1 = (f32[32,1024]{1,0:T(8,128)}, f32[32,4096]{1,0:T(8,128)}) custom-call(f32[64,24,128]{2,1,0:T(8,128)S(1)} %all_to_all.23.same_ref, f32[64,24,128]{2,1,0:T(8,128)S(1)} %collective-permute-done.7.other_ref, f32[32,1024]{1,0:T(8,128)S(1)} %bitcast.16, f32[1,256]{1,0:T(1,128)S(1)} %bitcast.17, bf16[4096,256]{1,0:T(8,128)(2,1)S(1)} %copy-done.1), custom_call_target="tpu_custom_call" | custom-call | tf_op jit(solution)/shard_map/final/pallas_call | solution.py:194
  (19 shorter events, 0.1 us)
Async XLA Ops:
  0.6 40.2 %copy-start.2 = (bf16[8192,32]{0,1:T(8,128)(2,1)S(1)}, bf16[8192,32]{0,1:T(8,128)(2,1)}, u32[]{:S(2)}) copy-start(bf16[8192,32]{0,1:T(8,128)(2,1)} %param.8) | copy-start | bytes 1572868
  0.6 44.8 %copy-start.1 = (bf16[4096,256]{1,0:T(8,128)(2,1)S(1)}, bf16[4096,256]{1,0:T(8,128)(2,1)}, u32[]{:S(2)}) copy-start(bf16[4096,256]{1,0:T(8,128)(2,1)} %eig_ref.1) | copy-start | bytes 6291460
  0.7 40.2 %collective-permute-start.2 = (bf16[32,8192]{1,0:T(8,128)(2,1)}, bf16[32,8192]{1,0:T(8,128)(2,1)S(1)}, u32[]{:S(2)}, u32[]{:S(2)}) collective-permute-start(bf16[32,8192]{1,0:T(8,128)(2,1)} %bitcast.11), channel_id=1, source_target_pairs={{0,6},{1,7},{2,0},{3,1},{4,2},{5,3},{6,4},{7,5},{8,14},{9,15},{10,... | collective-permute-start | bytes 1572872 | tf_op jit(solution)/shard_map/ppermute | solution.py:212
  4.8 36.0 %collective-permute-start.1 = (bf16[32,8192]{1,0:T(8,128)(2,1)}, bf16[32,8192]{1,0:T(8,128)(2,1)}, u32[]{:S(2)}, u32[]{:S(2)}) collective-permute-start(bf16[32,8192]{1,0:T(8,128)(2,1)} %bitcast.12), channel_id=1, source_target_pairs={{0,4},{1,5},{2,6},{3,7},{4,0},{5,1},{6,2},{7,3},{8,12},{9,13},{10,... | collective-permute-start | bytes 1572872 | tf_op jit(solution)/shard_map/ppermute | solution.py:212
  4.8 36.0 %collective-permute-start = (bf16[32,8192]{1,0:T(8,128)(2,1)}, bf16[32,8192]{1,0:T(8,128)(2,1)}, u32[]{:S(2)}, u32[]{:S(2)}) collective-permute-start(bf16[32,8192]{1,0:T(8,128)(2,1)} %bitcast.13), channel_id=1, source_target_pairs={{0,2},{1,3},{2,4},{3,5},{4,6},{5,7},{6,0},{7,1},{8,10},{9,11},{10,... | collective-permute-start | bytes 1572872 | tf_op jit(solution)/shard_map/ppermute | solution.py:212
  6.1 0.7 copy-start.5
  12.2 90.3 %copy-start.3 = (f32[1024,32]{0,1:T(8,128)S(1)}, f32[1024,32]{0,1:T(8,128)}, u32[]{:S(2)}) copy-start(f32[1024,32]{0,1:T(8,128)} %param.9) | copy-start | bytes 393220
  12.2 90.2 %copy-start.4 = (f32[256]{0:T(256)S(1)}, f32[256]{0:T(256)}, u32[]{:S(2)}) copy-start(f32[256]{0:T(256)} %param.11) | copy-start | bytes 3076
  40.8 2.1 %collective-permute-start.3 = (bf16[32,8192]{1,0:T(8,128)(2,1)S(1)}, bf16[32,8192]{1,0:T(8,128)(2,1)}, u32[]{:S(2)}, u32[]{:S(2)}) collective-permute-start(bf16[32,8192]{1,0:T(8,128)(2,1)S(1)} %bitcast.14), channel_id=1, source_target_pairs={{0,1},{1,0},{2,3},{3,2},{4,5},{5,4},{6,7},{7,6},{8,9},{9,8},{10,11... | collective-permute-start | bytes 1572872 | tf_op jit(solution)/shard_map/ppermute | solution.py:221
  40.9 3.7 %collective-permute-start.4 = (bf16[32,8192]{1,0:T(8,128)(2,1)}, bf16[32,8192]{1,0:T(8,128)(2,1)}, u32[]{:S(2)}, u32[]{:S(2)}) collective-permute-start(bf16[32,8192]{1,0:T(8,128)(2,1)} %collective-permute-done.rest_2_), channel_id=1, source_target_pairs={{0,1},{1,0},{2,3},{3,2},{4,5},{5,4},{6,7},{7,6},{8,9},{9,8},{10,11... | collective-permute-start | bytes 1572872 | tf_op jit(solution)/shard_map/ppermute | solution.py:221
  41.4 4.0 %collective-permute-start.5 = (bf16[32,8192]{1,0:T(8,128)(2,1)}, bf16[32,8192]{1,0:T(8,128)(2,1)}, u32[]{:S(2)}, u32[]{:S(2)}) collective-permute-start(bf16[32,8192]{1,0:T(8,128)(2,1)} %collective-permute-done.1.rest_4_), channel_id=1, source_target_pairs={{0,1},{1,0},{2,3},{3,2},{4,5},{5,4},{6,7},{7,6},{8,9},{9,8},{10,11... | collective-permute-start | bytes 1572872 | tf_op jit(solution)/shard_map/ppermute | solution.py:221
  41.5 3.9 %collective-permute-start.6 = (bf16[32,8192]{1,0:T(8,128)(2,1)S(1)}, bf16[32,8192]{1,0:T(8,128)(2,1)}, u32[]{:S(2)}, u32[]{:S(2)}) collective-permute-start(bf16[32,8192]{1,0:T(8,128)(2,1)S(1)} %collective-permute-done.2.rest_6_), channel_id=1, source_target_pairs={{0,1},{1,0},{2,3},{3,2},{4,5},{5,4},{6,7},{7,6},{8,9},{9,8},{10,11... | collective-permute-start | bytes 1572872 | tf_op jit(solution)/shard_map/ppermute | solution.py:221
  45.4 5.8 %copy-start = (bf16[8192,1024]{1,0:T(8,128)(2,1)S(1)}, bf16[8192,1024]{1,0:T(8,128)(2,1)}, u32[]{:S(2)}) copy-start(bf16[8192,1024]{1,0:T(8,128)(2,1)} %table_ref.3) | copy-start | bytes 50331652
  100.2 2.3 %collective-permute-start.7 = (f32[64,24,128]{2,1,0:T(8,128)S(1)}, f32[64,24,128]{2,1,0:T(8,128)S(1)}, u32[]{:S(2)}, u32[]{:S(2)}) collective-permute-start(f32[64,24,128]{2,1,0:T(8,128)S(1)} %all_to_all.23.same_ref), channel_id=1, source_target_pairs={{0,1},{1,0},{2,3},{3,2},{4,5},{5,4},{6,7},{7,6},{8,9},{9,8},{10,11... | collective-permute-start | bytes 2359304 | tf_op jit(solution)/shard_map/ppermute | solution.py:229

commit v2 on v1

--- a/solution.py
+++ b/solution.py
@@ -31,85 +31,113 @@
     return pltpu.with_memory_space_constraint(x, pltpu.VMEM)
 
 
-def pick_kernel(idx_ref, table_ref, out_ref, groups, rows, sems):
+def pick_kernel(idx_ref, nys_ref, table_ref, out_ref, local_ref, listed, groups, rows, sems):
     n = rows.shape[0]
     c_rows = table_ref.shape[0]
     first_row = lax.axis_index("ctr") * c_rows
+
+    def note(i, count):
+        pos = idx_ref[i] - first_row
+        listed[count] = i
+        return count + jnp.where((pos >= 0) & (pos < c_rows), 1, 0)
+
+    count = lax.fori_loop(0, n, note, 0, unroll=8)
+
+    def copy_of(s):
+        pos = idx_ref[listed[s]] - first_row
+        start = pl.multiple_of(pos // GROUP * GROUP, GROUP)
+        return pltpu.make_async_copy(table_ref.at[pl.ds(start, GROUP)], groups.at[s], sems.at[s])
+
+    def start(s, carry):
+        copy_of(s).start()
+        return carry
+
+    lax.fori_loop(0, count, start, 0)
+    local_ref[...] = nys_ref[...] - first_row
     rows[...] = jnp.zeros_like(rows)
 
-    def copy_of(i, pos):
-        start = pl.multiple_of(pos // GROUP * GROUP, GROUP)
-        return pltpu.make_async_copy(table_ref.at[pl.ds(start, GROUP)], groups.at[i], sems.at[i])
-
-    def start(i, carry):
-        pos = idx_ref[i] - first_row
-
-        @pl.when((pos >= 0) & (pos < c_rows))
-        def _():
-            copy_of(i, pos).start()
-
-        return carry
-
-    def finish(i, carry):
-        pos = idx_ref[i] - first_row
-
-        @pl.when((pos >= 0) & (pos < c_rows))
-        def _():
-            copy_of(i, pos).wait()
-            group = groups[i].astype(F32)
-            place = lax.broadcasted_iota(jnp.int32, group.shape, 0)
-            kept = jnp.where(place == pos % GROUP, group, 0.0)
-            rows[pl.ds(i, 1), :] = jnp.sum(kept, axis=0, keepdims=True)
-
-        return carry
-
-    lax.fori_loop(0, n, start, 0)
-    lax.fori_loop(0, n, finish, 0)
+    def finish(s, carry):
+        copy_of(s).wait()
+        i = listed[s]
+        group = groups[s].astype(F32)
+        place = lax.broadcasted_iota(jnp.int32, group.shape, 0)
+        kept = jnp.where(place == (idx_ref[i] - first_row) % GROUP, group, 0.0)
+        rows[pl.ds(i, 1), :] = jnp.sum(kept, axis=0, keepdims=True)
+        return carry
+
+    lax.fori_loop(0, count, finish, 0)
     out_ref[...] = rows[...].astype(BF16)
 
 
-def pick(batch_idx, table):
+def pick(batch_idx, nystrom_idx, table):
     n = batch_idx.shape[0]
     return pl.pallas_call(
         pick_kernel,
-        in_specs=[SMEM, HBM],
-        out_specs=VMEM,
-        out_shape=jax.ShapeDtypeStruct((n, D), BF16),
+        in_specs=[SMEM, VMEM, HBM],
+        out_specs=[VMEM, VMEM],
+        out_shape=[
+            jax.ShapeDtypeStruct((n, D), BF16),
+            jax.ShapeDtypeStruct(nystrom_idx.shape, jnp.int32),
+        ],
         scratch_shapes=[
+            pltpu.SMEM((n + 1,), jnp.int32),
             pltpu.VMEM((n, GROUP, D), BF16),
             pltpu.VMEM((n, D), F32),
             pltpu.SemaphoreType.DMA((n,)),
         ],
         compiler_params=pltpu.CompilerParams(vmem_limit_bytes=8 * MIB),
         name="pick",
-    )(batch_idx, pltpu.with_memory_space_constraint(table, pltpu.HBM))
-
-
-def main_kernel(tile, idx_ref, pts_ref, table_ref, *rest):
+    )(batch_idx, nystrom_idx, pltpu.with_memory_space_constraint(table, pltpu.HBM))
+
+
+N_TILES = 8
+
+
+def main_kernel(idx_ref, pts_ref, table_ref, *rest):
     coef_refs = rest[:8]
-    eig_ref, out_ref, kern, nys, acc = rest[8:]
+    eig_ref, out_ref, held, cross, kern, kern16, nys, acc, sems = rest[8:]
+
+    n_tiles = sems.shape[0]
+    tile = held.shape[0] // n_tiles
+    q = eig_ref.shape[1]
+
+    def rows_of(i):
+        return pl.ds(pl.multiple_of(i * tile, tile), tile)
+
+    def copy_of(i):
+        rows = rows_of(i)
+        return pltpu.make_async_copy(table_ref.at[rows], held.at[rows], sems.at[i])
+
+    for i in range(n_tiles):
+        copy_of(i).start()
     pts = pts_ref[...].astype(F32)
     pts_sq = lax.dot_general(
         jnp.ones((8, D), F32), pts * pts, (((1,), (1,)), ((), ())),
         precision=lax.Precision.HIGHEST, preferred_element_type=F32,
     )[0:1]
-    acc[...] = jnp.zeros_like(acc)
-
-    def one_tile(i, carry):
-        rows = pl.ds(pl.multiple_of(i * tile, tile), tile)
-        block = table_ref[rows, :]
-        cross = lax.dot_general(
-            block, pts_ref[...], (((1,), (1,)), ((), ())), preferred_element_type=F32
+
+    def multiply(i):
+        copy_of(i).wait()
+        cross[i % 2] = lax.dot_general(
+            held[rows_of(i), :], pts_ref[...], (((1,), (1,)), ((), ())),
+            preferred_element_type=F32,
         )
-        wide = block.astype(F32)
+
+    def finish(i):
+        wide = held[rows_of(i), :].astype(F32)
         row_sq = jnp.sum(wide * wide, axis=1, keepdims=True)
-        k = jnp.exp(-SHARPNESS * (row_sq + pts_sq - 2.0 * cross)).astype(BF16)
-        kern[rows, :] = k.astype(F32)
-        coefs = jnp.concatenate([ref[:, rows] for ref in coef_refs], axis=0)
-        acc[...] += jnp.dot(coefs, k, preferred_element_type=F32)
-        return carry
-
-    lax.fori_loop(0, table_ref.shape[0] // tile, one_tile, 0)
+        k = jnp.exp(-SHARPNESS * (row_sq + pts_sq - 2.0 * cross[i % 2])).astype(BF16)
+        kern[rows_of(i), :] = k.astype(F32)
+        kern16[rows_of(i), :] = k
+
+    def both(i, carry):
+        multiply(i)
+        finish(i - 1)
+        return carry
+
+    multiply(0)
+    lax.fori_loop(1, n_tiles, both, 0)
+    finish(n_tiles - 1)
 
     unroll = 32
 
@@ -120,6 +148,8 @@
         return carry
 
     lax.fori_loop(0, nys.shape[0] // unroll, gather, 0)
+    coefs = jnp.concatenate([ref[...] for ref in coef_refs], axis=0)
+    acc[...] = jnp.dot(coefs, kern16[...], preferred_element_type=F32)
     comp = lax.dot_general(
         eig_ref[...], nys[...].astype(BF16), (((0,), (0,)), ((), ())), preferred_element_type=F32
     )
@@ -132,28 +162,35 @@
         for s in range(2):
             from_z = (z + N_Z - k) % N_Z
             from_core = core if s == 0 else 1 - core
-            piece = acc[(2 * k + s) * 32:(2 * k + s + 1) * 32, :]
+            first = (2 * k + s) * 32
             for i in range(8):
-                out_ref[from_core * 8 + i, pl.ds(16 + from_z * 4, 4), :] = piece[4 * i:4 * i + 4]
+                out_ref[from_core * 8 + i, pl.ds(16 + from_z * 4, 4), :] = acc[first + 4 * i:first + 4 * i + 4]
 
 
 def main(local_idx, points, table, pieces, eigvecs):
     c_rows = table.shape[0]
     m_rows, q = eigvecs.shape
     return pl.pallas_call(
-        functools.partial(main_kernel, 1024),
-        in_specs=[SMEM] + [VMEM] * 11,
+        main_kernel,
+        in_specs=[SMEM, VMEM, HBM] + [VMEM] * 9,
         out_specs=VMEM,
         out_shape=jax.ShapeDtypeStruct((N_CTR, 32, LANES), F32),
         scratch_shapes=[
+            pltpu.VMEM((c_rows, D), BF16),
+            pltpu.VMEM((2, c_rows // N_TILES, LANES), F32),
             pltpu.VMEM((c_rows, LANES), F32),
+            pltpu.VMEM((c_rows, LANES), BF16),
             pltpu.VMEM((m_rows, LANES), F32),
-            pltpu.VMEM((q, LANES), F32),
-        ],
-        compiler_params=pltpu.CompilerParams(vmem_limit_bytes=20 * MIB),
+            pltpu.VMEM((256, LANES), F32),
+            pltpu.SemaphoreType.DMA((N_TILES,)),
+        ],
+        compiler_params=pltpu.CompilerParams(vmem_limit_bytes=40 * MIB),
         cost_estimate=pl.CostEstimate(flops=3 * 10**9, bytes_accessed=24 * MIB, transcendentals=10**6),
         name="main",
-    )(local_idx, points, in_vmem(table), *[in_vmem(x) for x in pieces], in_vmem(eigvecs))
+    )(
+        local_idx, points, pltpu.with_memory_space_constraint(table, pltpu.HBM),
+        *[in_vmem(x) for x in pieces], in_vmem(eigvecs),
+    )
 
 
 def split3(x):
@@ -206,12 +243,10 @@
 
 
 def per_device(table, coefs, targets, eigvecs, correction, batch_idx, nystrom_idx):
-    c_rows = table.shape[0]
-    first_row = lax.axis_index("ctr") * c_rows
-    own = coefs.T
+    picked, local_idx = pick(batch_idx, nystrom_idx.reshape(-1, LANES), table)
+    picked, own = lax.optimization_barrier((picked.reshape(N_CTR, -1, D), coefs.T))
     from_z = [lax.ppermute(own, "bat", z_shift(k)) if k else own for k in range(N_Z)]
 
-    picked = pick(batch_idx, table).reshape(N_CTR, -1, D)
     parts = lax.all_to_all(picked, "ctr", 0, 0)
     own_points = jnp.sum(parts.astype(F32), axis=0).astype(BF16)
     spread = jnp.broadcast_to(own_points[None], parts.shape)
@@ -219,7 +254,7 @@
 
     points, *from_z = lax.optimization_barrier((points, *from_z))
     pieces = [x for here in from_z for x in (here, lax.ppermute(here, "bat", SWAP))]
-    partial = main(nystrom_idx - first_row, points, table, pieces, eigvecs)
+    partial = main(local_idx.reshape(-1), points, table, pieces, eigvecs)
     mine = jnp.sum(lax.all_to_all(partial, "ctr", 0, 0), axis=0)
     comp = jnp.broadcast_to(mine[None, :16], (N_Z, 16, LANES))
     pred = jnp.pad(mine[16:].reshape(N_Z, 4, LANES), ((0, 0), (0, 4), (0, 0)))

time: 107 us -> 99.4 us (0.929)
  local copies, waits for them, and re-layouts: 7.26 us -> 1.64 us
  Pallas kernels: 24.9 us -> 22.7 us
    unnamed x12, local copies, waits for them, and re-layouts: 6.44 us -> 1.54 us
    pallas_call x2, Pallas kernels: 21.9 us -> 19.8 us  [the longest x1 16.7 us: main(): pl.pallas_call(main_kernel, in_specs=[SMEM, VMEM, HBM] + [VMEM] * 9, out_...]
  transfers between devices with their start and end apart: 8 -> 8, of which waited for: 4 -> 4; matrix products, arithmetic and copies ran while one was open for 2% -> 1% of each run, Pallas kernels for 5% -> 0%
where the time goes in v2:
time: 99.4 us; the launch traced here: 97.9 us
  blocking collectives  59.4 us (60%)
  Pallas kernels  22.7 us (23%)
  starting transfers between devices  6.75 us (7%)
  waiting for transfers between devices  5.64 us (6%)
  local copies, waits for them, and re-layouts  1.64 us (2%)
  other arithmetic  1.02 us (1%)
    all_to_all x1, blocking collectives, per_device(): lax.all_to_all(sent, ('ctr', 'bat'), 0, 0, axis_index_groups=SAME_CORE)  20.1 us
    pallas_call x1, Pallas kernels, main(): pl.pallas_call(main_kernel, in_specs=[SMEM, VMEM, HBM] + [VMEM] * 9, out_...  16.7 us
    all_to_all x1, blocking collectives, per_device(): parts = lax.all_to_all(picked, 'ctr', 0, 0)  15.5 us
    all_to_all x1, blocking collectives, per_device(): mine = jnp.sum(lax.all_to_all(partial, 'ctr', 0, 0), axis=0)  12.2 us
    all_to_all x1, blocking collectives, per_device(): points = lax.all_to_all(spread, 'ctr', 0, 0).reshape(-1, D)  11.6 us
    ppermute x3, starting transfers between devices, per_device(): lax.ppermute(own, 'bat', z_shift(k))  5.66 us
    ppermute x4, waiting for transfers between devices, per_device(): lax.ppermute(here, 'bat', SWAP)  3.35 us
    pallas_call x1, Pallas kernels, pick(): pl.pallas_call(pick_kernel, in_specs=[SMEM, VMEM, HBM], out_specs=[VMEM,...  3.05 us
  transfers between devices with their start and end apart: 8, of which 4 were waited for; matrix products, arithmetic and copies ran while one was open for 1% of the time, Pallas kernels for 0%

profile of v2, /device:TPU:0, one launch (start us, length us, event | category | flops | bytes accessed | tf_op | source)
XLA Modules:
  0.0 97.9 jit_solution(2973209083850210288)
XLA Ops:
  0.7 0.9 copy-done.3
  1.5 0.7 copy-done.5
  2.2 3.0 %pick.1 = (bf16[128,1024]{1,0:T(8,128)(2,1)S(1)}, s32[32,128]{1,0:T(8,128)S(1)}) custom-call(s32[128]{0:T(128)S(1)} %copy-done.5, s32[32,128]{1,0:T(8,128)S(1)} %bitcast.20, bf16[8192,1024]{1,0:T(8,128)(2,1)} %table_ref.3), custom_call_target="tpu_custom_call" | custom-call | tf_op jit(solution)/shard_map/pick/pallas_call | solution.py:74
  5.2 0.0 copy-start.2
  5.2 0.0 copy-start.4
  5.3 4.3 %collective-permute-start.2 = (bf16[32,8192]{1,0:T(8,128)(2,1)S(1)}, bf16[32,8192]{1,0:T(8,128)(2,1)S(1)}, u32[]{:S(2)}, u32[]{:S(2)}) collective-permute-start(bf16[32,8192]{1,0:T(8,128)(2,1)S(1)} %bitcast.12), channel_id=1, source_target_pairs={{0,6},{1,7},{2,0},{3,1},{4,2},{5,3},{6,4},{7,5},{8,14},{9,15},{10,... | collective-permute-start | bytes 1572872 | tf_op jit(solution)/shard_map/ppermute | solution.py:248
  9.5 0.1 collective-permute-start.1
  9.6 1.3 %collective-permute-start = (bf16[32,8192]{1,0:T(8,128)(2,1)S(1)}, bf16[32,8192]{1,0:T(8,128)(2,1)}, u32[]{:S(2)}, u32[]{:S(2)}) collective-permute-start(bf16[32,8192]{1,0:T(8,128)(2,1)S(1)} %bitcast.14), channel_id=1, source_target_pairs={{0,2},{1,3},{2,4},{3,5},{4,6},{5,7},{6,0},{7,1},{8,10},{9,11},{10,... | collective-permute-start | bytes 1572872 | tf_op jit(solution)/shard_map/ppermute | solution.py:248
  10.9 15.5 %all_to_all.20 = bf16[16,8,1024]{2,1,0:T(8,128)(2,1)} all-to-all(bf16[16,8,1024]{2,1,0:T(8,128)(2,1)S(1)} %bitcast.17), channel_id=1, replica_groups=mesh['ctr'=16,'bat'=8] {'ctr'}, dimensions={0} | all-to-all | bytes 524288 | tf_op jit(solution)/shard_map/all_to_all | solution.py:250
  26.4 1.0 %reduce_sum.21 = bf16[8,1024]{1,0:T(8,128)(2,1)S(1)} reduce(bf16[16,8,1024]{2,1,0:T(8,128)(2,1)} %all_to_all.20, bf16[]{:T(256)} %constant.4.clone.1), dimensions={0}, to_apply=%region_0.0 | reduce | flops 122880 | bytes 278530 | tf_op jit(solution)/shard_map/reduce_sum | solution.py:251
  27.4 11.6 %all_to_all.21 = bf16[16,8,1024]{2,1,0:T(8,128)(2,1)S(1)} all-to-all(bf16[16,8,1024]{2,1,0:T(8,128)(2,1)S(1)} %broadcast_in_dim.8), channel_id=1, replica_groups=mesh['ctr'=16,'bat'=8] {'ctr'}, dimensions={0} | all-to-all | bytes 524288 | tf_op jit(solution)/shard_map/all_to_all | solution.py:253
  39.0 0.1 collective-permute-start.3
  39.1 0.5 collective-permute-start.4
  39.6 0.1 collective-permute-start.5
  39.7 0.4 collective-permute-start.6
  40.1 0.9 collective-permute-done.3.rest_1_
  41.0 1.7 %collective-permute-done.4.rest_3_ = bf16[32,8192]{1,0:T(8,128)(2,1)S(1)} collective-permute-done((bf16[32,8192]{1,0:T(8,128)(2,1)}, bf16[32,8192]{1,0:T(8,128)(2,1)S(1)}, u32[]{:S(2)}, u32[]{:S(2)}) %collective-permute-start.4) | collective-permute-done | bytes 524320 | tf_op jit(solution)/shard_map/ppermute | solution.py:256
  42.7 0.8 collective-permute-done.5.rest_5_
  43.5 16.7 %main.1 = f32[16,32,128]{2,1,0:T(8,128)S(1)} custom-call(s32[4096]{0:T(1024)S(1)} %bitcast.19, bf16[128,1024]{1,0:T(8,128)(2,1)S(1)} %bitcast.11, bf16[8192,1024]{1,0:T(8,128)(2,1)} %table_ref.3, bf16[32,8192]{1,0:T(8,128)(2,1)S(1)} %bitcast.16, bf16[32,8192]{1,0:T(8,128)(2,1)S(1)} %collective-permute-done.3.rest_1_, ...), custom_call_target="tpu_custom_call" | custom-call | flops 3000000000 | bytes 25165824 | tf_op jit(solution)/shard_map/main/pallas_call | solution.py:173
  60.2 12.2 %all_to_all.22 = f32[16,32,128]{2,1,0:T(8,128)S(1)} all-to-all(f32[16,32,128]{2,1,0:T(8,128)S(1)} %main.1), channel_id=1, replica_groups=mesh['ctr'=16,'bat'=8] {'ctr'}, dimensions={0} | all-to-all | bytes 524288 | tf_op jit(solution)/shard_map/all_to_all | solution.py:258
  72.4 0.1 broadcast_in_dim.10
  72.5 20.1 %all_to_all.23.same_ref = f32[64,24,128]{2,1,0:T(8,128)S(1)} all-to-all(f32[64,24,128]{2,1,0:T(8,128)S(1)} %bitcast.22), channel_id=1, replica_groups={{0,2,4,6,8,10,12,14,16,18,20,22,24,26,28,30,32,34,36,38,40,42,44,46,48,..., dimensions={0} | all-to-all | bytes 1572864 | tf_op jit(solution)/shard_map/all_to_all | solution.py:263
  92.6 2.3 %collective-permute-done.7.other_ref = f32[64,24,128]{2,1,0:T(8,128)S(1)} collective-permute-done((f32[64,24,128]{2,1,0:T(8,128)S(1)}, f32[64,24,128]{2,1,0:T(8,128)S(1)}, u32[]{:S(2)}, u32[]{:S(2)}) %collective-permute-start.7) | collective-permute-done | bytes 786464 | tf_op jit(solution)/shard_map/ppermute | solution.py:264
  94.9 3.0 %final.1 = (f32[32,1024]{1,0:T(8,128)}, f32[32,4096]{1,0:T(8,128)}) custom-call(f32[64,24,128]{2,1,0:T(8,128)S(1)} %all_to_all.23.same_ref, f32[64,24,128]{2,1,0:T(8,128)S(1)} %collective-permute-done.7.other_ref, f32[32,1024]{1,0:T(8,128)S(1)} %bitcast.18, f32[1,256]{1,0:T(1,128)S(1)} %bitcast.21, bf16[4096,256]{1,0:T(8,128)(2,1)S(1)} %copy-done), custom_call_target="tpu_custom_call" | custom-call | tf_op jit(solution)/shard_map/final/pallas_call | solution.py:231
  (18 shorter events, 0.1 us)
Async XLA Ops:
  0.6 4.6 %copy-start.1 = (bf16[8192,32]{0,1:T(8,128)(2,1)S(1)}, bf16[8192,32]{0,1:T(8,128)(2,1)}, u32[]{:S(2)}) copy-start(bf16[8192,32]{0,1:T(8,128)(2,1)} %param.8) | copy-start | bytes 1572868
  0.6 42.8 %copy-start = (bf16[4096,256]{1,0:T(8,128)(2,1)S(1)}, bf16[4096,256]{1,0:T(8,128)(2,1)}, u32[]{:S(2)}) copy-start(bf16[4096,256]{1,0:T(8,128)(2,1)} %eig_ref.1) | copy-start | bytes 6291460
  0.7 0.9 copy-start.3
  1.5 0.7 copy-start.5
  5.2 89.7 %copy-start.2 = (f32[1024,32]{0,1:T(8,128)S(1)}, f32[1024,32]{0,1:T(8,128)}, u32[]{:S(2)}) copy-start(f32[1024,32]{0,1:T(8,128)} %param.9) | copy-start | bytes 393220
  5.2 89.7 %copy-start.4 = (f32[256]{0:T(256)S(1)}, f32[256]{0:T(256)}, u32[]{:S(2)}) copy-start(f32[256]{0:T(256)} %param.11) | copy-start | bytes 3076
  5.3 33.7 %collective-permute-start.2 = (bf16[32,8192]{1,0:T(8,128)(2,1)S(1)}, bf16[32,8192]{1,0:T(8,128)(2,1)S(1)}, u32[]{:S(2)}, u32[]{:S(2)}) collective-permute-start(bf16[32,8192]{1,0:T(8,128)(2,1)S(1)} %bitcast.12), channel_id=1, source_target_pairs={{0,6},{1,7},{2,0},{3,1},{4,2},{5,3},{6,4},{7,5},{8,14},{9,15},{10,... | collective-permute-start | bytes 1572872 | tf_op jit(solution)/shard_map/ppermute | solution.py:248
  9.5 29.5 %collective-permute-start.1 = (bf16[32,8192]{1,0:T(8,128)(2,1)S(1)}, bf16[32,8192]{1,0:T(8,128)(2,1)}, u32[]{:S(2)}, u32[]{:S(2)}) collective-permute-start(bf16[32,8192]{1,0:T(8,128)(2,1)S(1)} %bitcast.13), channel_id=1, source_target_pairs={{0,4},{1,5},{2,6},{3,7},{4,0},{5,1},{6,2},{7,3},{8,12},{9,13},{10,... | collective-permute-start | bytes 1572872 | tf_op jit(solution)/shard_map/ppermute | solution.py:248
  9.6 29.4 %collective-permute-start = (bf16[32,8192]{1,0:T(8,128)(2,1)S(1)}, bf16[32,8192]{1,0:T(8,128)(2,1)}, u32[]{:S(2)}, u32[]{:S(2)}) collective-permute-start(bf16[32,8192]{1,0:T(8,128)(2,1)S(1)} %bitcast.14), channel_id=1, source_target_pairs={{0,2},{1,3},{2,4},{3,5},{4,6},{5,7},{6,0},{7,1},{8,10},{9,11},{10,... | collective-permute-start | bytes 1572872 | tf_op jit(solution)/shard_map/ppermute | solution.py:248
  39.0 2.0 %collective-permute-start.3 = (bf16[32,8192]{1,0:T(8,128)(2,1)S(1)}, bf16[32,8192]{1,0:T(8,128)(2,1)S(1)}, u32[]{:S(2)}, u32[]{:S(2)}) collective-permute-start(bf16[32,8192]{1,0:T(8,128)(2,1)S(1)} %bitcast.15), channel_id=1, source_target_pairs={{0,1},{1,0},{2,3},{3,2},{4,5},{5,4},{6,7},{7,6},{8,9},{9,8},{10,11... | collective-permute-start | bytes 1572872 | tf_op jit(solution)/shard_map/ppermute | solution.py:256
  39.1 3.6 %collective-permute-start.4 = (bf16[32,8192]{1,0:T(8,128)(2,1)}, bf16[32,8192]{1,0:T(8,128)(2,1)S(1)}, u32[]{:S(2)}, u32[]{:S(2)}) collective-permute-start(bf16[32,8192]{1,0:T(8,128)(2,1)} %collective-permute-done.rest_2_), channel_id=1, source_target_pairs={{0,1},{1,0},{2,3},{3,2},{4,5},{5,4},{6,7},{7,6},{8,9},{9,8},{10,11... | collective-permute-start | bytes 1572872 | tf_op jit(solution)/shard_map/ppermute | solution.py:256
  39.6 3.9 %collective-permute-start.5 = (bf16[32,8192]{1,0:T(8,128)(2,1)}, bf16[32,8192]{1,0:T(8,128)(2,1)S(1)}, u32[]{:S(2)}, u32[]{:S(2)}) collective-permute-start(bf16[32,8192]{1,0:T(8,128)(2,1)} %collective-permute-done.1.rest_4_), channel_id=1, source_target_pairs={{0,1},{1,0},{2,3},{3,2},{4,5},{5,4},{6,7},{7,6},{8,9},{9,8},{10,11... | collective-permute-start | bytes 1572872 | tf_op jit(solution)/shard_map/ppermute | solution.py:256
  39.7 3.8 %collective-permute-start.6 = (bf16[32,8192]{1,0:T(8,128)(2,1)S(1)}, bf16[32,8192]{1,0:T(8,128)(2,1)S(1)}, u32[]{:S(2)}, u32[]{:S(2)}) collective-permute-start(bf16[32,8192]{1,0:T(8,128)(2,1)S(1)} %collective-permute-done.2.rest_6_), channel_id=1, source_target_pairs={{0,1},{1,0},{2,3},{3,2},{4,5},{5,4},{6,7},{7,6},{8,9},{9,8},{10,11... | collective-permute-start | bytes 1572872 | tf_op jit(solution)/shard_map/ppermute | solution.py:256
  92.6 2.3 %collective-permute-start.7 = (f32[64,24,128]{2,1,0:T(8,128)S(1)}, f32[64,24,128]{2,1,0:T(8,128)S(1)}, u32[]{:S(2)}, u32[]{:S(2)}) collective-permute-start(f32[64,24,128]{2,1,0:T(8,128)S(1)} %all_to_all.23.same_ref), channel_id=1, source_target_pairs={{0,1},{1,0},{2,3},{3,2},{4,5},{5,4},{6,7},{7,6},{8,9},{9,8},{10,11... | collective-permute-start | bytes 2359304 | tf_op jit(solution)/shard_map/ppermute | solution.py:264

commit v3 on v2

--- a/solution.py
+++ b/solution.py
@@ -13,6 +13,7 @@
 N_Z = 4
 LANES = 128
 GROUP = 16
+SLOTS = 24
 MIB = 2**20
 F32 = jnp.float32
 BF16 = jnp.bfloat16
@@ -31,20 +32,33 @@
     return pltpu.with_memory_space_constraint(x, pltpu.VMEM)
 
 
-def pick_kernel(idx_ref, nys_ref, table_ref, out_ref, local_ref, listed, groups, rows, sems):
-    n = rows.shape[0]
+def pick_kernel(first, *refs):
+    round_ref = None if first else refs[0]
+    idx_hbm, table_ref, out_ref, rounds_ref, idx_ref, counts, listed, groups, rows, sems = refs[0 if first else 1:]
+    n = listed.shape[0] - 1
     c_rows = table_ref.shape[0]
-    first_row = lax.axis_index("ctr") * c_rows
-
-    def note(i, count):
-        pos = idx_ref[i] - first_row
-        listed[count] = i
-        return count + jnp.where((pos >= 0) & (pos < c_rows), 1, 0)
-
-    count = lax.fori_loop(0, n, note, 0, unroll=8)
+    ctr = lax.axis_index("ctr")
+    idx_copy = pltpu.make_async_copy(idx_hbm, idx_ref, sems.at[SLOTS])
+    idx_copy.start()
+    rows[...] = jnp.zeros_like(rows)
+    for c in range(N_CTR):
+        counts[c] = 0
+    idx_copy.wait()
+
+    def note(i, most):
+        owner = idx_ref[i] // c_rows
+        count = counts[owner]
+        listed[jnp.where(owner == ctr, count, n)] = i
+        counts[owner] = count + 1
+        return jnp.maximum(most, count + 1)
+
+    most = lax.fori_loop(0, n, note, 0, unroll=8)
+    rounds_ref[0] = (most + SLOTS - 1) // SLOTS
+    done = 0 if first else round_ref[0] * SLOTS
+    count = jnp.clip(counts[ctr] - done, 0, SLOTS)
 
     def copy_of(s):
-        pos = idx_ref[listed[s]] - first_row
+        pos = idx_ref[listed[done + s]] - ctr * c_rows
         start = pl.multiple_of(pos // GROUP * GROUP, GROUP)
         return pltpu.make_async_copy(table_ref.at[pl.ds(start, GROUP)], groups.at[s], sems.at[s])
 
@@ -52,54 +66,90 @@
         copy_of(s).start()
         return carry
 
-    lax.fori_loop(0, count, start, 0)
-    local_ref[...] = nys_ref[...] - first_row
-    rows[...] = jnp.zeros_like(rows)
-
     def finish(s, carry):
         copy_of(s).wait()
-        i = listed[s]
         group = groups[s].astype(F32)
         place = lax.broadcasted_iota(jnp.int32, group.shape, 0)
-        kept = jnp.where(place == (idx_ref[i] - first_row) % GROUP, group, 0.0)
-        rows[pl.ds(i, 1), :] = jnp.sum(kept, axis=0, keepdims=True)
+        kept = jnp.where(place == idx_ref[listed[done + s]] % GROUP, group, 0.0)
+        rows[pl.ds(s, 1), :] = jnp.sum(kept, axis=0, keepdims=True)
         return carry
 
+    lax.fori_loop(0, count, start, 0)
     lax.fori_loop(0, count, finish, 0)
-    out_ref[...] = rows[...].astype(BF16)
-
-
-def pick(batch_idx, nystrom_idx, table):
+    packed = rows[...].astype(BF16)
+    for c in range(N_CTR):
+        out_ref[c] = packed
+
+
+def pick(batch_idx, table, at_round=None):
     n = batch_idx.shape[0]
-    return pl.pallas_call(
-        pick_kernel,
-        in_specs=[SMEM, VMEM, HBM],
-        out_specs=[VMEM, VMEM],
+    first = at_round is None
+    return pl.pallas_call(
+        functools.partial(pick_kernel, first),
+        in_specs=([] if first else [SMEM]) + [HBM, HBM],
+        out_specs=[VMEM, SMEM],
         out_shape=[
-            jax.ShapeDtypeStruct((n, D), BF16),
-            jax.ShapeDtypeStruct(nystrom_idx.shape, jnp.int32),
+            jax.ShapeDtypeStruct((N_CTR, SLOTS, D), BF16),
+            jax.ShapeDtypeStruct((1,), jnp.int32),
         ],
         scratch_shapes=[
+            pltpu.SMEM((n,), jnp.int32),
+            pltpu.SMEM((N_CTR,), jnp.int32),
             pltpu.SMEM((n + 1,), jnp.int32),
-            pltpu.VMEM((n, GROUP, D), BF16),
-            pltpu.VMEM((n, D), F32),
-            pltpu.SemaphoreType.DMA((n,)),
+            pltpu.VMEM((SLOTS, GROUP, D), BF16),
+            pltpu.VMEM((SLOTS, D), F32),
+            pltpu.SemaphoreType.DMA((SLOTS + 1,)),
         ],
         compiler_params=pltpu.CompilerParams(vmem_limit_bytes=8 * MIB),
         name="pick",
-    )(batch_idx, nystrom_idx, pltpu.with_memory_space_constraint(table, pltpu.HBM))
+    )(
+        *([] if first else [at_round]),
+        pltpu.with_memory_space_constraint(batch_idx, pltpu.HBM),
+        pltpu.with_memory_space_constraint(table, pltpu.HBM),
+    )
+
+
+def settled(idx_row, received, at_round, c_rows):
+    n = idx_row.shape[1]
+    owner_row = (idx_row // c_rows).astype(F32)
+    i = lax.broadcasted_iota(jnp.int32, (n, n), 0)
+    j = lax.broadcasted_iota(jnp.int32, (n, n), 1)
+    owner = jnp.sum(jnp.where(i == j, owner_row, 0.0), axis=1, keepdims=True)
+    before = (owner == owner_row) & (j < i)
+    slot = jnp.sum(jnp.where(before, 1.0, 0.0), axis=1, keepdims=True) - at_round * SLOTS
+    here = (slot >= 0.0) & (slot < SLOTS)
+    place = jnp.where(here, owner * SLOTS + slot, -1.0)
+    column = lax.broadcasted_iota(jnp.int32, (n, N_CTR * SLOTS), 1).astype(F32)
+    chosen = jnp.where(column == place, 1.0, 0.0).astype(BF16)
+    return jnp.dot(chosen, received, preferred_element_type=F32)
+
+
+def settle_kernel(c_rows, round_ref, idx_ref, received_ref, before_ref, out_ref):
+    at_round = round_ref[0].astype(F32)
+    rows = settled(idx_ref[...], received_ref[...], at_round, c_rows)
+    out_ref[...] = (rows + before_ref[...].astype(F32)).astype(BF16)
+
+
+def settle(at_round, idx_row, received, before, c_rows):
+    return pl.pallas_call(
+        functools.partial(settle_kernel, c_rows),
+        in_specs=[SMEM, VMEM, VMEM, VMEM],
+        out_specs=VMEM,
+        out_shape=jax.ShapeDtypeStruct(before.shape, BF16),
+        compiler_params=pltpu.CompilerParams(vmem_limit_bytes=8 * MIB),
+        name="settle",
+    )(at_round, idx_row, received, before)
 
 
 N_TILES = 8
 
 
-def main_kernel(idx_ref, pts_ref, table_ref, *rest):
-    coef_refs = rest[:8]
-    eig_ref, out_ref, held, cross, kern, kern16, nys, acc, sems = rest[8:]
-
+def kern_kernel(
+    idx_ref, received_ref, more_ref, nys_ref, table_ref, kern, kern16, local_ref, held, pts_ref, cross, sems
+):
     n_tiles = sems.shape[0]
-    tile = held.shape[0] // n_tiles
-    q = eig_ref.shape[1]
+    c_rows = held.shape[0]
+    tile = c_rows // n_tiles
 
     def rows_of(i):
         return pl.ds(pl.multiple_of(i * tile, tile), tile)
@@ -110,7 +160,9 @@
 
     for i in range(n_tiles):
         copy_of(i).start()
-    pts = pts_ref[...].astype(F32)
+    local_ref[...] = nys_ref[...] - lax.axis_index("ctr") * c_rows
+    pts = settled(idx_ref[...], received_ref[...], 0.0, c_rows) + more_ref[...].astype(F32)
+    pts_ref[...] = pts.astype(BF16)
     pts_sq = lax.dot_general(
         jnp.ones((8, D), F32), pts * pts, (((1,), (1,)), ((), ())),
         precision=lax.Precision.HIGHEST, preferred_element_type=F32,
@@ -139,6 +191,32 @@
     lax.fori_loop(1, n_tiles, both, 0)
     finish(n_tiles - 1)
 
+
+def kernel_rows(idx_row, received, more, nystrom_idx, table):
+    c_rows = table.shape[0]
+    n = idx_row.shape[1]
+    return pl.pallas_call(
+        kern_kernel,
+        in_specs=[VMEM, VMEM, VMEM, VMEM, HBM],
+        out_specs=[VMEM, VMEM, VMEM],
+        out_shape=[
+            jax.ShapeDtypeStruct((c_rows, n), F32),
+            jax.ShapeDtypeStruct((c_rows, n), BF16),
+            jax.ShapeDtypeStruct(nystrom_idx.shape, jnp.int32),
+        ],
+        scratch_shapes=[
+            pltpu.VMEM((c_rows, D), BF16),
+            pltpu.VMEM((n, D), BF16),
+            pltpu.VMEM((2, c_rows // N_TILES, n), F32),
+            pltpu.SemaphoreType.DMA((N_TILES,)),
+        ],
+        compiler_params=pltpu.CompilerParams(vmem_limit_bytes=30 * MIB),
+        cost_estimate=pl.CostEstimate(flops=10**10, bytes_accessed=24 * MIB, transcendentals=10**6),
+        name="kernel_rows",
+    )(idx_row, received, more, nystrom_idx, pltpu.with_memory_space_constraint(table, pltpu.HBM))
+
+
+def comp_kernel(idx_ref, kern, eig_ref, out_ref, nys):
     unroll = 32
 
     def gather(j, carry):
@@ -148,13 +226,33 @@
         return carry
 
     lax.fori_loop(0, nys.shape[0] // unroll, gather, 0)
+    out_ref[...] = lax.dot_general(
+        eig_ref[...], nys[...].astype(BF16), (((0,), (0,)), ((), ())), preferred_element_type=F32
+    )
+
+
+def components(local_idx, kern, eigvecs):
+    m_rows, q = eigvecs.shape
+    n = kern.shape[1]
+    return pl.pallas_call(
+        comp_kernel,
+        in_specs=[SMEM, VMEM, VMEM],
+        out_specs=VMEM,
+        out_shape=jax.ShapeDtypeStruct((q, n), F32),
+        scratch_shapes=[pltpu.VMEM((m_rows, n), F32)],
+        compiler_params=pltpu.CompilerParams(vmem_limit_bytes=16 * MIB),
+        cost_estimate=pl.CostEstimate(flops=5 * 10**9, bytes_accessed=6 * MIB, transcendentals=0),
+        name="components",
+    )(local_idx, kern, in_vmem(eigvecs))
+
+
+def pred_kernel(comp_ref, kern16, *rest):
+    coef_refs = rest[:8]
+    out_ref, acc = rest[8:]
     coefs = jnp.concatenate([ref[...] for ref in coef_refs], axis=0)
     acc[...] = jnp.dot(coefs, kern16[...], preferred_element_type=F32)
-    comp = lax.dot_general(
-        eig_ref[...], nys[...].astype(BF16), (((0,), (0,)), ((), ())), preferred_element_type=F32
-    )
     for c in range(N_CTR):
-        out_ref[c, 0:16, :] = comp[c * 16:(c + 1) * 16]
+        out_ref[c, 0:16, :] = comp_ref[c * 16:(c + 1) * 16, :]
     bat = lax.axis_index("bat")
     z = bat // 2
     core = bat % 2
@@ -167,30 +265,16 @@
                 out_ref[from_core * 8 + i, pl.ds(16 + from_z * 4, 4), :] = acc[first + 4 * i:first + 4 * i + 4]
 
 
-def main(local_idx, points, table, pieces, eigvecs):
-    c_rows = table.shape[0]
-    m_rows, q = eigvecs.shape
-    return pl.pallas_call(
-        main_kernel,
-        in_specs=[SMEM, VMEM, HBM] + [VMEM] * 9,
+def predict(comp, kern16, pieces):
+    return pl.pallas_call(
+        pred_kernel,
+        in_specs=[VMEM] * 10,
         out_specs=VMEM,
         out_shape=jax.ShapeDtypeStruct((N_CTR, 32, LANES), F32),
-        scratch_shapes=[
-            pltpu.VMEM((c_rows, D), BF16),
-            pltpu.VMEM((2, c_rows // N_TILES, LANES), F32),
-            pltpu.VMEM((c_rows, LANES), F32),
-            pltpu.VMEM((c_rows, LANES), BF16),
-            pltpu.VMEM((m_rows, LANES), F32),
-            pltpu.VMEM((256, LANES), F32),
-            pltpu.SemaphoreType.DMA((N_TILES,)),
-        ],
-        compiler_params=pltpu.CompilerParams(vmem_limit_bytes=40 * MIB),
-        cost_estimate=pl.CostEstimate(flops=3 * 10**9, bytes_accessed=24 * MIB, transcendentals=10**6),
-        name="main",
-    )(
-        local_idx, points, pltpu.with_memory_space_constraint(table, pltpu.HBM),
-        *[in_vmem(x) for x in pieces], in_vmem(eigvecs),
-    )
+        scratch_shapes=[pltpu.VMEM((256, LANES), F32)],
+        compiler_params=pltpu.CompilerParams(vmem_limit_bytes=16 * MIB),
+        name="predict",
+    )(comp, kern16, *[in_vmem(x) for x in pieces])
 
 
 def split3(x):
@@ -243,18 +327,31 @@
 
 
 def per_device(table, coefs, targets, eigvecs, correction, batch_idx, nystrom_idx):
-    picked, local_idx = pick(batch_idx, nystrom_idx.reshape(-1, LANES), table)
-    picked, own = lax.optimization_barrier((picked.reshape(N_CTR, -1, D), coefs.T))
+    c_rows = table.shape[0]
+    picked, rounds = pick(batch_idx, table)
+    picked, own = lax.optimization_barrier((picked, coefs.T))
     from_z = [lax.ppermute(own, "bat", z_shift(k)) if k else own for k in range(N_Z)]
 
-    parts = lax.all_to_all(picked, "ctr", 0, 0)
-    own_points = jnp.sum(parts.astype(F32), axis=0).astype(BF16)
-    spread = jnp.broadcast_to(own_points[None], parts.shape)
-    points = lax.all_to_all(spread, "ctr", 0, 0).reshape(-1, D)
-
-    points, *from_z = lax.optimization_barrier((points, *from_z))
+    idx_row = batch_idx.reshape(1, -1)
+    received = lax.all_to_all(picked, "ctr", 0, 0).reshape(-1, D)
+
+    def further(state):
+        at_round, more = state
+        sent, _ = pick(batch_idx, table, at_round.reshape(1))
+        got = lax.all_to_all(sent, "ctr", 0, 0).reshape(-1, D)
+        return at_round + 1, settle(at_round.reshape(1), idx_row, got, more, c_rows)
+
+    none = jnp.zeros((batch_idx.shape[0], D), BF16)
+    _, more = lax.while_loop(lambda state: state[0] < rounds[0], further, (jnp.int32(1), none))
+
+    kern, kern16, local_idx = kernel_rows(
+        idx_row, received, more, nystrom_idx.reshape(-1, LANES), table
+    )
+    kern, *from_z = lax.optimization_barrier((kern, *from_z))
     pieces = [x for here in from_z for x in (here, lax.ppermute(here, "bat", SWAP))]
-    partial = main(local_idx.reshape(-1), points, table, pieces, eigvecs)
+    comp = components(local_idx.reshape(-1), kern, eigvecs)
+    comp, *pieces = lax.optimization_barrier((comp, *pieces))
+    partial = predict(comp, kern16, pieces)
     mine = jnp.sum(lax.all_to_all(partial, "ctr", 0, 0), axis=0)
     comp = jnp.broadcast_to(mine[None, :16], (N_Z, 16, LANES))
     pred = jnp.pad(mine[16:].reshape(N_Z, 4, LANES), ((0, 0), (0, 4), (0, 0)))

time: 99.4 us -> 92.8 us (0.934)
  blocking collectives: 59.4 us -> 35.9 us
  starting transfers between devices: 6.75 us -> 14.8 us
  waiting for transfers between devices: 5.64 us -> 12.9 us
  Pallas kernels: 22.7 us -> 26 us
  local copies, waits for them, and re-layouts: 1.64 us -> 0.14 us
    all_to_all x2 -> x0, blocking collectives: 27.1 us -> none  [the longest x1 15.5 us: per_device(): parts = lax.all_to_all(picked, 'ctr', 0, 0)]
    all_to_all x0 -> x1, waiting for transfers between devices: none -> 8.02 us  [per_device(): received = lax.all_to_all(picked, 'ctr', 0, 0).reshape(-1, D)]
    all_to_all x0 -> x1, starting transfers between devices: none -> 7.19 us  [per_device(): received = lax.all_to_all(picked, 'ctr', 0, 0).reshape(-1, D)]
    all_to_all x1, blocking collectives: 12.2 us -> 15.6 us  [per_device(): mine = jnp.sum(lax.all_to_all(partial, 'ctr', 0, 0), axis=0)]
    ppermute x4, waiting for transfers between devices: 3.35 us -> 0.01 us  [per_device(): lax.ppermute(here, 'bat', SWAP)]
    pallas_call x2 -> x4, Pallas kernels: 19.8 us -> 23 us  [the longest x1 11 us: kernel_rows(): pl.pallas_call(kern_kernel, in_specs=[VMEM, VMEM, VMEM, VMEM, HBM], out_s...]
    ppermute x3, waiting for transfers between devices: 0.01 us -> 2.61 us  [per_device(): lax.ppermute(own, 'bat', z_shift(k))]
    unnamed x12 -> x14, local copies, waits for them, and re-layouts: 1.54 us -> 0.04 us
  transfers between devices with their start and end apart: 8 -> 9, of which waited for: 4 -> 3; matrix products, arithmetic and copies ran while one was open for 1% -> 0% of each run, Pallas kernels for 0% -> 18%
where the time goes in v3:
time: 92.8 us; the launch traced here: 91.3 us
  blocking collectives  35.9 us (39%)
  Pallas kernels  26 us (28%)
  starting transfers between devices  14.8 us (16%)
  waiting for transfers between devices  12.9 us (14%)
    all_to_all x1, blocking collectives, per_device(): lax.all_to_all(sent, ('ctr', 'bat'), 0, 0, axis_index_groups=SAME_CORE)  20.3 us
    all_to_all x1, blocking collectives, per_device(): mine = jnp.sum(lax.all_to_all(partial, 'ctr', 0, 0), axis=0)  15.6 us
    pallas_call x1, Pallas kernels, kernel_rows(): pl.pallas_call(kern_kernel, in_specs=[VMEM, VMEM, VMEM, VMEM, HBM], out_s...  11 us
    all_to_all x1, waiting for transfers between devices, per_device(): received = lax.all_to_all(picked, 'ctr', 0, 0).reshape(-1, D)  8.02 us
    all_to_all x1, starting transfers between devices, per_device(): received = lax.all_to_all(picked, 'ctr', 0, 0).reshape(-1, D)  7.19 us
    ppermute x3, starting transfers between devices, per_device(): lax.ppermute(own, 'bat', z_shift(k))  6.58 us
    pallas_call x1, Pallas kernels, components(): pl.pallas_call(comp_kernel, in_specs=[SMEM, VMEM, VMEM], out_specs=VMEM,...  5.32 us
    pallas_call x1, Pallas kernels, pick(): pl.pallas_call(functools.partial(pick_kernel, first), in_specs=([] if fir...  4.03 us
  transfers between devices with their start and end apart: 9, of which 3 were waited for; matrix products, arithmetic and copies ran while one was open for 0% of the time, Pallas kernels for 18%

profile of v3, /device:TPU:0, one launch (start us, length us, event | category | flops | bytes accessed | tf_op | source)
XLA Modules:
  0.0 91.3 jit_solution(5229016543786871556)
XLA Ops:
  0.6 0.0 copy-start.6
  0.6 4.0 %pick.2 = (bf16[16,24,1024]{2,1,0:T(8,128)(2,1)}, s32[1]{0:T(128)}) custom-call(s32[128]{0:T(128)} %refs_0_.1, bf16[8192,1024]{1,0:T(8,128)(2,1)} %table_ref.1), custom_call_target="tpu_custom_call" | custom-call | tf_op jit(solution)/shard_map/pick/pallas_call | solution.py:87
  4.7 0.0 copy-start.1
  4.7 0.0 copy-start.4
  4.7 0.7 while.10
  5.5 0.0 copy-start.5
  5.5 7.2 %all-to-all-start.1 = ((bf16[16,24,1024]{2,1,0:T(8,128)(2,1)}), bf16[16,24,1024]{2,1,0:T(8,128)(2,1)S(1)}, u32[]{:S(2)}, u32[]{:S(2)}) async-start(bf16[16,24,1024]{2,1,0:T(8,128)(2,1)} %get-tuple-element.60), calls=%async_computation.1 | async-start | bytes 1572864 | tf_op jit(solution)/shard_map/all_to_all | solution.py:336
  12.7 2.0 %collective-permute-start = (bf16[32,8192]{1,0:T(8,128)(2,1)S(1)}, bf16[32,8192]{1,0:T(8,128)(2,1)}, u32[]{:S(2)}, u32[]{:S(2)}) collective-permute-start(bf16[32,8192]{1,0:T(8,128)(2,1)S(1)} %bitcast.21), channel_id=1, source_target_pairs={{0,2},{1,3},{2,4},{3,5},{4,6},{5,7},{6,0},{7,1},{8,10},{9,11},{10,... | collective-permute-start | bytes 1572872 | tf_op jit(solution)/shard_map/ppermute | solution.py:333
  14.6 3.6 %collective-permute-start.1 = (bf16[32,8192]{1,0:T(8,128)(2,1)S(1)}, bf16[32,8192]{1,0:T(8,128)(2,1)}, u32[]{:S(2)}, u32[]{:S(2)}) collective-permute-start(bf16[32,8192]{1,0:T(8,128)(2,1)S(1)} %bitcast.22), channel_id=1, source_target_pairs={{0,4},{1,5},{2,6},{3,7},{4,0},{5,1},{6,2},{7,3},{8,12},{9,13},{10,... | collective-permute-start | bytes 1572872 | tf_op jit(solution)/shard_map/ppermute | solution.py:333
  18.2 1.0 %collective-permute-start.2 = (bf16[32,8192]{1,0:T(8,128)(2,1)S(1)}, bf16[32,8192]{1,0:T(8,128)(2,1)}, u32[]{:S(2)}, u32[]{:S(2)}) collective-permute-start(bf16[32,8192]{1,0:T(8,128)(2,1)S(1)} %bitcast.23), channel_id=1, source_target_pairs={{0,6},{1,7},{2,0},{3,1},{4,2},{5,3},{6,4},{7,5},{8,14},{9,15},{10,... | collective-permute-start | bytes 1572872 | tf_op jit(solution)/shard_map/ppermute | solution.py:333
  19.3 8.0 %all-to-all-done.1 = bf16[16,24,1024]{2,1,0:T(8,128)(2,1)S(1)} async-done(((bf16[16,24,1024]{2,1,0:T(8,128)(2,1)}), bf16[16,24,1024]{2,1,0:T(8,128)(2,1)S(1)}, u32[]{:S(2)}, u32[]{:S(2)}) %all-to-all-start.1) | async-done | bytes 786464 | tf_op jit(solution)/shard_map/all_to_all | solution.py:336
  27.3 11.0 %kernel_rows.1 = (f32[8192,128]{1,0:T(8,128)S(1)}, bf16[8192,128]{1,0:T(8,128)(2,1)S(1)}, s32[32,128]{1,0:T(8,128)S(1)}) custom-call(s32[1,128]{1,0:T(1,128)S(1)} %get-tuple-element.176, bf16[384,1024]{1,0:T(8,128)(2,1)S(1)} %bitcast.20, bf16[128,1024]{1,0:T(8,128)(2,1)} %copy-done.5, s32[32,128]{1,0:T(8,128)S(1)} %bitcast.28, ...), custom_call_target="tpu_custom_call" | custom-call | flops 10000000000 | bytes 25165824 | tf_op jit(solution)/shard_map/kernel_rows/pallas_call | solution.py:198
  38.3 2.6 %collective-permute-done.1.rest_4_ = bf16[32,8192]{1,0:T(8,128)(2,1)} collective-permute-done((bf16[32,8192]{1,0:T(8,128)(2,1)S(1)}, bf16[32,8192]{1,0:T(8,128)(2,1)}, u32[]{:S(2)}, u32[]{:S(2)}) %collective-permute-start.1) | collective-permute-done | bytes 524320 | tf_op jit(solution)/shard_map/ppermute | solution.py:333
  40.9 0.5 collective-permute-start.4
  41.4 0.5 collective-permute-start.6
  41.9 5.3 %components.1.comp_ref = f32[256,128]{1,0:T(8,128)S(1)} custom-call(s32[4096]{0:T(1024)S(1)} %bitcast.29, f32[8192,128]{1,0:T(8,128)S(1)} %get-tuple-element.66.kern, bf16[4096,256]{1,0:T(8,128)(2,1)S(1)} %copy-done), custom_call_target="tpu_custom_call" | custom-call | flops 5000000000 | bytes 6291456 | tf_op jit(solution)/shard_map/components/pallas_call | solution.py:237
  47.3 0.0 copy-start.2
  47.3 0.0 copy-start.3
  47.3 2.7 %predict.1 = f32[16,32,128]{2,1,0:T(8,128)S(1)} custom-call(f32[256,128]{1,0:T(8,128)S(1)} %components.1.comp_ref, bf16[8192,128]{1,0:T(8,128)(2,1)S(1)} %get-tuple-element.72.kern16, bf16[32,8192]{1,0:T(8,128)(2,1)S(1)} %bitcast.25, bf16[32,8192]{1,0:T(8,128)(2,1)S(1)} %collective-permute-done.3.rest_1_, bf16[32,8192]{1,0:T(8,128)(2,1)} %collective-permute-done.rest_2_, ...), custom_call_target="tpu_custom_call" | custom-call | tf_op jit(solution)/shard_map/predict/pallas_call | solution.py:269
  50.0 15.6 %all_to_all.21 = f32[16,32,128]{2,1,0:T(8,128)S(1)} all-to-all(f32[16,32,128]{2,1,0:T(8,128)S(1)} %predict.1), channel_id=1, replica_groups=mesh['ctr'=16,'bat'=8] {'ctr'}, dimensions={0} | all-to-all | bytes 524288 | tf_op jit(solution)/shard_map/all_to_all | solution.py:355
  65.7 0.1 broadcast_in_dim.20
  65.7 20.3 %all_to_all.22.same_ref = f32[64,24,128]{2,1,0:T(8,128)S(1)} all-to-all(f32[64,24,128]{2,1,0:T(8,128)S(1)} %bitcast.30), channel_id=1, replica_groups={{0,2,4,6,8,10,12,14,16,18,20,22,24,26,28,30,32,34,36,38,40,42,44,46,48,..., dimensions={0} | all-to-all | bytes 1572864 | tf_op jit(solution)/shard_map/all_to_all | solution.py:360
  86.0 2.3 %collective-permute-done.7.other_ref = f32[64,24,128]{2,1,0:T(8,128)S(1)} collective-permute-done((f32[64,24,128]{2,1,0:T(8,128)S(1)}, f32[64,24,128]{2,1,0:T(8,128)S(1)}, u32[]{:S(2)}, u32[]{:S(2)}) %collective-permute-start.7) | collective-permute-done | bytes 786464 | tf_op jit(solution)/shard_map/ppermute | solution.py:361
  88.3 3.0 %final.1 = (f32[32,1024]{1,0:T(8,128)}, f32[32,4096]{1,0:T(8,128)}) custom-call(f32[64,24,128]{2,1,0:T(8,128)S(1)} %all_to_all.22.same_ref, f32[64,24,128]{2,1,0:T(8,128)S(1)} %collective-permute-done.7.other_ref, f32[32,1024]{1,0:T(8,128)S(1)} %bitcast.26, f32[1,256]{1,0:T(1,128)S(1)} %bitcast.27, bf16[4096,256]{1,0:T(8,128)(2,1)S(1)} %copy-done), custom_call_target="tpu_custom_call" | custom-call | tf_op jit(solution)/shard_map/final/pallas_call | solution.py:315
  (22 shorter events, 0.1 us)
Async XLA Ops:
  0.6 4.1 %copy-start.6 = (s32[128]{0:T(128)S(1)}, s32[128]{0:T(128)}, u32[]{:S(2)}) copy-start(s32[128]{0:T(128)} %refs_0_.1) | copy-start | bytes 1540
  4.7 8.0 %copy-start.1 = (bf16[8192,32]{0,1:T(8,128)(2,1)S(1)}, bf16[8192,32]{0,1:T(8,128)(2,1)}, u32[]{:S(2)}) copy-start(bf16[8192,32]{0,1:T(8,128)(2,1)} %param.10) | copy-start | bytes 1572868
  4.7 22.6 %copy-start.4 = (s32[4096]{0:T(1024)S(1)}, s32[4096]{0:T(1024)}, u32[]{:S(2)}) copy-start(s32[4096]{0:T(1024)} %param.15) | copy-start | bytes 49156
  5.5 21.8 %copy-start.5 = (bf16[128,1024]{1,0:T(8,128)(2,1)}, bf16[128,1024]{1,0:T(8,128)(2,1)S(1)}, u32[]{:S(2)}) copy-start(bf16[128,1024]{1,0:T(8,128)(2,1)S(1)} %get-tuple-element.172) | copy-start | bytes 786436
  5.5 21.8 %all-to-all-start.1 = ((bf16[16,24,1024]{2,1,0:T(8,128)(2,1)}), bf16[16,24,1024]{2,1,0:T(8,128)(2,1)S(1)}, u32[]{:S(2)}, u32[]{:S(2)}) async-start(bf16[16,24,1024]{2,1,0:T(8,128)(2,1)} %get-tuple-element.60), calls=%async_computation.1 | async-start | bytes 1572864 | tf_op jit(solution)/shard_map/all_to_all | solution.py:336
  12.7 25.6 %collective-permute-start = (bf16[32,8192]{1,0:T(8,128)(2,1)S(1)}, bf16[32,8192]{1,0:T(8,128)(2,1)}, u32[]{:S(2)}, u32[]{:S(2)}) collective-permute-start(bf16[32,8192]{1,0:T(8,128)(2,1)S(1)} %bitcast.21), channel_id=1, source_target_pairs={{0,2},{1,3},{2,4},{3,5},{4,6},{5,7},{6,0},{7,1},{8,10},{9,11},{10,... | collective-permute-start | bytes 1572872 | tf_op jit(solution)/shard_map/ppermute | solution.py:333
  14.6 26.3 %collective-permute-start.1 = (bf16[32,8192]{1,0:T(8,128)(2,1)S(1)}, bf16[32,8192]{1,0:T(8,128)(2,1)}, u32[]{:S(2)}, u32[]{:S(2)}) collective-permute-start(bf16[32,8192]{1,0:T(8,128)(2,1)S(1)} %bitcast.22), channel_id=1, source_target_pairs={{0,4},{1,5},{2,6},{3,7},{4,0},{5,1},{6,2},{7,3},{8,12},{9,13},{10,... | collective-permute-start | bytes 1572872 | tf_op jit(solution)/shard_map/ppermute | solution.py:333
  18.2 22.7 %collective-permute-start.2 = (bf16[32,8192]{1,0:T(8,128)(2,1)S(1)}, bf16[32,8192]{1,0:T(8,128)(2,1)}, u32[]{:S(2)}, u32[]{:S(2)}) collective-permute-start(bf16[32,8192]{1,0:T(8,128)(2,1)S(1)} %bitcast.23), channel_id=1, source_target_pairs={{0,6},{1,7},{2,0},{3,1},{4,2},{5,3},{6,4},{7,5},{8,14},{9,15},{10,... | collective-permute-start | bytes 1572872 | tf_op jit(solution)/shard_map/ppermute | solution.py:333
  27.3 14.7 %copy-start = (bf16[4096,256]{1,0:T(8,128)(2,1)S(1)}, bf16[4096,256]{1,0:T(8,128)(2,1)}, u32[]{:S(2)}) copy-start(bf16[4096,256]{1,0:T(8,128)(2,1)} %eig_ref.3) | copy-start | bytes 6291460
  40.9 6.4 %collective-permute-start.3 = (bf16[32,8192]{1,0:T(8,128)(2,1)S(1)}, bf16[32,8192]{1,0:T(8,128)(2,1)S(1)}, u32[]{:S(2)}, u32[]{:S(2)}) collective-permute-start(bf16[32,8192]{1,0:T(8,128)(2,1)S(1)} %bitcast.24), channel_id=1, source_target_pairs={{0,1},{1,0},{2,3},{3,2},{4,5},{5,4},{6,7},{7,6},{8,9},{9,8},{10,11... | collective-permute-start | bytes 1572872 | tf_op jit(solution)/shard_map/ppermute | solution.py:351
  40.9 6.4 %collective-permute-start.4 = (bf16[32,8192]{1,0:T(8,128)(2,1)}, bf16[32,8192]{1,0:T(8,128)(2,1)S(1)}, u32[]{:S(2)}, u32[]{:S(2)}) collective-permute-start(bf16[32,8192]{1,0:T(8,128)(2,1)} %collective-permute-done.rest_2_), channel_id=1, source_target_pairs={{0,1},{1,0},{2,3},{3,2},{4,5},{5,4},{6,7},{7,6},{8,9},{9,8},{10,11... | collective-permute-start | bytes 1572872 | tf_op jit(solution)/shard_map/ppermute | solution.py:351
  41.4 5.9 %collective-permute-start.5 = (bf16[32,8192]{1,0:T(8,128)(2,1)}, bf16[32,8192]{1,0:T(8,128)(2,1)S(1)}, u32[]{:S(2)}, u32[]{:S(2)}) collective-permute-start(bf16[32,8192]{1,0:T(8,128)(2,1)} %collective-permute-done.1.rest_4_), channel_id=1, source_target_pairs={{0,1},{1,0},{2,3},{3,2},{4,5},{5,4},{6,7},{7,6},{8,9},{9,8},{10,11... | collective-permute-start | bytes 1572872 | tf_op jit(solution)/shard_map/ppermute | solution.py:351
  41.4 5.9 %collective-permute-start.6 = (bf16[32,8192]{1,0:T(8,128)(2,1)}, bf16[32,8192]{1,0:T(8,128)(2,1)S(1)}, u32[]{:S(2)}, u32[]{:S(2)}) collective-permute-start(bf16[32,8192]{1,0:T(8,128)(2,1)} %collective-permute-done.2.rest_6_), channel_id=1, source_target_pairs={{0,1},{1,0},{2,3},{3,2},{4,5},{5,4},{6,7},{7,6},{8,9},{9,8},{10,11... | collective-permute-start | bytes 1572872 | tf_op jit(solution)/shard_map/ppermute | solution.py:351
  47.3 41.0 %copy-start.2 = (f32[1024,32]{0,1:T(8,128)S(1)}, f32[1024,32]{0,1:T(8,128)}, u32[]{:S(2)}) copy-start(f32[1024,32]{0,1:T(8,128)} %param.11) | copy-start | bytes 393220
  47.3 41.0 %copy-start.3 = (f32[256]{0:T(256)S(1)}, f32[256]{0:T(256)}, u32[]{:S(2)}) copy-start(f32[256]{0:T(256)} %param.13) | copy-start | bytes 3076
  86.0 2.3 %collective-permute-start.7 = (f32[64,24,128]{2,1,0:T(8,128)S(1)}, f32[64,24,128]{2,1,0:T(8,128)S(1)}, u32[]{:S(2)}, u32[]{:S(2)}) collective-permute-start(f32[64,24,128]{2,1,0:T(8,128)S(1)} %all_to_all.22.same_ref), channel_id=1, source_target_pairs={{0,1},{1,0},{2,3},{3,2},{4,5},{5,4},{6,7},{7,6},{8,9},{9,8},{10,11... | collective-permute-start | bytes 2359304 | tf_op jit(solution)/shard_map/ppermute | solution.py:361

commit v4 on v3

--- a/solution.py
+++ b/solution.py
@@ -14,12 +14,14 @@
 LANES = 128
 GROUP = 16
 SLOTS = 24
+PARTS = ((0, 2048), (2048, 2048))
 MIB = 2**20
 F32 = jnp.float32
 BF16 = jnp.bfloat16
 SMEM = pl.BlockSpec(memory_space=pltpu.SMEM)
 VMEM = pl.BlockSpec(memory_space=pltpu.VMEM)
 HBM = pl.BlockSpec(memory_space=pltpu.HBM)
+ANY = pl.BlockSpec(memory_space=pl.ANY)
 SWAP = [(i, i ^ 1) for i in range(2 * N_Z)]
 SAME_CORE = [[c * 8 + z * 2 + k for c in range(N_CTR) for z in range(N_Z)] for k in range(2)]
 
@@ -30,6 +32,10 @@
 
 def in_vmem(x):
     return pltpu.with_memory_space_constraint(x, pltpu.VMEM)
+
+
+def in_hbm(x):
+    return pltpu.with_memory_space_constraint(x, pltpu.HBM)
 
 
 def pick_kernel(first, *refs):
@@ -104,8 +110,8 @@
         name="pick",
     )(
         *([] if first else [at_round]),
-        pltpu.with_memory_space_constraint(batch_idx, pltpu.HBM),
-        pltpu.with_memory_space_constraint(table, pltpu.HBM),
+        in_hbm(batch_idx),
+        in_hbm(table),
     )
 
 
@@ -145,9 +151,10 @@
 
 
 def kern_kernel(
-    idx_ref, received_ref, more_ref, nys_ref, table_ref, kern, kern16, local_ref, held, pts_ref, cross, sems
+    idx_ref, received_in, more_in, nys_ref, table_ref, kern, kern16, local_ref,
+    held, received_ref, more_ref, pts_ref, cross, sems
 ):
-    n_tiles = sems.shape[0]
+    n_tiles = sems.shape[0] - 2
     c_rows = held.shape[0]
     tile = c_rows // n_tiles
 
@@ -158,9 +165,15 @@
         rows = rows_of(i)
         return pltpu.make_async_copy(table_ref.at[rows], held.at[rows], sems.at[i])
 
+    received_copy = pltpu.make_async_copy(received_in, received_ref, sems.at[n_tiles])
+    more_copy = pltpu.make_async_copy(more_in, more_ref, sems.at[n_tiles + 1])
+    received_copy.start()
+    more_copy.start()
     for i in range(n_tiles):
         copy_of(i).start()
     local_ref[...] = nys_ref[...] - lax.axis_index("ctr") * c_rows
+    received_copy.wait()
+    more_copy.wait()
     pts = settled(idx_ref[...], received_ref[...], 0.0, c_rows) + more_ref[...].astype(F32)
     pts_ref[...] = pts.astype(BF16)
     pts_sq = lax.dot_general(
@@ -197,7 +210,7 @@
     n = idx_row.shape[1]
     return pl.pallas_call(
         kern_kernel,
-        in_specs=[VMEM, VMEM, VMEM, VMEM, HBM],
+        in_specs=[VMEM, ANY, ANY, VMEM, HBM],
         out_specs=[VMEM, VMEM, VMEM],
         out_shape=[
             jax.ShapeDtypeStruct((c_rows, n), F32),
@@ -206,44 +219,68 @@
         ],
         scratch_shapes=[
             pltpu.VMEM((c_rows, D), BF16),
+            pltpu.VMEM(received.shape, BF16),
+            pltpu.VMEM((n, D), BF16),
             pltpu.VMEM((n, D), BF16),
             pltpu.VMEM((2, c_rows // N_TILES, n), F32),
-            pltpu.SemaphoreType.DMA((N_TILES,)),
+            pltpu.SemaphoreType.DMA((N_TILES + 2,)),
         ],
         compiler_params=pltpu.CompilerParams(vmem_limit_bytes=30 * MIB),
         cost_estimate=pl.CostEstimate(flops=10**10, bytes_accessed=24 * MIB, transcendentals=10**6),
         name="kernel_rows",
-    )(idx_row, received, more, nystrom_idx, pltpu.with_memory_space_constraint(table, pltpu.HBM))
-
-
-def comp_kernel(idx_ref, kern, eig_ref, out_ref, nys):
+    )(
+        idx_row, received, more, nystrom_idx, in_hbm(table)
+    )
+
+
+def comp_kernel(part, idx_ref, kern, eig_ref, *rest):
+    if part:
+        n_arrived = rest[-1].shape[0]
+        before_ref, *arrived = rest[:1 + n_arrived]
+        out_ref, *landed = rest[1 + n_arrived:-2]
+        nys, sems = rest[-2:]
+        copies = [pltpu.make_async_copy(x, y, sems.at[i]) for i, (x, y) in enumerate(zip(arrived, landed))]
+        for copy in copies:
+            copy.start()
+    else:
+        out_ref, nys = rest
     unroll = 32
+    first, n = PARTS[part]
 
     def gather(j, carry):
         for u in range(unroll):
             m = j * unroll + u
-            nys[pl.ds(m, 1), :] = kern[pl.ds(idx_ref[m], 1), :]
+            nys[pl.ds(m, 1), :] = kern[pl.ds(idx_ref[first + m], 1), :]
         return carry
 
-    lax.fori_loop(0, nys.shape[0] // unroll, gather, 0)
-    out_ref[...] = lax.dot_general(
-        eig_ref[...], nys[...].astype(BF16), (((0,), (0,)), ((), ())), preferred_element_type=F32
-    )
-
-
-def components(local_idx, kern, eigvecs):
-    m_rows, q = eigvecs.shape
+    lax.fori_loop(0, n // unroll, gather, 0)
+    comp = lax.dot_general(
+        eig_ref[first:first + n, :], nys[...].astype(BF16), (((0,), (0,)), ((), ())),
+        preferred_element_type=F32,
+    )
+    if part:
+        comp += before_ref[...]
+        for copy in copies:
+            copy.wait()
+    out_ref[...] = comp
+
+
+def components(part, local_idx, kern, eigvecs, *rest):
+    q = eigvecs.shape[1]
     n = kern.shape[1]
-    return pl.pallas_call(
-        comp_kernel,
-        in_specs=[SMEM, VMEM, VMEM],
-        out_specs=VMEM,
-        out_shape=jax.ShapeDtypeStruct((q, n), F32),
-        scratch_shapes=[pltpu.VMEM((m_rows, n), F32)],
+    arrived = rest[1:]
+    return pl.pallas_call(
+        functools.partial(comp_kernel, part),
+        in_specs=[SMEM, VMEM, VMEM] + ([VMEM] + [ANY] * len(arrived) if part else []),
+        out_specs=[VMEM] * (1 + len(arrived)),
+        out_shape=[jax.ShapeDtypeStruct((q, n), F32)]
+        + [jax.ShapeDtypeStruct(x.shape, x.dtype) for x in arrived],
+        scratch_shapes=[pltpu.VMEM((PARTS[part][1], n), F32)]
+        + ([pltpu.SemaphoreType.DMA((len(arrived),))] if part else []),
         compiler_params=pltpu.CompilerParams(vmem_limit_bytes=16 * MIB),
-        cost_estimate=pl.CostEstimate(flops=5 * 10**9, bytes_accessed=6 * MIB, transcendentals=0),
+        cost_estimate=pl.CostEstimate(flops=3 * 10**9, bytes_accessed=6 * MIB, transcendentals=0),
         name="components",
-    )(local_idx, kern, in_vmem(eigvecs))
+    )(local_idx, kern, in_vmem(eigvecs), *rest)
 
 
 def pred_kernel(comp_ref, kern16, *rest):
@@ -277,63 +314,83 @@
     )(comp, kern16, *[in_vmem(x) for x in pieces])
 
 
-def split3(x):
+def split2(x):
     hi = x.astype(BF16)
-    rest = x - hi.astype(F32)
-    mid = rest.astype(BF16)
-    lo = (rest - mid.astype(F32)).astype(BF16)
-    return hi, mid, lo
-
-
-def final_kernel(same_ref, other_ref, targets_ref, corr_ref, eig_ref, res_ref, upd_ref, comp):
+    return hi, (x - hi.astype(F32)).astype(BF16)
+
+
+def residual_of(ref, targets_ref, core, from_core, z):
+    lanes = pl.ds(pl.multiple_of((2 * z + from_core) * LANES, LANES), LANES)
+    pred = [ref[(core * 8 + i) * N_Z + z, 16:20, :] for i in range(8)]
+    return lanes, jnp.concatenate(pred, axis=0) - targets_ref[:, lanes]
+
+
+def projected(ref, z, residual):
+    comp = jnp.concatenate([ref[c * N_Z + z, 0:16, :] for c in range(N_CTR)], axis=0)
+    hi, lo = split2(comp)
+    grad = residual.astype(BF16)
+    dims = (((1,), (1,)), ((), ()))
+    return lax.dot_general(grad, hi, dims, preferred_element_type=F32) + lax.dot_general(
+        grad, lo, dims, preferred_element_type=F32
+    )
+
+
+def same_kernel(same_ref, targets_ref, proj_ref):
     core = lax.axis_index("bat") % 2
+    proj = jnp.zeros(proj_ref.shape, F32)
     for z in range(N_Z):
-        for s, ref in enumerate((same_ref, other_ref)):
-            from_core = core if s == 0 else 1 - core
-            lanes = pl.ds(pl.multiple_of((2 * z + from_core) * LANES, LANES), LANES)
-            for c in range(N_CTR):
-                comp[c * 16:(c + 1) * 16, lanes] = ref[c * N_Z + z, 0:16, :]
-            for i in range(8):
-                row = (core * 8 + i) * N_Z + z
-                res_ref[4 * i:4 * i + 4, lanes] = ref[row, 16:20, :]
-    residual = res_ref[...] - targets_ref[...]
-    res_ref[...] = residual
-    grad = residual.astype(BF16)
-    proj = jnp.zeros((32, comp.shape[0]), F32)
-    for part in split3(comp[...]):
-        proj += lax.dot_general(grad, part, (((1,), (1,)), ((), ())), preferred_element_type=F32)
-    scaled = jnp.concatenate(split3(proj * corr_ref[...]), axis=0)
+        _, residual = residual_of(same_ref, targets_ref, core, core, z)
+        proj += projected(same_ref, z, residual)
+    proj_ref[...] = proj
+
+
+def same_part(same, targets, q):
+    return pl.pallas_call(
+        same_kernel,
+        in_specs=[VMEM, VMEM],
+        out_specs=VMEM,
+        out_shape=jax.ShapeDtypeStruct((targets.shape[0], q), F32),
+        compiler_params=pltpu.CompilerParams(vmem_limit_bytes=16 * MIB),
+        name="same_part",
+    )(same, targets)
+
+
+def final_kernel(same_ref, other_ref, proj_ref, targets_ref, corr_ref, eig_ref, res_ref, upd_ref):
+    core = lax.axis_index("bat") % 2
+    proj = proj_ref[...]
+    for z in range(N_Z):
+        lanes, residual = residual_of(same_ref, targets_ref, core, core, z)
+        res_ref[:, lanes] = residual
+        lanes, residual = residual_of(other_ref, targets_ref, core, 1 - core, z)
+        res_ref[:, lanes] = residual
+        proj += projected(other_ref, z, residual)
+    scaled = jnp.concatenate(split2(proj * corr_ref[...]), axis=0)
     upd = lax.dot_general(
         scaled, eig_ref[...], (((1,), (1,)), ((), ())), preferred_element_type=F32
     )
-    upd_ref[...] = upd[0:32] + (upd[32:64] + upd[64:96])
-
-
-def final(same, other, targets, correction, eigvecs):
+    upd_ref[...] = upd[0:32] + upd[32:64]
+
+
+def final(same, other, proj, targets, correction, eigvecs):
     cols, n = targets.shape
     m_rows, q = eigvecs.shape
     return pl.pallas_call(
         final_kernel,
-        in_specs=[VMEM] * 5,
+        in_specs=[VMEM] * 6,
         out_specs=[VMEM, VMEM],
         out_shape=[
             jax.ShapeDtypeStruct((cols, n), F32),
             jax.ShapeDtypeStruct((cols, m_rows), F32),
         ],
-        scratch_shapes=[pltpu.VMEM((q, n), F32)],
         compiler_params=pltpu.CompilerParams(vmem_limit_bytes=16 * MIB),
         name="final",
-    )(same, other, targets, correction, in_vmem(eigvecs))
+    )(same, other, proj, targets, correction, in_vmem(eigvecs))
 
 
 def per_device(table, coefs, targets, eigvecs, correction, batch_idx, nystrom_idx):
     c_rows = table.shape[0]
     picked, rounds = pick(batch_idx, table)
-    picked, own = lax.optimization_barrier((picked, coefs.T))
-    from_z = [lax.ppermute(own, "bat", z_shift(k)) if k else own for k in range(N_Z)]
-
     idx_row = batch_idx.reshape(1, -1)
-    received = lax.all_to_all(picked, "ctr", 0, 0).reshape(-1, D)
 
     def further(state):
         at_round, more = state
@@ -343,14 +400,19 @@
 
     none = jnp.zeros((batch_idx.shape[0], D), BF16)
     _, more = lax.while_loop(lambda state: state[0] < rounds[0], further, (jnp.int32(1), none))
+    picked, more, own = lax.optimization_barrier((picked, more, coefs.T))
+    from_z = [lax.ppermute(own, "bat", z_shift(k)) if k else own for k in range(N_Z)]
+    received = lax.all_to_all(picked, "ctr", 0, 0).reshape(-1, D)
 
     kern, kern16, local_idx = kernel_rows(
         idx_row, received, more, nystrom_idx.reshape(-1, LANES), table
     )
-    kern, *from_z = lax.optimization_barrier((kern, *from_z))
-    pieces = [x for here in from_z for x in (here, lax.ppermute(here, "bat", SWAP))]
-    comp = components(local_idx.reshape(-1), kern, eigvecs)
-    comp, *pieces = lax.optimization_barrier((comp, *pieces))
+    local_idx = local_idx.reshape(-1)
+    comp, = components(0, local_idx, kern, eigvecs)
+    comp, late, *arrived = lax.optimization_barrier((comp, *from_z))
+    own_swapped, *swapped = [lax.ppermute(x, "bat", SWAP) for x in (late, *arrived)]
+    comp, *arrived = components(1, local_idx, kern, eigvecs, comp, *arrived)
+    pieces = [x for pair in zip((own, *arrived), (own_swapped, *swapped)) for x in pair]
     partial = predict(comp, kern16, pieces)
     mine = jnp.sum(lax.all_to_all(partial, "ctr", 0, 0), axis=0)
     comp = jnp.broadcast_to(mine[None, :16], (N_Z, 16, LANES))
@@ -359,7 +421,8 @@
     sent = jnp.broadcast_to(sent[None], (N_CTR,) + sent.shape).reshape((-1,) + sent.shape[1:])
     same = lax.all_to_all(sent, ("ctr", "bat"), 0, 0, axis_index_groups=SAME_CORE)
     other = lax.ppermute(same, "bat", SWAP)
-    residual, update = final(same, other, targets.T, correction[None], eigvecs)
+    proj = same_part(same, targets.T, eigvecs.shape[1])
+    residual, update = final(same, other, proj, targets.T, correction[None], eigvecs)
     return residual.T, update.T
 
 

time: 92.8 us -> 88.9 us (0.958)
  Pallas kernels: 26 us -> 24.7 us
  starting transfers between devices: 14.8 us -> 13.7 us
    pallas_call x1, Pallas kernels: 2.67 us -> 1.27 us  [predict(): pl.pallas_call(pred_kernel, in_specs=[VMEM] * 10, out_specs=VMEM, out_sha...]
    ppermute x3, waiting for transfers between devices: 2.61 us -> 1.3 us  [per_device(): lax.ppermute(own, 'bat', z_shift(k))]
    ppermute x3, starting transfers between devices: 6.58 us -> 5.48 us  [per_device(): lax.ppermute(own, 'bat', z_shift(k))]
    all_to_all x1, blocking collectives: 20.3 us -> 19.2 us  [per_device(): lax.all_to_all(sent, ('ctr', 'bat'), 0, 0, axis_index_groups=SAME_CORE)]
    all_to_all x1, waiting for transfers between devices: 8.02 us -> 9.01 us  [per_device(): received = lax.all_to_all(picked, 'ctr', 0, 0).reshape(-1, D)]
    pallas_call x3 -> x5, Pallas kernels: 19.3 us -> 19.4 us  [the longest x1 10.8 us: kernel_rows(): pl.pallas_call(kern_kernel, in_specs=[VMEM, ANY, ANY, VMEM, HBM], out_spe...]
  transfers between devices with their start and end apart: 9 -> 9, of which waited for: 3 -> 4; matrix products, arithmetic and copies ran while one was open for 0% -> 0% of each run, Pallas kernels for 18% -> 20%
where the time goes in v4:
time: 88.9 us; the launch traced here: 87.4 us
  blocking collectives  35 us (39%)
  Pallas kernels  24.7 us (28%)
  starting transfers between devices  13.7 us (15%)
  waiting for transfers between devices  12.4 us (14%)
    all_to_all x1, blocking collectives, per_device(): lax.all_to_all(sent, ('ctr', 'bat'), 0, 0, axis_index_groups=SAME_CORE)  19.2 us
    all_to_all x1, blocking collectives, per_device(): mine = jnp.sum(lax.all_to_all(partial, 'ctr', 0, 0), axis=0)  15.7 us
    pallas_call x1, Pallas kernels, kernel_rows(): pl.pallas_call(kern_kernel, in_specs=[VMEM, ANY, ANY, VMEM, HBM], out_spe...  10.8 us
    all_to_all x1, waiting for transfers between devices, per_device(): received = lax.all_to_all(picked, 'ctr', 0, 0).reshape(-1, D)  9.01 us
    all_to_all x1, starting transfers between devices, per_device(): received = lax.all_to_all(picked, 'ctr', 0, 0).reshape(-1, D)  7.19 us
    pallas_call x2, Pallas kernels, components(): pl.pallas_call(functools.partial(comp_kernel, part), in_specs=[SMEM, VMEM...  6.38 us
    ppermute x3, starting transfers between devices, per_device(): lax.ppermute(own, 'bat', z_shift(k))  5.48 us
    pallas_call x1, Pallas kernels, pick(): pl.pallas_call(functools.partial(pick_kernel, first), in_specs=([] if fir...  3.99 us
  transfers between devices with their start and end apart: 9, of which 4 were waited for; matrix products, arithmetic and copies ran while one was open for 0% of the time, Pallas kernels for 20%

profile of v4, /device:TPU:0, one launch (start us, length us, event | category | flops | bytes accessed | tf_op | source)
XLA Modules:
  0.0 87.4 jit_solution(11159373716247176415)
XLA Ops:
  0.6 0.0 copy-start.6
  0.6 4.0 %pick.2 = (bf16[16,24,1024]{2,1,0:T(8,128)(2,1)}, s32[1]{0:T(128)}) custom-call(s32[128]{0:T(128)} %refs_0_.1, bf16[8192,1024]{1,0:T(8,128)(2,1)} %table_ref.1), custom_call_target="tpu_custom_call" | custom-call | tf_op jit(solution)/shard_map/pick/pallas_call | solution.py:93
  4.7 0.0 copy-start.4
  4.7 0.7 while.10
  5.4 0.0 copy-start.5
  5.4 7.2 %all-to-all-start.1 = ((bf16[16,24,1024]{2,1,0:T(8,128)(2,1)}), bf16[16,24,1024]{2,1,0:T(8,128)(2,1)S(1)}, u32[]{:S(2)}, u32[]{:S(2)}) async-start(bf16[16,24,1024]{2,1,0:T(8,128)(2,1)} %get-tuple-element.58), calls=%async_computation.1 | async-start | bytes 1572864 | tf_op jit(solution)/shard_map/all_to_all | solution.py:405
  12.6 4.1 %collective-permute-start.2 = (bf16[32,8192]{1,0:T(8,128)(2,1)S(1)}, bf16[32,8192]{1,0:T(8,128)(2,1)}, u32[]{:S(2)}, u32[]{:S(2)}) collective-permute-start(bf16[32,8192]{1,0:T(8,128)(2,1)S(1)} %bitcast.21), channel_id=1, source_target_pairs={{0,6},{1,7},{2,0},{3,1},{4,2},{5,3},{6,4},{7,5},{8,14},{9,15},{10,... | collective-permute-start | bytes 1572872 | tf_op jit(solution)/shard_map/ppermute | solution.py:404
  16.7 0.1 collective-permute-start.1
  16.8 1.3 %collective-permute-start = (bf16[32,8192]{1,0:T(8,128)(2,1)S(1)}, bf16[32,8192]{1,0:T(8,128)(2,1)}, u32[]{:S(2)}, u32[]{:S(2)}) collective-permute-start(bf16[32,8192]{1,0:T(8,128)(2,1)S(1)} %bitcast.23), channel_id=1, source_target_pairs={{0,2},{1,3},{2,4},{3,5},{4,6},{5,7},{6,0},{7,1},{8,10},{9,11},{10,... | collective-permute-start | bytes 1572872 | tf_op jit(solution)/shard_map/ppermute | solution.py:404
  18.1 9.0 %all-to-all-done.1 = bf16[16,24,1024]{2,1,0:T(8,128)(2,1)S(1)} async-done(((bf16[16,24,1024]{2,1,0:T(8,128)(2,1)}), bf16[16,24,1024]{2,1,0:T(8,128)(2,1)S(1)}, u32[]{:S(2)}, u32[]{:S(2)}) %all-to-all-start.1) | async-done | bytes 786464 | tf_op jit(solution)/shard_map/all_to_all | solution.py:405
  27.1 10.8 %kernel_rows.1 = (f32[8192,128]{1,0:T(8,128)S(1)}, bf16[8192,128]{1,0:T(8,128)(2,1)S(1)}, s32[32,128]{1,0:T(8,128)S(1)}) custom-call(s32[1,128]{1,0:T(1,128)S(1)} %get-tuple-element.168, bf16[384,1024]{1,0:T(8,128)(2,1)S(1)} %bitcast.20, bf16[128,1024]{1,0:T(8,128)(2,1)} %copy-done.5, s32[32,128]{1,0:T(8,128)S(1)} %bitcast.29, ...), custom_call_target="tpu_custom_call" | custom-call | flops 10000000000 | bytes 25165824 | tf_op jit(solution)/shard_map/kernel_rows/pallas_call | solution.py:211
  37.9 3.2 %components.2.rest_0_ = f32[256,128]{1,0:T(8,128)S(1)} custom-call(s32[4096]{0:T(1024)S(1)} %bitcast.30, f32[8192,128]{1,0:T(8,128)S(1)} %get-tuple-element.61.kern, bf16[4096,256]{1,0:T(8,128)(2,1)S(1)} %copy-done), custom_call_target="tpu_custom_call" | custom-call | flops 3000000000 | bytes 6291456 | tf_op jit(solution)/shard_map/components/pallas_call | solution.py:272
  41.1 1.3 %collective-permute-done.rest_1_ = bf16[32,8192]{1,0:T(8,128)(2,1)} collective-permute-done((bf16[32,8192]{1,0:T(8,128)(2,1)S(1)}, bf16[32,8192]{1,0:T(8,128)(2,1)}, u32[]{:S(2)}, u32[]{:S(2)}) %collective-permute-start) | collective-permute-done | bytes 524320 | tf_op jit(solution)/shard_map/ppermute | solution.py:404
  42.4 0.5 collective-permute-start.4
  42.9 0.5 collective-permute-start.6
  43.4 3.2 %components.3 = (f32[256,128]{1,0:T(8,128)S(1)}, bf16[32,8192]{1,0:T(8,128)(2,1)S(1)}, bf16[32,8192]{1,0:T(8,128)(2,1)S(1)}, bf16[32,8192]{1,0:T(8,128)(2,1)S(1)}) custom-call(s32[4096]{0:T(1024)S(1)} %bitcast.31, f32[8192,128]{1,0:T(8,128)S(1)} %get-tuple-element.61.kern, bf16[4096,256]{1,0:T(8,128)(2,1)S(1)} %copy-done, f32[256,128]{1,0:T(8,128)S(1)} %components.2.rest_0_, ...), custom_call_target="tpu_custom_call" | custom-call | flops 3000000000 | bytes 6291456 | tf_op jit(solution)/shard_map/components/pallas_call | solution.py:272
  46.7 0.1 collective-permute-done.6.rest_7_
  46.8 1.3 %predict.1 = f32[16,32,128]{2,1,0:T(8,128)S(1)} custom-call(f32[256,128]{1,0:T(8,128)S(1)} %get-tuple-element.67.comp_ref, bf16[8192,128]{1,0:T(8,128)(2,1)S(1)} %get-tuple-element.68.kern16, bf16[32,8192]{1,0:T(8,128)(2,1)S(1)} %bitcast.25, bf16[32,8192]{1,0:T(8,128)(2,1)S(1)} %collective-permute-done.3.rest_1_, ...), custom_call_target="tpu_custom_call" | custom-call | tf_op jit(solution)/shard_map/predict/pallas_call | solution.py:306
  48.0 15.7 %all_to_all.21 = f32[16,32,128]{2,1,0:T(8,128)S(1)} all-to-all(f32[16,32,128]{2,1,0:T(8,128)S(1)} %predict.1), channel_id=1, replica_groups=mesh['ctr'=16,'bat'=8] {'ctr'}, dimensions={0} | all-to-all | bytes 524288 | tf_op jit(solution)/shard_map/all_to_all | solution.py:417
  63.8 0.1 broadcast_in_dim.20
  63.9 19.2 %all_to_all.22.same_ref = f32[64,24,128]{2,1,0:T(8,128)S(1)} all-to-all(f32[64,24,128]{2,1,0:T(8,128)S(1)} %bitcast.32), channel_id=1, replica_groups={{0,2,4,6,8,10,12,14,16,18,20,22,24,26,28,30,32,34,36,38,40,42,44,46,48,..., dimensions={0} | all-to-all | bytes 1572864 | tf_op jit(solution)/shard_map/all_to_all | solution.py:422
  83.2 0.3 same_part.1.proj_ref
  83.4 2.0 %collective-permute-done.7.other_ref = f32[64,24,128]{2,1,0:T(8,128)S(1)} collective-permute-done((f32[64,24,128]{2,1,0:T(8,128)S(1)}, f32[64,24,128]{2,1,0:T(8,128)S(1)}, u32[]{:S(2)}, u32[]{:S(2)}) %collective-permute-start.7) | collective-permute-done | bytes 786464 | tf_op jit(solution)/shard_map/ppermute | solution.py:423
  85.4 2.0 %final.1 = (f32[32,1024]{1,0:T(8,128)}, f32[32,4096]{1,0:T(8,128)}) custom-call(f32[64,24,128]{2,1,0:T(8,128)S(1)} %all_to_all.22.same_ref, f32[64,24,128]{2,1,0:T(8,128)S(1)} %collective-permute-done.7.other_ref, f32[32,256]{1,0:T(8,128)S(1)} %same_part.1.proj_ref, f32[32,1024]{1,0:T(8,128)S(1)} %bitcast.27, f32[1,256]{1,0:T(1,128)S(1)} %bitcast.28, ...), custom_call_target="tpu_custom_call" | custom-call | tf_op jit(solution)/shard_map/final/pallas_call | solution.py:377
  (24 shorter events, 0.1 us)
Async XLA Ops:
  0.6 4.0 %copy-start.6 = (s32[128]{0:T(128)S(1)}, s32[128]{0:T(128)}, u32[]{:S(2)}) copy-start(s32[128]{0:T(128)} %refs_0_.1) | copy-start | bytes 1540
  4.7 8.0 %copy-start.1 = (bf16[8192,32]{0,1:T(8,128)(2,1)S(1)}, bf16[8192,32]{0,1:T(8,128)(2,1)}, u32[]{:S(2)}) copy-start(bf16[8192,32]{0,1:T(8,128)(2,1)} %param.10) | copy-start | bytes 1572868
  4.7 22.4 %copy-start.4 = (s32[4096]{0:T(1024)S(1)}, s32[4096]{0:T(1024)}, u32[]{:S(2)}) copy-start(s32[4096]{0:T(1024)} %param.15) | copy-start | bytes 49156
  5.4 21.7 %copy-start.5 = (bf16[128,1024]{1,0:T(8,128)(2,1)}, bf16[128,1024]{1,0:T(8,128)(2,1)S(1)}, u32[]{:S(2)}) copy-start(bf16[128,1024]{1,0:T(8,128)(2,1)S(1)} %get-tuple-element.164) | copy-start | bytes 786436
  5.4 21.7 %all-to-all-start.1 = ((bf16[16,24,1024]{2,1,0:T(8,128)(2,1)}), bf16[16,24,1024]{2,1,0:T(8,128)(2,1)S(1)}, u32[]{:S(2)}, u32[]{:S(2)}) async-start(bf16[16,24,1024]{2,1,0:T(8,128)(2,1)} %get-tuple-element.58), calls=%async_computation.1 | async-start | bytes 1572864 | tf_op jit(solution)/shard_map/all_to_all | solution.py:405
  12.6 28.4 %collective-permute-start.2 = (bf16[32,8192]{1,0:T(8,128)(2,1)S(1)}, bf16[32,8192]{1,0:T(8,128)(2,1)}, u32[]{:S(2)}, u32[]{:S(2)}) collective-permute-start(bf16[32,8192]{1,0:T(8,128)(2,1)S(1)} %bitcast.21), channel_id=1, source_target_pairs={{0,6},{1,7},{2,0},{3,1},{4,2},{5,3},{6,4},{7,5},{8,14},{9,15},{10,... | collective-permute-start | bytes 1572872 | tf_op jit(solution)/shard_map/ppermute | solution.py:404
  16.7 24.4 %collective-permute-start.1 = (bf16[32,8192]{1,0:T(8,128)(2,1)S(1)}, bf16[32,8192]{1,0:T(8,128)(2,1)}, u32[]{:S(2)}, u32[]{:S(2)}) collective-permute-start(bf16[32,8192]{1,0:T(8,128)(2,1)S(1)} %bitcast.22), channel_id=1, source_target_pairs={{0,4},{1,5},{2,6},{3,7},{4,0},{5,1},{6,2},{7,3},{8,12},{9,13},{10,... | collective-permute-start | bytes 1572872 | tf_op jit(solution)/shard_map/ppermute | solution.py:404
  16.8 25.6 %collective-permute-start = (bf16[32,8192]{1,0:T(8,128)(2,1)S(1)}, bf16[32,8192]{1,0:T(8,128)(2,1)}, u32[]{:S(2)}, u32[]{:S(2)}) collective-permute-start(bf16[32,8192]{1,0:T(8,128)(2,1)S(1)} %bitcast.23), channel_id=1, source_target_pairs={{0,2},{1,3},{2,4},{3,5},{4,6},{5,7},{6,0},{7,1},{8,10},{9,11},{10,... | collective-permute-start | bytes 1572872 | tf_op jit(solution)/shard_map/ppermute | solution.py:404
  27.1 10.8 %copy-start = (bf16[4096,256]{1,0:T(8,128)(2,1)S(1)}, bf16[4096,256]{1,0:T(8,128)(2,1)}, u32[]{:S(2)}) copy-start(bf16[4096,256]{1,0:T(8,128)(2,1)} %eig_ref.5) | copy-start | bytes 6291460
  42.4 4.2 %collective-permute-start.3 = (bf16[32,8192]{1,0:T(8,128)(2,1)S(1)}, bf16[32,8192]{1,0:T(8,128)(2,1)S(1)}, u32[]{:S(2)}, u32[]{:S(2)}) collective-permute-start(bf16[32,8192]{1,0:T(8,128)(2,1)S(1)} %bitcast.24), channel_id=1, source_target_pairs={{0,1},{1,0},{2,3},{3,2},{4,5},{5,4},{6,7},{7,6},{8,9},{9,8},{10,11... | collective-permute-start | bytes 1572872 | tf_op jit(solution)/shard_map/ppermute | solution.py:413
  42.4 4.3 %collective-permute-start.4 = (bf16[32,8192]{1,0:T(8,128)(2,1)}, bf16[32,8192]{1,0:T(8,128)(2,1)S(1)}, u32[]{:S(2)}, u32[]{:S(2)}) collective-permute-start(bf16[32,8192]{1,0:T(8,128)(2,1)} %collective-permute-done.rest_1_), channel_id=1, source_target_pairs={{0,1},{1,0},{2,3},{3,2},{4,5},{5,4},{6,7},{7,6},{8,9},{9,8},{10,11... | collective-permute-start | bytes 1572872 | tf_op jit(solution)/shard_map/ppermute | solution.py:413
  42.9 3.8 %collective-permute-start.5 = (bf16[32,8192]{1,0:T(8,128)(2,1)}, bf16[32,8192]{1,0:T(8,128)(2,1)S(1)}, u32[]{:S(2)}, u32[]{:S(2)}) collective-permute-start(bf16[32,8192]{1,0:T(8,128)(2,1)} %collective-permute-done.1.rest_2_), channel_id=1, source_target_pairs={{0,1},{1,0},{2,3},{3,2},{4,5},{5,4},{6,7},{7,6},{8,9},{9,8},{10,11... | collective-permute-start | bytes 1572872 | tf_op jit(solution)/shard_map/ppermute | solution.py:413
  42.9 3.9 %collective-permute-start.6 = (bf16[32,8192]{1,0:T(8,128)(2,1)}, bf16[32,8192]{1,0:T(8,128)(2,1)S(1)}, u32[]{:S(2)}, u32[]{:S(2)}) collective-permute-start(bf16[32,8192]{1,0:T(8,128)(2,1)} %collective-permute-done.2.rest_3_), channel_id=1, source_target_pairs={{0,1},{1,0},{2,3},{3,2},{4,5},{5,4},{6,7},{7,6},{8,9},{9,8},{10,11... | collective-permute-start | bytes 1572872 | tf_op jit(solution)/shard_map/ppermute | solution.py:413
  46.8 36.4 %copy-start.2 = (f32[1024,32]{0,1:T(8,128)S(1)}, f32[1024,32]{0,1:T(8,128)}, u32[]{:S(2)}) copy-start(f32[1024,32]{0,1:T(8,128)} %param.11) | copy-start | bytes 393220
  46.8 38.7 %copy-start.3 = (f32[256]{0:T(256)S(1)}, f32[256]{0:T(256)}, u32[]{:S(2)}) copy-start(f32[256]{0:T(256)} %param.13) | copy-start | bytes 3076
  83.1 2.3 %collective-permute-start.7 = (f32[64,24,128]{2,1,0:T(8,128)S(1)}, f32[64,24,128]{2,1,0:T(8,128)S(1)}, u32[]{:S(2)}, u32[]{:S(2)}) collective-permute-start(f32[64,24,128]{2,1,0:T(8,128)S(1)} %all_to_all.22.same_ref), channel_id=1, source_target_pairs={{0,1},{1,0},{2,3},{3,2},{4,5},{5,4},{6,7},{7,6},{8,9},{9,8},{10,11... | collective-permute-start | bytes 2359304 | tf_op jit(solution)/shard_map/ppermute | solution.py:423

commit v5 on v4

--- a/solution.py
+++ b/solution.py
@@ -39,33 +39,25 @@
 
 
 def pick_kernel(first, *refs):
-    round_ref = None if first else refs[0]
-    idx_hbm, table_ref, out_ref, rounds_ref, idx_ref, counts, listed, groups, rows, sems = refs[0 if first else 1:]
-    n = listed.shape[0] - 1
+    done = 0 if first else refs[0][0] * SLOTS
+    idx_hbm, table_ref, out_ref, idx_ref, listed, groups, rows, sems = refs[0 if first else 1:]
+    n = idx_ref.shape[0]
     c_rows = table_ref.shape[0]
-    ctr = lax.axis_index("ctr")
+    first_row = lax.axis_index("ctr") * c_rows
     idx_copy = pltpu.make_async_copy(idx_hbm, idx_ref, sems.at[SLOTS])
     idx_copy.start()
     rows[...] = jnp.zeros_like(rows)
-    for c in range(N_CTR):
-        counts[c] = 0
     idx_copy.wait()
 
-    def note(i, most):
-        owner = idx_ref[i] // c_rows
-        count = counts[owner]
-        listed[jnp.where(owner == ctr, count, n)] = i
-        counts[owner] = count + 1
-        return jnp.maximum(most, count + 1)
-
-    most = lax.fori_loop(0, n, note, 0, unroll=8)
-    rounds_ref[0] = (most + SLOTS - 1) // SLOTS
-    done = 0 if first else round_ref[0] * SLOTS
-    count = jnp.clip(counts[ctr] - done, 0, SLOTS)
+    def note(i, count):
+        pos = idx_ref[i] - first_row
+        listed[count] = pos
+        return count + jnp.where((pos >= 0) & (pos < c_rows), 1, 0)
+
+    count = jnp.clip(lax.fori_loop(0, n, note, 0, unroll=16) - done, 0, SLOTS)
 
     def copy_of(s):
-        pos = idx_ref[listed[done + s]] - ctr * c_rows
-        start = pl.multiple_of(pos // GROUP * GROUP, GROUP)
+        start = pl.multiple_of(listed[done + s] // GROUP * GROUP, GROUP)
         return pltpu.make_async_copy(table_ref.at[pl.ds(start, GROUP)], groups.at[s], sems.at[s])
 
     def start(s, carry):
@@ -76,7 +68,7 @@
         copy_of(s).wait()
         group = groups[s].astype(F32)
         place = lax.broadcasted_iota(jnp.int32, group.shape, 0)
-        kept = jnp.where(place == idx_ref[listed[done + s]] % GROUP, group, 0.0)
+        kept = jnp.where(place == listed[done + s] % GROUP, group, 0.0)
         rows[pl.ds(s, 1), :] = jnp.sum(kept, axis=0, keepdims=True)
         return carry
 
@@ -93,14 +85,10 @@
     return pl.pallas_call(
         functools.partial(pick_kernel, first),
         in_specs=([] if first else [SMEM]) + [HBM, HBM],
-        out_specs=[VMEM, SMEM],
-        out_shape=[
-            jax.ShapeDtypeStruct((N_CTR, SLOTS, D), BF16),
-            jax.ShapeDtypeStruct((1,), jnp.int32),
-        ],
+        out_specs=VMEM,
+        out_shape=jax.ShapeDtypeStruct((N_CTR, SLOTS, D), BF16),
         scratch_shapes=[
             pltpu.SMEM((n,), jnp.int32),
-            pltpu.SMEM((N_CTR,), jnp.int32),
             pltpu.SMEM((n + 1,), jnp.int32),
             pltpu.VMEM((SLOTS, GROUP, D), BF16),
             pltpu.VMEM((SLOTS, D), F32),
@@ -108,20 +96,39 @@
         ],
         compiler_params=pltpu.CompilerParams(vmem_limit_bytes=8 * MIB),
         name="pick",
-    )(
-        *([] if first else [at_round]),
-        in_hbm(batch_idx),
-        in_hbm(table),
-    )
+    )(*([] if first else [at_round]), in_hbm(batch_idx), in_hbm(table))
+
+
+def owners(idx_row, c_rows):
+    n = idx_row.shape[1]
+    row = (idx_row // c_rows).astype(F32)
+    i = lax.broadcasted_iota(jnp.int32, (n, n), 0)
+    j = lax.broadcasted_iota(jnp.int32, (n, n), 1)
+    column = jnp.sum(jnp.where(i == j, row, 0.0), axis=1, keepdims=True)
+    return column, column == row, j < i
+
+
+def count_kernel(c_rows, idx_ref, rounds_ref):
+    _, alike, _ = owners(idx_ref[...], c_rows)
+    most = jnp.max(jnp.sum(jnp.where(alike, 1.0, 0.0), axis=1, keepdims=True))
+    rounds_ref[0] = (most.astype(jnp.int32) + SLOTS - 1) // SLOTS
+
+
+def count_rounds(idx_row, c_rows):
+    return pl.pallas_call(
+        functools.partial(count_kernel, c_rows),
+        in_specs=[VMEM],
+        out_specs=SMEM,
+        out_shape=jax.ShapeDtypeStruct((1,), jnp.int32),
+        cost_estimate=pl.CostEstimate(flops=10**9, bytes_accessed=MIB, transcendentals=0),
+        name="count_rounds",
+    )(idx_row)
 
 
 def settled(idx_row, received, at_round, c_rows):
     n = idx_row.shape[1]
-    owner_row = (idx_row // c_rows).astype(F32)
-    i = lax.broadcasted_iota(jnp.int32, (n, n), 0)
-    j = lax.broadcasted_iota(jnp.int32, (n, n), 1)
-    owner = jnp.sum(jnp.where(i == j, owner_row, 0.0), axis=1, keepdims=True)
-    before = (owner == owner_row) & (j < i)
+    owner, alike, earlier = owners(idx_row, c_rows)
+    before = alike & earlier
     slot = jnp.sum(jnp.where(before, 1.0, 0.0), axis=1, keepdims=True) - at_round * SLOTS
     here = (slot >= 0.0) & (slot < SLOTS)
     place = jnp.where(here, owner * SLOTS + slot, -1.0)
@@ -176,10 +183,10 @@
     more_copy.wait()
     pts = settled(idx_ref[...], received_ref[...], 0.0, c_rows) + more_ref[...].astype(F32)
     pts_ref[...] = pts.astype(BF16)
-    pts_sq = lax.dot_general(
-        jnp.ones((8, D), F32), pts * pts, (((1,), (1,)), ((), ())),
-        precision=lax.Precision.HIGHEST, preferred_element_type=F32,
-    )[0:1]
+    n = pts.shape[0]
+    on_diagonal = lax.broadcasted_iota(jnp.int32, (n, n), 0) == lax.broadcasted_iota(jnp.int32, (n, n), 1)
+    sums = jnp.sum(pts * pts, axis=1, keepdims=True)
+    pts_sq = jnp.sum(jnp.where(on_diagonal, sums, 0.0), axis=0, keepdims=True)
 
     def multiply(i):
         copy_of(i).wait()
@@ -244,7 +251,7 @@
             copy.start()
     else:
         out_ref, nys = rest
-    unroll = 32
+    unroll = 64
     first, n = PARTS[part]
 
     def gather(j, carry):
@@ -389,21 +396,22 @@
 
 def per_device(table, coefs, targets, eigvecs, correction, batch_idx, nystrom_idx):
     c_rows = table.shape[0]
-    picked, rounds = pick(batch_idx, table)
     idx_row = batch_idx.reshape(1, -1)
+    picked = pick(batch_idx, table)
+    picked, idx_row, own = lax.optimization_barrier((picked, idx_row, coefs.T))
+    from_z = [lax.ppermute(own, "bat", z_shift(k)) if k else own for k in range(N_Z)]
+    received = lax.all_to_all(picked, "ctr", 0, 0).reshape(-1, D)
+    rounds = count_rounds(idx_row, c_rows)
+    received, rounds = lax.optimization_barrier((received, rounds))
 
     def further(state):
         at_round, more = state
-        sent, _ = pick(batch_idx, table, at_round.reshape(1))
+        sent = pick(batch_idx, table, at_round.reshape(1))
         got = lax.all_to_all(sent, "ctr", 0, 0).reshape(-1, D)
         return at_round + 1, settle(at_round.reshape(1), idx_row, got, more, c_rows)
 
     none = jnp.zeros((batch_idx.shape[0], D), BF16)
     _, more = lax.while_loop(lambda state: state[0] < rounds[0], further, (jnp.int32(1), none))
-    picked, more, own = lax.optimization_barrier((picked, more, coefs.T))
-    from_z = [lax.ppermute(own, "bat", z_shift(k)) if k else own for k in range(N_Z)]
-    received = lax.all_to_all(picked, "ctr", 0, 0).reshape(-1, D)
-
     kern, kern16, local_idx = kernel_rows(
         idx_row, received, more, nystrom_idx.reshape(-1, LANES), table
     )

time: 88.9 us -> 87.5 us (0.984)
  Pallas kernels: 24.7 us -> 23.6 us
    pallas_call x1, Pallas kernels: 10.8 us -> 9.78 us  [kernel_rows(): pl.pallas_call(kern_kernel, in_specs=[VMEM, ANY, ANY, VMEM, HBM], out_spe...]
where the time goes in v5:
time: 87.5 us; the launch traced here: 86.1 us
  blocking collectives  35 us (40%)
  Pallas kernels  23.6 us (27%)
  starting transfers between devices  13.5 us (15%)
  waiting for transfers between devices  11.6 us (13%)
    all_to_all x1, blocking collectives, per_device(): lax.all_to_all(sent, ('ctr', 'bat'), 0, 0, axis_index_groups=SAME_CORE)  19.2 us
    all_to_all x1, blocking collectives, per_device(): mine = jnp.sum(lax.all_to_all(partial, 'ctr', 0, 0), axis=0)  15.7 us
    pallas_call x1, Pallas kernels, kernel_rows(): pl.pallas_call(kern_kernel, in_specs=[VMEM, ANY, ANY, VMEM, HBM], out_spe...  9.78 us
    all_to_all x1, waiting for transfers between devices, per_device(): received = lax.all_to_all(picked, 'ctr', 0, 0).reshape(-1, D)  8.28 us
    all_to_all x1, starting transfers between devices, per_device(): received = lax.all_to_all(picked, 'ctr', 0, 0).reshape(-1, D)  7.21 us
    pallas_call x2, Pallas kernels, components(): pl.pallas_call(functools.partial(comp_kernel, part), in_specs=[SMEM, VMEM...  6.11 us
    ppermute x3, starting transfers between devices, per_device(): lax.ppermute(own, 'bat', z_shift(k))  5.31 us
    pallas_call x1, Pallas kernels, pick(): pl.pallas_call(functools.partial(pick_kernel, first), in_specs=([] if fir...  3.38 us
  transfers between devices with their start and end apart: 9, of which 4 were waited for; matrix products, arithmetic and copies ran while one was open for 0% of the time, Pallas kernels for 20%

profile of v5, /device:TPU:0, one launch (start us, length us, event | category | flops | bytes accessed | tf_op | source)
XLA Modules:
  0.0 86.1 jit_solution(2677564092138458472)
XLA Ops:
  0.6 0.0 copy-start.6
  0.7 3.4 %pick.2 = bf16[16,24,1024]{2,1,0:T(8,128)(2,1)} custom-call(s32[128]{0:T(128)} %refs_0_.1, bf16[8192,1024]{1,0:T(8,128)(2,1)} %table_ref.1), custom_call_target="tpu_custom_call" | custom-call | tf_op jit(solution)/shard_map/pick/pallas_call | solution.py:85
  4.0 7.2 %all-to-all-start.1 = ((bf16[16,24,1024]{2,1,0:T(8,128)(2,1)}), bf16[16,24,1024]{2,1,0:T(8,128)(2,1)S(1)}, u32[]{:S(2)}, u32[]{:S(2)}) async-start(bf16[16,24,1024]{2,1,0:T(8,128)(2,1)} %pick.2), calls=%async_computation.1 | async-start | bytes 1572864 | tf_op jit(solution)/shard_map/all_to_all | solution.py:403
  11.3 4.2 %collective-permute-start.2 = (bf16[32,8192]{1,0:T(8,128)(2,1)S(1)}, bf16[32,8192]{1,0:T(8,128)(2,1)}, u32[]{:S(2)}, u32[]{:S(2)}) collective-permute-start(bf16[32,8192]{1,0:T(8,128)(2,1)S(1)} %bitcast.21), channel_id=1, source_target_pairs={{0,6},{1,7},{2,0},{3,1},{4,2},{5,3},{6,4},{7,5},{8,14},{9,15},{10,... | collective-permute-start | bytes 1572872 | tf_op jit(solution)/shard_map/ppermute | solution.py:402
  15.4 1.2 %collective-permute-start = (bf16[32,8192]{1,0:T(8,128)(2,1)S(1)}, bf16[32,8192]{1,0:T(8,128)(2,1)}, u32[]{:S(2)}, u32[]{:S(2)}) collective-permute-start(bf16[32,8192]{1,0:T(8,128)(2,1)S(1)} %bitcast.23), channel_id=1, source_target_pairs={{0,2},{1,3},{2,4},{3,5},{4,6},{5,7},{6,0},{7,1},{8,10},{9,11},{10,... | collective-permute-start | bytes 1572872 | tf_op jit(solution)/shard_map/ppermute | solution.py:402
  16.6 0.7 count_rounds.1
  17.3 8.3 %all-to-all-done.1 = bf16[16,24,1024]{2,1,0:T(8,128)(2,1)S(1)} async-done(((bf16[16,24,1024]{2,1,0:T(8,128)(2,1)}), bf16[16,24,1024]{2,1,0:T(8,128)(2,1)S(1)}, u32[]{:S(2)}, u32[]{:S(2)}) %all-to-all-start.1) | async-done | bytes 786464 | tf_op jit(solution)/shard_map/all_to_all | solution.py:403
  25.6 0.0 copy-start.4
  25.7 0.7 while.10
  26.3 0.7 copy-done.5
  27.0 9.8 %kernel_rows.1 = (f32[8192,128]{1,0:T(8,128)S(1)}, bf16[8192,128]{1,0:T(8,128)(2,1)S(1)}, s32[32,128]{1,0:T(8,128)S(1)}) custom-call(s32[1,128]{1,0:T(1,128)S(1)} %get-tuple-element.165, bf16[384,1024]{1,0:T(8,128)(2,1)S(1)} %bitcast.20, bf16[128,1024]{1,0:T(8,128)(2,1)} %copy-done.5, s32[32,128]{1,0:T(8,128)S(1)} %bitcast.29, ...), custom_call_target="tpu_custom_call" | custom-call | flops 10000000000 | bytes 25165824 | tf_op jit(solution)/shard_map/kernel_rows/pallas_call | solution.py:218
  36.8 3.0 %components.2.rest_0_ = f32[256,128]{1,0:T(8,128)S(1)} custom-call(s32[4096]{0:T(1024)S(1)} %bitcast.30, f32[8192,128]{1,0:T(8,128)S(1)} %get-tuple-element.60.kern, bf16[4096,256]{1,0:T(8,128)(2,1)S(1)} %copy-done), custom_call_target="tpu_custom_call" | custom-call | flops 3000000000 | bytes 6291456 | tf_op jit(solution)/shard_map/components/pallas_call | solution.py:279
  39.9 1.1 %collective-permute-done.rest_1_ = bf16[32,8192]{1,0:T(8,128)(2,1)} collective-permute-done((bf16[32,8192]{1,0:T(8,128)(2,1)S(1)}, bf16[32,8192]{1,0:T(8,128)(2,1)}, u32[]{:S(2)}, u32[]{:S(2)}) %collective-permute-start) | collective-permute-done | bytes 524320 | tf_op jit(solution)/shard_map/ppermute | solution.py:402
  41.0 0.5 collective-permute-start.4
  41.5 0.5 collective-permute-start.6
  42.0 3.1 %components.3 = (f32[256,128]{1,0:T(8,128)S(1)}, bf16[32,8192]{1,0:T(8,128)(2,1)S(1)}, bf16[32,8192]{1,0:T(8,128)(2,1)S(1)}, bf16[32,8192]{1,0:T(8,128)(2,1)S(1)}) custom-call(s32[4096]{0:T(1024)S(1)} %bitcast.31, f32[8192,128]{1,0:T(8,128)S(1)} %get-tuple-element.60.kern, bf16[4096,256]{1,0:T(8,128)(2,1)S(1)} %copy-done, f32[256,128]{1,0:T(8,128)S(1)} %components.2.rest_0_, ...), custom_call_target="tpu_custom_call" | custom-call | flops 3000000000 | bytes 6291456 | tf_op jit(solution)/shard_map/components/pallas_call | solution.py:279
  45.1 0.2 collective-permute-done.6.rest_7_
  45.4 1.3 %predict.1 = f32[16,32,128]{2,1,0:T(8,128)S(1)} custom-call(f32[256,128]{1,0:T(8,128)S(1)} %get-tuple-element.66.comp_ref, bf16[8192,128]{1,0:T(8,128)(2,1)S(1)} %get-tuple-element.67.kern16, bf16[32,8192]{1,0:T(8,128)(2,1)S(1)} %bitcast.25, bf16[32,8192]{1,0:T(8,128)(2,1)S(1)} %collective-permute-done.3.rest_1_, ...), custom_call_target="tpu_custom_call" | custom-call | tf_op jit(solution)/shard_map/predict/pallas_call | solution.py:313
  46.6 15.7 %all_to_all.21 = f32[16,32,128]{2,1,0:T(8,128)S(1)} all-to-all(f32[16,32,128]{2,1,0:T(8,128)S(1)} %predict.1), channel_id=1, replica_groups=mesh['ctr'=16,'bat'=8] {'ctr'}, dimensions={0} | all-to-all | bytes 524288 | tf_op jit(solution)/shard_map/all_to_all | solution.py:425
  62.4 0.1 broadcast_in_dim.20
  62.5 19.2 %all_to_all.22.same_ref = f32[64,24,128]{2,1,0:T(8,128)S(1)} all-to-all(f32[64,24,128]{2,1,0:T(8,128)S(1)} %bitcast.32), channel_id=1, replica_groups={{0,2,4,6,8,10,12,14,16,18,20,22,24,26,28,30,32,34,36,38,40,42,44,46,48,..., dimensions={0} | all-to-all | bytes 1572864 | tf_op jit(solution)/shard_map/all_to_all | solution.py:430
  81.8 0.3 same_part.1.proj_ref
  82.0 2.0 %collective-permute-done.7.other_ref = f32[64,24,128]{2,1,0:T(8,128)S(1)} collective-permute-done((f32[64,24,128]{2,1,0:T(8,128)S(1)}, f32[64,24,128]{2,1,0:T(8,128)S(1)}, u32[]{:S(2)}, u32[]{:S(2)}) %collective-permute-start.7) | collective-permute-done | bytes 786464 | tf_op jit(solution)/shard_map/ppermute | solution.py:431
  84.0 2.0 %final.1 = (f32[32,1024]{1,0:T(8,128)}, f32[32,4096]{1,0:T(8,128)}) custom-call(f32[64,24,128]{2,1,0:T(8,128)S(1)} %all_to_all.22.same_ref, f32[64,24,128]{2,1,0:T(8,128)S(1)} %collective-permute-done.7.other_ref, f32[32,256]{1,0:T(8,128)S(1)} %same_part.1.proj_ref, f32[32,1024]{1,0:T(8,128)S(1)} %bitcast.27, f32[1,256]{1,0:T(1,128)S(1)} %bitcast.28, ...), custom_call_target="tpu_custom_call" | custom-call | tf_op jit(solution)/shard_map/final/pallas_call | solution.py:384
  (25 shorter events, 0.1 us)
Async XLA Ops:
  0.6 16.0 %copy-start.6 = (s32[128]{0:T(128)S(1)}, s32[128]{0:T(128)}, u32[]{:S(2)}) copy-start(s32[128]{0:T(128)} %refs_0_.1) | copy-start | bytes 1540
  0.6 10.6 %copy-start.1 = (bf16[8192,32]{0,1:T(8,128)(2,1)S(1)}, bf16[8192,32]{0,1:T(8,128)(2,1)}, u32[]{:S(2)}) copy-start(bf16[8192,32]{0,1:T(8,128)(2,1)} %param.10) | copy-start | bytes 1572868
  4.0 21.6 %all-to-all-start.1 = ((bf16[16,24,1024]{2,1,0:T(8,128)(2,1)}), bf16[16,24,1024]{2,1,0:T(8,128)(2,1)S(1)}, u32[]{:S(2)}, u32[]{:S(2)}) async-start(bf16[16,24,1024]{2,1,0:T(8,128)(2,1)} %pick.2), calls=%async_computation.1 | async-start | bytes 1572864 | tf_op jit(solution)/shard_map/all_to_all | solution.py:403
  11.3 28.6 %collective-permute-start.2 = (bf16[32,8192]{1,0:T(8,128)(2,1)S(1)}, bf16[32,8192]{1,0:T(8,128)(2,1)}, u32[]{:S(2)}, u32[]{:S(2)}) collective-permute-start(bf16[32,8192]{1,0:T(8,128)(2,1)S(1)} %bitcast.21), channel_id=1, source_target_pairs={{0,6},{1,7},{2,0},{3,1},{4,2},{5,3},{6,4},{7,5},{8,14},{9,15},{10,... | collective-permute-start | bytes 1572872 | tf_op jit(solution)/shard_map/ppermute | solution.py:402
  15.4 24.5 %collective-permute-start.1 = (bf16[32,8192]{1,0:T(8,128)(2,1)S(1)}, bf16[32,8192]{1,0:T(8,128)(2,1)}, u32[]{:S(2)}, u32[]{:S(2)}) collective-permute-start(bf16[32,8192]{1,0:T(8,128)(2,1)S(1)} %bitcast.22), channel_id=1, source_target_pairs={{0,4},{1,5},{2,6},{3,7},{4,0},{5,1},{6,2},{7,3},{8,12},{9,13},{10,... | collective-permute-start | bytes 1572872 | tf_op jit(solution)/shard_map/ppermute | solution.py:402
  15.4 25.6 %collective-permute-start = (bf16[32,8192]{1,0:T(8,128)(2,1)S(1)}, bf16[32,8192]{1,0:T(8,128)(2,1)}, u32[]{:S(2)}, u32[]{:S(2)}) collective-permute-start(bf16[32,8192]{1,0:T(8,128)(2,1)S(1)} %bitcast.23), channel_id=1, source_target_pairs={{0,2},{1,3},{2,4},{3,5},{4,6},{5,7},{6,0},{7,1},{8,10},{9,11},{10,... | collective-permute-start | bytes 1572872 | tf_op jit(solution)/shard_map/ppermute | solution.py:402
  25.6 1.4 %copy-start.4 = (s32[4096]{0:T(1024)S(1)}, s32[4096]{0:T(1024)}, u32[]{:S(2)}) copy-start(s32[4096]{0:T(1024)} %param.15) | copy-start | bytes 49156
  26.3 0.7 copy-start.5
  27.0 9.8 %copy-start = (bf16[4096,256]{1,0:T(8,128)(2,1)S(1)}, bf16[4096,256]{1,0:T(8,128)(2,1)}, u32[]{:S(2)}) copy-start(bf16[4096,256]{1,0:T(8,128)(2,1)} %eig_ref.5) | copy-start | bytes 6291460
  41.0 4.1 %collective-permute-start.3 = (bf16[32,8192]{1,0:T(8,128)(2,1)S(1)}, bf16[32,8192]{1,0:T(8,128)(2,1)S(1)}, u32[]{:S(2)}, u32[]{:S(2)}) collective-permute-start(bf16[32,8192]{1,0:T(8,128)(2,1)S(1)} %bitcast.24), channel_id=1, source_target_pairs={{0,1},{1,0},{2,3},{3,2},{4,5},{5,4},{6,7},{7,6},{8,9},{9,8},{10,11... | collective-permute-start | bytes 1572872 | tf_op jit(solution)/shard_map/ppermute | solution.py:421
  41.0 4.1 %collective-permute-start.4 = (bf16[32,8192]{1,0:T(8,128)(2,1)}, bf16[32,8192]{1,0:T(8,128)(2,1)S(1)}, u32[]{:S(2)}, u32[]{:S(2)}) collective-permute-start(bf16[32,8192]{1,0:T(8,128)(2,1)} %collective-permute-done.rest_1_), channel_id=1, source_target_pairs={{0,1},{1,0},{2,3},{3,2},{4,5},{5,4},{6,7},{7,6},{8,9},{9,8},{10,11... | collective-permute-start | bytes 1572872 | tf_op jit(solution)/shard_map/ppermute | solution.py:421
  41.5 3.6 %collective-permute-start.5 = (bf16[32,8192]{1,0:T(8,128)(2,1)}, bf16[32,8192]{1,0:T(8,128)(2,1)S(1)}, u32[]{:S(2)}, u32[]{:S(2)}) collective-permute-start(bf16[32,8192]{1,0:T(8,128)(2,1)} %collective-permute-done.1.rest_2_), channel_id=1, source_target_pairs={{0,1},{1,0},{2,3},{3,2},{4,5},{5,4},{6,7},{7,6},{8,9},{9,8},{10,11... | collective-permute-start | bytes 1572872 | tf_op jit(solution)/shard_map/ppermute | solution.py:421
  41.5 3.9 %collective-permute-start.6 = (bf16[32,8192]{1,0:T(8,128)(2,1)}, bf16[32,8192]{1,0:T(8,128)(2,1)S(1)}, u32[]{:S(2)}, u32[]{:S(2)}) collective-permute-start(bf16[32,8192]{1,0:T(8,128)(2,1)} %collective-permute-done.2.rest_3_), channel_id=1, source_target_pairs={{0,1},{1,0},{2,3},{3,2},{4,5},{5,4},{6,7},{7,6},{8,9},{9,8},{10,11... | collective-permute-start | bytes 1572872 | tf_op jit(solution)/shard_map/ppermute | solution.py:421
  45.4 36.4 %copy-start.2 = (f32[1024,32]{0,1:T(8,128)S(1)}, f32[1024,32]{0,1:T(8,128)}, u32[]{:S(2)}) copy-start(f32[1024,32]{0,1:T(8,128)} %param.11) | copy-start | bytes 393220
  45.4 38.7 %copy-start.3 = (f32[256]{0:T(256)S(1)}, f32[256]{0:T(256)}, u32[]{:S(2)}) copy-start(f32[256]{0:T(256)} %param.13) | copy-start | bytes 3076
  81.8 2.3 %collective-permute-start.7 = (f32[64,24,128]{2,1,0:T(8,128)S(1)}, f32[64,24,128]{2,1,0:T(8,128)S(1)}, u32[]{:S(2)}, u32[]{:S(2)}) collective-permute-start(f32[64,24,128]{2,1,0:T(8,128)S(1)} %all_to_all.22.same_ref), channel_id=1, source_target_pairs={{0,1},{1,0},{2,3},{3,2},{4,5},{5,4},{6,7},{7,6},{8,9},{9,8},{10,11... | collective-permute-start | bytes 2359304 | tf_op jit(solution)/shard_map/ppermute | solution.py:431

commit v6 on v5

--- a/solution.py
+++ b/solution.py
@@ -11,6 +11,7 @@
 SHARPNESS = 4.0 / D
 N_CTR = 16
 N_Z = 4
+SHIFTS = (0, 1, 3, 2)
 LANES = 128
 GROUP = 16
 SLOTS = 24
@@ -137,21 +138,27 @@
     return jnp.dot(chosen, received, preferred_element_type=F32)
 
 
-def settle_kernel(c_rows, round_ref, idx_ref, received_ref, before_ref, out_ref):
-    at_round = round_ref[0].astype(F32)
-    rows = settled(idx_ref[...], received_ref[...], at_round, c_rows)
-    out_ref[...] = (rows + before_ref[...].astype(F32)).astype(BF16)
+def settle_kernel(c_rows, round_ref, idx_ref, received_ref, before_hbm, out_hbm, rows_ref, sem):
+    copy_in = pltpu.make_async_copy(before_hbm, rows_ref, sem)
+    copy_in.start()
+    rows = settled(idx_ref[...], received_ref[...], round_ref[0].astype(F32), c_rows)
+    copy_in.wait()
+    rows_ref[...] = (rows + rows_ref[...].astype(F32)).astype(BF16)
+    copy_out = pltpu.make_async_copy(rows_ref, out_hbm, sem)
+    copy_out.start()
+    copy_out.wait()
 
 
 def settle(at_round, idx_row, received, before, c_rows):
     return pl.pallas_call(
         functools.partial(settle_kernel, c_rows),
-        in_specs=[SMEM, VMEM, VMEM, VMEM],
-        out_specs=VMEM,
+        in_specs=[SMEM, VMEM, VMEM, HBM],
+        out_specs=HBM,
         out_shape=jax.ShapeDtypeStruct(before.shape, BF16),
+        scratch_shapes=[pltpu.VMEM(before.shape, BF16), pltpu.SemaphoreType.DMA(())],
         compiler_params=pltpu.CompilerParams(vmem_limit_bytes=8 * MIB),
         name="settle",
-    )(at_round, idx_row, received, before)
+    )(at_round, idx_row, received, in_hbm(before))
 
 
 N_TILES = 8
@@ -300,11 +307,11 @@
     bat = lax.axis_index("bat")
     z = bat // 2
     core = bat % 2
-    for k in range(N_Z):
+    for p, k in enumerate(SHIFTS):
         for s in range(2):
             from_z = (z + N_Z - k) % N_Z
             from_core = core if s == 0 else 1 - core
-            first = (2 * k + s) * 32
+            first = (2 * p + s) * 32
             for i in range(8):
                 out_ref[from_core * 8 + i, pl.ds(16 + from_z * 4, 4), :] = acc[first + 4 * i:first + 4 * i + 4]
 
@@ -399,7 +406,7 @@
     idx_row = batch_idx.reshape(1, -1)
     picked = pick(batch_idx, table)
     picked, idx_row, own = lax.optimization_barrier((picked, idx_row, coefs.T))
-    from_z = [lax.ppermute(own, "bat", z_shift(k)) if k else own for k in range(N_Z)]
+    from_z = [lax.ppermute(own, "bat", z_shift(k)) if k else own for k in SHIFTS]
     received = lax.all_to_all(picked, "ctr", 0, 0).reshape(-1, D)
     rounds = count_rounds(idx_row, c_rows)
     received, rounds = lax.optimization_barrier((received, rounds))

time: 87.5 us -> 86.9 us (level)
  waiting for transfers between devices: 11.6 us -> 9.95 us
    all_to_all x1, blocking collectives: 19.2 us -> 20.7 us  [per_device(): lax.all_to_all(sent, ('ctr', 'bat'), 0, 0, axis_index_groups=SAME_CORE)]
    ppermute x3, waiting for transfers between devices: 1.11 us -> 0.01 us  [per_device(): lax.ppermute(own, 'bat', z_shift(k))]
    all_to_all x1, blocking collectives: 15.7 us -> 14.6 us  [per_device(): mine = jnp.sum(lax.all_to_all(partial, 'ctr', 0, 0), axis=0)]
  transfers between devices with their start and end apart: 9 -> 9, of which waited for: 4 -> 3; matrix products, arithmetic and copies ran while one was open for 0% -> 0% of each run, Pallas kernels for 20% -> 20%
where the time goes in v6:
time: 86.9 us; the launch traced here: 85.3 us
  blocking collectives  35.3 us (41%)
  Pallas kernels  23.5 us (27%)
  starting transfers between devices  14.2 us (16%)
  waiting for transfers between devices  9.95 us (11%)
    all_to_all x1, blocking collectives, per_device(): lax.all_to_all(sent, ('ctr', 'bat'), 0, 0, axis_index_groups=SAME_CORE)  20.7 us
    all_to_all x1, blocking collectives, per_device(): mine = jnp.sum(lax.all_to_all(partial, 'ctr', 0, 0), axis=0)  14.6 us
    pallas_call x1, Pallas kernels, kernel_rows(): pl.pallas_call(kern_kernel, in_specs=[VMEM, ANY, ANY, VMEM, HBM], out_spe...  9.79 us
    all_to_all x1, waiting for transfers between devices, per_device(): received = lax.all_to_all(picked, 'ctr', 0, 0).reshape(-1, D)  7.68 us
    all_to_all x1, starting transfers between devices, per_device(): received = lax.all_to_all(picked, 'ctr', 0, 0).reshape(-1, D)  7.21 us
    pallas_call x2, Pallas kernels, components(): pl.pallas_call(functools.partial(comp_kernel, part), in_specs=[SMEM, VMEM...  6.11 us
    ppermute x3, starting transfers between devices, per_device(): lax.ppermute(own, 'bat', z_shift(k))  5.91 us
    pallas_call x1, Pallas kernels, pick(): pl.pallas_call(functools.partial(pick_kernel, first), in_specs=([] if fir...  3.33 us
  transfers between devices with their start and end apart: 9, of which 3 were waited for; matrix products, arithmetic and copies ran while one was open for 0% of the time, Pallas kernels for 20%

profile of v6, /device:TPU:0, one launch (start us, length us, event | category | flops | bytes accessed | tf_op | source)
XLA Modules:
  0.0 85.3 jit_solution(16741430167444698342)
XLA Ops:
  0.7 3.3 %pick.2 = bf16[16,24,1024]{2,1,0:T(8,128)(2,1)} custom-call(s32[128]{0:T(128)} %refs_0_.1, bf16[8192,1024]{1,0:T(8,128)(2,1)} %table_ref.1), custom_call_target="tpu_custom_call" | custom-call | tf_op jit(solution)/shard_map/pick/pallas_call | solution.py:86
  4.0 7.2 %all-to-all-start.1 = ((bf16[16,24,1024]{2,1,0:T(8,128)(2,1)}), bf16[16,24,1024]{2,1,0:T(8,128)(2,1)S(1)}, u32[]{:S(2)}, u32[]{:S(2)}) async-start(bf16[16,24,1024]{2,1,0:T(8,128)(2,1)} %pick.2), calls=%async_computation.1 | async-start | bytes 1572864 | tf_op jit(solution)/shard_map/all_to_all | solution.py:410
  11.2 3.9 %collective-permute-start.2 = (bf16[32,8192]{1,0:T(8,128)(2,1)S(1)}, bf16[32,8192]{1,0:T(8,128)(2,1)}, u32[]{:S(2)}, u32[]{:S(2)}) collective-permute-start(bf16[32,8192]{1,0:T(8,128)(2,1)S(1)} %bitcast.21), channel_id=1, source_target_pairs={{0,4},{1,5},{2,6},{3,7},{4,0},{5,1},{6,2},{7,3},{8,12},{9,13},{10,... | collective-permute-start | bytes 1572872 | tf_op jit(solution)/shard_map/ppermute | solution.py:409
  15.1 0.7 collective-permute-start.1
  15.8 1.3 %collective-permute-start = (bf16[32,8192]{1,0:T(8,128)(2,1)S(1)}, bf16[32,8192]{1,0:T(8,128)(2,1)}, u32[]{:S(2)}, u32[]{:S(2)}) collective-permute-start(bf16[32,8192]{1,0:T(8,128)(2,1)S(1)} %bitcast.23), channel_id=1, source_target_pairs={{0,2},{1,3},{2,4},{3,5},{4,6},{5,7},{6,0},{7,1},{8,10},{9,11},{10,... | collective-permute-start | bytes 1572872 | tf_op jit(solution)/shard_map/ppermute | solution.py:409
  17.1 0.7 count_rounds.1
  17.9 7.7 %all-to-all-done.1 = bf16[16,24,1024]{2,1,0:T(8,128)(2,1)S(1)} async-done(((bf16[16,24,1024]{2,1,0:T(8,128)(2,1)}), bf16[16,24,1024]{2,1,0:T(8,128)(2,1)S(1)}, u32[]{:S(2)}, u32[]{:S(2)}) %all-to-all-start.1) | async-done | bytes 786464 | tf_op jit(solution)/shard_map/all_to_all | solution.py:410
  25.6 0.7 while.10
  26.3 0.7 copy-done.5
  27.0 9.8 %kernel_rows.1 = (f32[8192,128]{1,0:T(8,128)S(1)}, bf16[8192,128]{1,0:T(8,128)(2,1)S(1)}, s32[32,128]{1,0:T(8,128)S(1)}) custom-call(s32[1,128]{1,0:T(1,128)S(1)} %get-tuple-element.165, bf16[384,1024]{1,0:T(8,128)(2,1)S(1)} %bitcast.20, bf16[128,1024]{1,0:T(8,128)(2,1)} %copy-done.5, s32[32,128]{1,0:T(8,128)S(1)} %bitcast.29, ...), custom_call_target="tpu_custom_call" | custom-call | flops 10000000000 | bytes 25165824 | tf_op jit(solution)/shard_map/kernel_rows/pallas_call | solution.py:225
  36.8 3.0 %components.2.rest_0_ = f32[256,128]{1,0:T(8,128)S(1)} custom-call(s32[4096]{0:T(1024)S(1)} %bitcast.30, f32[8192,128]{1,0:T(8,128)S(1)} %get-tuple-element.60.kern, bf16[4096,256]{1,0:T(8,128)(2,1)S(1)} %copy-done), custom_call_target="tpu_custom_call" | custom-call | flops 3000000000 | bytes 6291456 | tf_op jit(solution)/shard_map/components/pallas_call | solution.py:286
  39.9 0.1 collective-permute-start.3
  40.0 0.5 collective-permute-start.4
  40.5 0.1 collective-permute-start.5
  40.6 0.4 collective-permute-start.6
  41.0 3.1 %components.3 = (f32[256,128]{1,0:T(8,128)S(1)}, bf16[32,8192]{1,0:T(8,128)(2,1)S(1)}, bf16[32,8192]{1,0:T(8,128)(2,1)S(1)}, bf16[32,8192]{1,0:T(8,128)(2,1)S(1)}) custom-call(s32[4096]{0:T(1024)S(1)} %bitcast.31, f32[8192,128]{1,0:T(8,128)S(1)} %get-tuple-element.60.kern, bf16[4096,256]{1,0:T(8,128)(2,1)S(1)} %copy-done, f32[256,128]{1,0:T(8,128)S(1)} %components.2.rest_0_, ...), custom_call_target="tpu_custom_call" | custom-call | flops 3000000000 | bytes 6291456 | tf_op jit(solution)/shard_map/components/pallas_call | solution.py:286
  44.1 0.2 collective-permute-done.6.rest_7_
  44.4 1.3 %predict.1 = f32[16,32,128]{2,1,0:T(8,128)S(1)} custom-call(f32[256,128]{1,0:T(8,128)S(1)} %get-tuple-element.66.comp_ref, bf16[8192,128]{1,0:T(8,128)(2,1)S(1)} %get-tuple-element.67.kern16, bf16[32,8192]{1,0:T(8,128)(2,1)S(1)} %bitcast.25, bf16[32,8192]{1,0:T(8,128)(2,1)S(1)} %collective-permute-done.3.rest_1_, ...), custom_call_target="tpu_custom_call" | custom-call | tf_op jit(solution)/shard_map/predict/pallas_call | solution.py:320
  45.6 14.6 %all_to_all.21 = f32[16,32,128]{2,1,0:T(8,128)S(1)} all-to-all(f32[16,32,128]{2,1,0:T(8,128)S(1)} %predict.1), channel_id=1, replica_groups=mesh['ctr'=16,'bat'=8] {'ctr'}, dimensions={0} | all-to-all | bytes 524288 | tf_op jit(solution)/shard_map/all_to_all | solution.py:432
  60.3 0.1 broadcast_in_dim.20
  60.4 20.7 %all_to_all.22.same_ref = f32[64,24,128]{2,1,0:T(8,128)S(1)} all-to-all(f32[64,24,128]{2,1,0:T(8,128)S(1)} %bitcast.32), channel_id=1, replica_groups={{0,2,4,6,8,10,12,14,16,18,20,22,24,26,28,30,32,34,36,38,40,42,44,46,48,..., dimensions={0} | all-to-all | bytes 1572864 | tf_op jit(solution)/shard_map/all_to_all | solution.py:437
  81.1 0.3 same_part.1.proj_ref
  81.3 2.0 %collective-permute-done.7.other_ref = f32[64,24,128]{2,1,0:T(8,128)S(1)} collective-permute-done((f32[64,24,128]{2,1,0:T(8,128)S(1)}, f32[64,24,128]{2,1,0:T(8,128)S(1)}, u32[]{:S(2)}, u32[]{:S(2)}) %collective-permute-start.7) | collective-permute-done | bytes 786464 | tf_op jit(solution)/shard_map/ppermute | solution.py:438
  83.3 2.0 %final.1 = (f32[32,1024]{1,0:T(8,128)}, f32[32,4096]{1,0:T(8,128)}) custom-call(f32[64,24,128]{2,1,0:T(8,128)S(1)} %all_to_all.22.same_ref, f32[64,24,128]{2,1,0:T(8,128)S(1)} %collective-permute-done.7.other_ref, f32[32,256]{1,0:T(8,128)S(1)} %same_part.1.proj_ref, f32[32,1024]{1,0:T(8,128)S(1)} %bitcast.27, f32[1,256]{1,0:T(1,128)S(1)} %bitcast.28, ...), custom_call_target="tpu_custom_call" | custom-call | tf_op jit(solution)/shard_map/final/pallas_call | solution.py:391
  (25 shorter events, 0.1 us)
Async XLA Ops:
  0.6 16.5 %copy-start.6 = (s32[128]{0:T(128)S(1)}, s32[128]{0:T(128)}, u32[]{:S(2)}) copy-start(s32[128]{0:T(128)} %refs_0_.1) | copy-start | bytes 1540
  0.6 10.6 %copy-start.1 = (bf16[8192,32]{0,1:T(8,128)(2,1)S(1)}, bf16[8192,32]{0,1:T(8,128)(2,1)}, u32[]{:S(2)}) copy-start(bf16[8192,32]{0,1:T(8,128)(2,1)} %param.10) | copy-start | bytes 1572868
  4.0 21.6 %all-to-all-start.1 = ((bf16[16,24,1024]{2,1,0:T(8,128)(2,1)}), bf16[16,24,1024]{2,1,0:T(8,128)(2,1)S(1)}, u32[]{:S(2)}, u32[]{:S(2)}) async-start(bf16[16,24,1024]{2,1,0:T(8,128)(2,1)} %pick.2), calls=%async_computation.1 | async-start | bytes 1572864 | tf_op jit(solution)/shard_map/all_to_all | solution.py:410
  11.2 28.7 %collective-permute-start.2 = (bf16[32,8192]{1,0:T(8,128)(2,1)S(1)}, bf16[32,8192]{1,0:T(8,128)(2,1)}, u32[]{:S(2)}, u32[]{:S(2)}) collective-permute-start(bf16[32,8192]{1,0:T(8,128)(2,1)S(1)} %bitcast.21), channel_id=1, source_target_pairs={{0,4},{1,5},{2,6},{3,7},{4,0},{5,1},{6,2},{7,3},{8,12},{9,13},{10,... | collective-permute-start | bytes 1572872 | tf_op jit(solution)/shard_map/ppermute | solution.py:409
  15.1 24.8 %collective-permute-start.1 = (bf16[32,8192]{1,0:T(8,128)(2,1)S(1)}, bf16[32,8192]{1,0:T(8,128)(2,1)}, u32[]{:S(2)}, u32[]{:S(2)}) collective-permute-start(bf16[32,8192]{1,0:T(8,128)(2,1)S(1)} %bitcast.22), channel_id=1, source_target_pairs={{0,6},{1,7},{2,0},{3,1},{4,2},{5,3},{6,4},{7,5},{8,14},{9,15},{10,... | collective-permute-start | bytes 1572872 | tf_op jit(solution)/shard_map/ppermute | solution.py:409
  15.8 24.1 %collective-permute-start = (bf16[32,8192]{1,0:T(8,128)(2,1)S(1)}, bf16[32,8192]{1,0:T(8,128)(2,1)}, u32[]{:S(2)}, u32[]{:S(2)}) collective-permute-start(bf16[32,8192]{1,0:T(8,128)(2,1)S(1)} %bitcast.23), channel_id=1, source_target_pairs={{0,2},{1,3},{2,4},{3,5},{4,6},{5,7},{6,0},{7,1},{8,10},{9,11},{10,... | collective-permute-start | bytes 1572872 | tf_op jit(solution)/shard_map/ppermute | solution.py:409
  25.6 1.4 %copy-start.4 = (s32[4096]{0:T(1024)S(1)}, s32[4096]{0:T(1024)}, u32[]{:S(2)}) copy-start(s32[4096]{0:T(1024)} %param.15) | copy-start | bytes 49156
  26.3 0.7 copy-start.5
  27.0 9.8 %copy-start = (bf16[4096,256]{1,0:T(8,128)(2,1)S(1)}, bf16[4096,256]{1,0:T(8,128)(2,1)}, u32[]{:S(2)}) copy-start(bf16[4096,256]{1,0:T(8,128)(2,1)} %eig_ref.5) | copy-start | bytes 6291460
  39.9 4.2 %collective-permute-start.3 = (bf16[32,8192]{1,0:T(8,128)(2,1)S(1)}, bf16[32,8192]{1,0:T(8,128)(2,1)S(1)}, u32[]{:S(2)}, u32[]{:S(2)}) collective-permute-start(bf16[32,8192]{1,0:T(8,128)(2,1)S(1)} %bitcast.24), channel_id=1, source_target_pairs={{0,1},{1,0},{2,3},{3,2},{4,5},{5,4},{6,7},{7,6},{8,9},{9,8},{10,11... | collective-permute-start | bytes 1572872 | tf_op jit(solution)/shard_map/ppermute | solution.py:428
  40.0 4.1 %collective-permute-start.4 = (bf16[32,8192]{1,0:T(8,128)(2,1)}, bf16[32,8192]{1,0:T(8,128)(2,1)S(1)}, u32[]{:S(2)}, u32[]{:S(2)}) collective-permute-start(bf16[32,8192]{1,0:T(8,128)(2,1)} %collective-permute-done.rest_1_), channel_id=1, source_target_pairs={{0,1},{1,0},{2,3},{3,2},{4,5},{5,4},{6,7},{7,6},{8,9},{9,8},{10,11... | collective-permute-start | bytes 1572872 | tf_op jit(solution)/shard_map/ppermute | solution.py:428
  40.5 3.6 %collective-permute-start.5 = (bf16[32,8192]{1,0:T(8,128)(2,1)}, bf16[32,8192]{1,0:T(8,128)(2,1)S(1)}, u32[]{:S(2)}, u32[]{:S(2)}) collective-permute-start(bf16[32,8192]{1,0:T(8,128)(2,1)} %collective-permute-done.1.rest_2_), channel_id=1, source_target_pairs={{0,1},{1,0},{2,3},{3,2},{4,5},{5,4},{6,7},{7,6},{8,9},{9,8},{10,11... | collective-permute-start | bytes 1572872 | tf_op jit(solution)/shard_map/ppermute | solution.py:428
  40.6 3.8 %collective-permute-start.6 = (bf16[32,8192]{1,0:T(8,128)(2,1)}, bf16[32,8192]{1,0:T(8,128)(2,1)S(1)}, u32[]{:S(2)}, u32[]{:S(2)}) collective-permute-start(bf16[32,8192]{1,0:T(8,128)(2,1)} %collective-permute-done.2.rest_3_), channel_id=1, source_target_pairs={{0,1},{1,0},{2,3},{3,2},{4,5},{5,4},{6,7},{7,6},{8,9},{9,8},{10,11... | collective-permute-start | bytes 1572872 | tf_op jit(solution)/shard_map/ppermute | solution.py:428
  44.3 36.7 %copy-start.2 = (f32[1024,32]{0,1:T(8,128)S(1)}, f32[1024,32]{0,1:T(8,128)}, u32[]{:S(2)}) copy-start(f32[1024,32]{0,1:T(8,128)} %param.11) | copy-start | bytes 393220
  44.4 39.0 %copy-start.3 = (f32[256]{0:T(256)S(1)}, f32[256]{0:T(256)}, u32[]{:S(2)}) copy-start(f32[256]{0:T(256)} %param.13) | copy-start | bytes 3076
  81.1 2.3 %collective-permute-start.7 = (f32[64,24,128]{2,1,0:T(8,128)S(1)}, f32[64,24,128]{2,1,0:T(8,128)S(1)}, u32[]{:S(2)}, u32[]{:S(2)}) collective-permute-start(f32[64,24,128]{2,1,0:T(8,128)S(1)} %all_to_all.22.same_ref), channel_id=1, source_target_pairs={{0,1},{1,0},{2,3},{3,2},{4,5},{5,4},{6,7},{7,6},{8,9},{9,8},{10,11... | collective-permute-start | bytes 2359304 | tf_op jit(solution)/shard_map/ppermute | solution.py:438

commit v7 on v6

--- a/solution.py
+++ b/solution.py
@@ -55,7 +55,7 @@
         listed[count] = pos
         return count + jnp.where((pos >= 0) & (pos < c_rows), 1, 0)
 
-    count = jnp.clip(lax.fori_loop(0, n, note, 0, unroll=16) - done, 0, SLOTS)
+    count = jnp.clip(lax.fori_loop(0, n, note, 0, unroll=32) - done, 0, SLOTS)
 
     def copy_of(s):
         start = pl.multiple_of(listed[done + s] // GROUP * GROUP, GROUP)
@@ -258,7 +258,7 @@
             copy.start()
     else:
         out_ref, nys = rest
-    unroll = 64
+    unroll = 128
     first, n = PARTS[part]
 
     def gather(j, carry):

time: 86.9 us -> 86.9 us (level)
  no operation moved by 1% of the time
where the time goes in v7:
time: 86.9 us; the launch traced here: 85.4 us
  blocking collectives  35.2 us (41%)
  Pallas kernels  23.3 us (27%)
  starting transfers between devices  14.2 us (16%)
  waiting for transfers between devices  10.3 us (12%)
    all_to_all x1, blocking collectives, per_device(): lax.all_to_all(sent, ('ctr', 'bat'), 0, 0, axis_index_groups=SAME_CORE)  20.8 us
    all_to_all x1, blocking collectives, per_device(): mine = jnp.sum(lax.all_to_all(partial, 'ctr', 0, 0), axis=0)  14.5 us
    pallas_call x1, Pallas kernels, kernel_rows(): pl.pallas_call(kern_kernel, in_specs=[VMEM, ANY, ANY, VMEM, HBM], out_spe...  9.78 us
    all_to_all x1, waiting for transfers between devices, per_device(): received = lax.all_to_all(picked, 'ctr', 0, 0).reshape(-1, D)  7.92 us
    all_to_all x1, starting transfers between devices, per_device(): received = lax.all_to_all(picked, 'ctr', 0, 0).reshape(-1, D)  7.28 us
    pallas_call x2, Pallas kernels, components(): pl.pallas_call(functools.partial(comp_kernel, part), in_specs=[SMEM, VMEM...  5.98 us
    ppermute x3, starting transfers between devices, per_device(): lax.ppermute(own, 'bat', z_shift(k))  5.83 us
    pallas_call x1, Pallas kernels, pick(): pl.pallas_call(functools.partial(pick_kernel, first), in_specs=([] if fir...  3.27 us
  transfers between devices with their start and end apart: 9, of which 3 were waited for; matrix products, arithmetic and copies ran while one was open for 0% of the time, Pallas kernels for 20%

profile of v7, /device:TPU:0, one launch (start us, length us, event | category | flops | bytes accessed | tf_op | source)
XLA Modules:
  0.0 85.4 jit_solution(17412562399444064725)
XLA Ops:
  0.7 3.3 %pick.2 = bf16[16,24,1024]{2,1,0:T(8,128)(2,1)} custom-call(s32[128]{0:T(128)} %refs_0_.1, bf16[8192,1024]{1,0:T(8,128)(2,1)} %table_ref.1), custom_call_target="tpu_custom_call" | custom-call | tf_op jit(solution)/shard_map/pick/pallas_call | solution.py:86
  3.9 7.3 %all-to-all-start.1 = ((bf16[16,24,1024]{2,1,0:T(8,128)(2,1)}), bf16[16,24,1024]{2,1,0:T(8,128)(2,1)S(1)}, u32[]{:S(2)}, u32[]{:S(2)}) async-start(bf16[16,24,1024]{2,1,0:T(8,128)(2,1)} %pick.2), calls=%async_computation.1 | async-start | bytes 1572864 | tf_op jit(solution)/shard_map/all_to_all | solution.py:410
  11.2 3.8 %collective-permute-start.2 = (bf16[32,8192]{1,0:T(8,128)(2,1)S(1)}, bf16[32,8192]{1,0:T(8,128)(2,1)}, u32[]{:S(2)}, u32[]{:S(2)}) collective-permute-start(bf16[32,8192]{1,0:T(8,128)(2,1)S(1)} %bitcast.21), channel_id=1, source_target_pairs={{0,4},{1,5},{2,6},{3,7},{4,0},{5,1},{6,2},{7,3},{8,12},{9,13},{10,... | collective-permute-start | bytes 1572872 | tf_op jit(solution)/shard_map/ppermute | solution.py:409
  15.0 0.7 collective-permute-start.1
  15.7 1.3 %collective-permute-start = (bf16[32,8192]{1,0:T(8,128)(2,1)S(1)}, bf16[32,8192]{1,0:T(8,128)(2,1)}, u32[]{:S(2)}, u32[]{:S(2)}) collective-permute-start(bf16[32,8192]{1,0:T(8,128)(2,1)S(1)} %bitcast.23), channel_id=1, source_target_pairs={{0,2},{1,3},{2,4},{3,5},{4,6},{5,7},{6,0},{7,1},{8,10},{9,11},{10,... | collective-permute-start | bytes 1572872 | tf_op jit(solution)/shard_map/ppermute | solution.py:409
  17.1 0.7 count_rounds.1
  17.8 7.9 %all-to-all-done.1 = bf16[16,24,1024]{2,1,0:T(8,128)(2,1)S(1)} async-done(((bf16[16,24,1024]{2,1,0:T(8,128)(2,1)}), bf16[16,24,1024]{2,1,0:T(8,128)(2,1)S(1)}, u32[]{:S(2)}, u32[]{:S(2)}) %all-to-all-start.1) | async-done | bytes 786464 | tf_op jit(solution)/shard_map/all_to_all | solution.py:410
  25.8 0.7 while.10
  26.5 0.7 copy-done.5
  27.2 9.8 %kernel_rows.1 = (f32[8192,128]{1,0:T(8,128)S(1)}, bf16[8192,128]{1,0:T(8,128)(2,1)S(1)}, s32[32,128]{1,0:T(8,128)S(1)}) custom-call(s32[1,128]{1,0:T(1,128)S(1)} %get-tuple-element.165, bf16[384,1024]{1,0:T(8,128)(2,1)S(1)} %bitcast.20, bf16[128,1024]{1,0:T(8,128)(2,1)} %copy-done.5, s32[32,128]{1,0:T(8,128)S(1)} %bitcast.29, ...), custom_call_target="tpu_custom_call" | custom-call | flops 10000000000 | bytes 25165824 | tf_op jit(solution)/shard_map/kernel_rows/pallas_call | solution.py:225
  37.0 3.0 %components.2.rest_0_ = f32[256,128]{1,0:T(8,128)S(1)} custom-call(s32[4096]{0:T(1024)S(1)} %bitcast.30, f32[8192,128]{1,0:T(8,128)S(1)} %get-tuple-element.60.kern, bf16[4096,256]{1,0:T(8,128)(2,1)S(1)} %copy-done), custom_call_target="tpu_custom_call" | custom-call | flops 3000000000 | bytes 6291456 | tf_op jit(solution)/shard_map/components/pallas_call | solution.py:286
  40.0 0.1 collective-permute-start.3
  40.1 0.5 collective-permute-start.4
  40.6 0.1 collective-permute-start.5
  40.7 0.4 collective-permute-start.6
  41.1 3.0 %components.3 = (f32[256,128]{1,0:T(8,128)S(1)}, bf16[32,8192]{1,0:T(8,128)(2,1)S(1)}, bf16[32,8192]{1,0:T(8,128)(2,1)S(1)}, bf16[32,8192]{1,0:T(8,128)(2,1)S(1)}) custom-call(s32[4096]{0:T(1024)S(1)} %bitcast.31, f32[8192,128]{1,0:T(8,128)S(1)} %get-tuple-element.60.kern, bf16[4096,256]{1,0:T(8,128)(2,1)S(1)} %copy-done, f32[256,128]{1,0:T(8,128)S(1)} %components.2.rest_0_, ...), custom_call_target="tpu_custom_call" | custom-call | flops 3000000000 | bytes 6291456 | tf_op jit(solution)/shard_map/components/pallas_call | solution.py:286
  44.2 0.3 collective-permute-done.6.rest_7_
  44.5 1.3 %predict.1 = f32[16,32,128]{2,1,0:T(8,128)S(1)} custom-call(f32[256,128]{1,0:T(8,128)S(1)} %get-tuple-element.66.comp_ref, bf16[8192,128]{1,0:T(8,128)(2,1)S(1)} %get-tuple-element.67.kern16, bf16[32,8192]{1,0:T(8,128)(2,1)S(1)} %bitcast.25, bf16[32,8192]{1,0:T(8,128)(2,1)S(1)} %collective-permute-done.3.rest_1_, ...), custom_call_target="tpu_custom_call" | custom-call | tf_op jit(solution)/shard_map/predict/pallas_call | solution.py:320
  45.7 14.5 %all_to_all.21 = f32[16,32,128]{2,1,0:T(8,128)S(1)} all-to-all(f32[16,32,128]{2,1,0:T(8,128)S(1)} %predict.1), channel_id=1, replica_groups=mesh['ctr'=16,'bat'=8] {'ctr'}, dimensions={0} | all-to-all | bytes 524288 | tf_op jit(solution)/shard_map/all_to_all | solution.py:432
  60.3 0.1 broadcast_in_dim.20
  60.4 20.8 %all_to_all.22.same_ref = f32[64,24,128]{2,1,0:T(8,128)S(1)} all-to-all(f32[64,24,128]{2,1,0:T(8,128)S(1)} %bitcast.32), channel_id=1, replica_groups={{0,2,4,6,8,10,12,14,16,18,20,22,24,26,28,30,32,34,36,38,40,42,44,46,48,..., dimensions={0} | all-to-all | bytes 1572864 | tf_op jit(solution)/shard_map/all_to_all | solution.py:437
  81.1 0.3 same_part.1.proj_ref
  81.4 2.0 %collective-permute-done.7.other_ref = f32[64,24,128]{2,1,0:T(8,128)S(1)} collective-permute-done((f32[64,24,128]{2,1,0:T(8,128)S(1)}, f32[64,24,128]{2,1,0:T(8,128)S(1)}, u32[]{:S(2)}, u32[]{:S(2)}) %collective-permute-start.7) | collective-permute-done | bytes 786464 | tf_op jit(solution)/shard_map/ppermute | solution.py:438
  83.4 2.0 %final.1 = (f32[32,1024]{1,0:T(8,128)}, f32[32,4096]{1,0:T(8,128)}) custom-call(f32[64,24,128]{2,1,0:T(8,128)S(1)} %all_to_all.22.same_ref, f32[64,24,128]{2,1,0:T(8,128)S(1)} %collective-permute-done.7.other_ref, f32[32,256]{1,0:T(8,128)S(1)} %same_part.1.proj_ref, f32[32,1024]{1,0:T(8,128)S(1)} %bitcast.27, f32[1,256]{1,0:T(1,128)S(1)} %bitcast.28, ...), custom_call_target="tpu_custom_call" | custom-call | tf_op jit(solution)/shard_map/final/pallas_call | solution.py:391
  (25 shorter events, 0.1 us)
Async XLA Ops:
  0.6 16.4 %copy-start.6 = (s32[128]{0:T(128)S(1)}, s32[128]{0:T(128)}, u32[]{:S(2)}) copy-start(s32[128]{0:T(128)} %refs_0_.1) | copy-start | bytes 1540
  0.6 10.6 %copy-start.1 = (bf16[8192,32]{0,1:T(8,128)(2,1)S(1)}, bf16[8192,32]{0,1:T(8,128)(2,1)}, u32[]{:S(2)}) copy-start(bf16[8192,32]{0,1:T(8,128)(2,1)} %param.10) | copy-start | bytes 1572868
  3.9 21.8 %all-to-all-start.1 = ((bf16[16,24,1024]{2,1,0:T(8,128)(2,1)}), bf16[16,24,1024]{2,1,0:T(8,128)(2,1)S(1)}, u32[]{:S(2)}, u32[]{:S(2)}) async-start(bf16[16,24,1024]{2,1,0:T(8,128)(2,1)} %pick.2), calls=%async_computation.1 | async-start | bytes 1572864 | tf_op jit(solution)/shard_map/all_to_all | solution.py:410
  11.2 28.8 %collective-permute-start.2 = (bf16[32,8192]{1,0:T(8,128)(2,1)S(1)}, bf16[32,8192]{1,0:T(8,128)(2,1)}, u32[]{:S(2)}, u32[]{:S(2)}) collective-permute-start(bf16[32,8192]{1,0:T(8,128)(2,1)S(1)} %bitcast.21), channel_id=1, source_target_pairs={{0,4},{1,5},{2,6},{3,7},{4,0},{5,1},{6,2},{7,3},{8,12},{9,13},{10,... | collective-permute-start | bytes 1572872 | tf_op jit(solution)/shard_map/ppermute | solution.py:409
  15.0 25.0 %collective-permute-start.1 = (bf16[32,8192]{1,0:T(8,128)(2,1)S(1)}, bf16[32,8192]{1,0:T(8,128)(2,1)}, u32[]{:S(2)}, u32[]{:S(2)}) collective-permute-start(bf16[32,8192]{1,0:T(8,128)(2,1)S(1)} %bitcast.22), channel_id=1, source_target_pairs={{0,6},{1,7},{2,0},{3,1},{4,2},{5,3},{6,4},{7,5},{8,14},{9,15},{10,... | collective-permute-start | bytes 1572872 | tf_op jit(solution)/shard_map/ppermute | solution.py:409
  15.7 24.3 %collective-permute-start = (bf16[32,8192]{1,0:T(8,128)(2,1)S(1)}, bf16[32,8192]{1,0:T(8,128)(2,1)}, u32[]{:S(2)}, u32[]{:S(2)}) collective-permute-start(bf16[32,8192]{1,0:T(8,128)(2,1)S(1)} %bitcast.23), channel_id=1, source_target_pairs={{0,2},{1,3},{2,4},{3,5},{4,6},{5,7},{6,0},{7,1},{8,10},{9,11},{10,... | collective-permute-start | bytes 1572872 | tf_op jit(solution)/shard_map/ppermute | solution.py:409
  25.8 1.4 %copy-start.4 = (s32[4096]{0:T(1024)S(1)}, s32[4096]{0:T(1024)}, u32[]{:S(2)}) copy-start(s32[4096]{0:T(1024)} %param.15) | copy-start | bytes 49156
  26.5 0.7 copy-start.5
  27.2 9.8 %copy-start = (bf16[4096,256]{1,0:T(8,128)(2,1)S(1)}, bf16[4096,256]{1,0:T(8,128)(2,1)}, u32[]{:S(2)}) copy-start(bf16[4096,256]{1,0:T(8,128)(2,1)} %eig_ref.5) | copy-start | bytes 6291460
  40.0 4.1 %collective-permute-start.3 = (bf16[32,8192]{1,0:T(8,128)(2,1)S(1)}, bf16[32,8192]{1,0:T(8,128)(2,1)S(1)}, u32[]{:S(2)}, u32[]{:S(2)}) collective-permute-start(bf16[32,8192]{1,0:T(8,128)(2,1)S(1)} %bitcast.24), channel_id=1, source_target_pairs={{0,1},{1,0},{2,3},{3,2},{4,5},{5,4},{6,7},{7,6},{8,9},{9,8},{10,11... | collective-permute-start | bytes 1572872 | tf_op jit(solution)/shard_map/ppermute | solution.py:428
  40.1 4.0 %collective-permute-start.4 = (bf16[32,8192]{1,0:T(8,128)(2,1)}, bf16[32,8192]{1,0:T(8,128)(2,1)S(1)}, u32[]{:S(2)}, u32[]{:S(2)}) collective-permute-start(bf16[32,8192]{1,0:T(8,128)(2,1)} %collective-permute-done.rest_1_), channel_id=1, source_target_pairs={{0,1},{1,0},{2,3},{3,2},{4,5},{5,4},{6,7},{7,6},{8,9},{9,8},{10,11... | collective-permute-start | bytes 1572872 | tf_op jit(solution)/shard_map/ppermute | solution.py:428
  40.6 3.5 %collective-permute-start.5 = (bf16[32,8192]{1,0:T(8,128)(2,1)}, bf16[32,8192]{1,0:T(8,128)(2,1)S(1)}, u32[]{:S(2)}, u32[]{:S(2)}) collective-permute-start(bf16[32,8192]{1,0:T(8,128)(2,1)} %collective-permute-done.1.rest_2_), channel_id=1, source_target_pairs={{0,1},{1,0},{2,3},{3,2},{4,5},{5,4},{6,7},{7,6},{8,9},{9,8},{10,11... | collective-permute-start | bytes 1572872 | tf_op jit(solution)/shard_map/ppermute | solution.py:428
  40.7 3.8 %collective-permute-start.6 = (bf16[32,8192]{1,0:T(8,128)(2,1)}, bf16[32,8192]{1,0:T(8,128)(2,1)S(1)}, u32[]{:S(2)}, u32[]{:S(2)}) collective-permute-start(bf16[32,8192]{1,0:T(8,128)(2,1)} %collective-permute-done.2.rest_3_), channel_id=1, source_target_pairs={{0,1},{1,0},{2,3},{3,2},{4,5},{5,4},{6,7},{7,6},{8,9},{9,8},{10,11... | collective-permute-start | bytes 1572872 | tf_op jit(solution)/shard_map/ppermute | solution.py:428
  44.5 36.7 %copy-start.2 = (f32[1024,32]{0,1:T(8,128)S(1)}, f32[1024,32]{0,1:T(8,128)}, u32[]{:S(2)}) copy-start(f32[1024,32]{0,1:T(8,128)} %param.11) | copy-start | bytes 393220
  44.5 38.9 %copy-start.3 = (f32[256]{0:T(256)S(1)}, f32[256]{0:T(256)}, u32[]{:S(2)}) copy-start(f32[256]{0:T(256)} %param.13) | copy-start | bytes 3076
  81.1 2.3 %collective-permute-start.7 = (f32[64,24,128]{2,1,0:T(8,128)S(1)}, f32[64,24,128]{2,1,0:T(8,128)S(1)}, u32[]{:S(2)}, u32[]{:S(2)}) collective-permute-start(f32[64,24,128]{2,1,0:T(8,128)S(1)} %all_to_all.22.same_ref), channel_id=1, source_target_pairs={{0,1},{1,0},{2,3},{3,2},{4,5},{5,4},{6,7},{7,6},{8,9},{9,8},{10,11... | collective-permute-start | bytes 2359304 | tf_op jit(solution)/shard_map/ppermute | solution.py:438
